TPU v7x, 256 devices: a whole 4x4x8 slice. The times are simulated.
256 devices in a mesh: gx: 64 (over y, z, x_hi), gy: 4 (over x_lo, core).
Axes of the slice: x: 4 (x_hi: 2, x_lo: 2; x = x_hi * 2 + x_lo), y: 4, z: 8, core: 2. Of those that a mesh axis runs over, the one named last changes fastest.
Arguments:
- layer_input: bfloat16 [128, 128, 32, 512], P('gx', 'gy'), may hold values from -6 to 6
- cotangent: bfloat16 [128, 128, 32, 512], P('gx', 'gy'), may hold values from -6 to 6
- spectral_weight: bfloat16 [32, 64, 32, 1024], P('gy', 'gx'), may hold values from -12 to 12
- bypass_weight: bfloat16 [32, 32], replicated, may hold values from -1 to 1
- channel_bias: float32 [32], replicated, may hold values from -4 to 4
- hash_key: int32 [2], replicated, may hold values from 0 to 1073741823
Outputs:
- grad_input: bfloat16 [128, 128, 32, 512], P('gx', 'gy')
- grad_spectral: float32 [32, 64, 32, 1024], P('gy', 'gx')
- grad_bypass: float32 [32, 32], replicated
- grad_bias: float32 [32], replicated
All inputs are finite; a program needn't handle non-finite values.
Results may differ from a plain program's by a relative error of at most 0.011.
Values sent between devices are 32-bit elements; how exact they have to be, the bound alone decides.
No kernel may reach another device: no remote copies, remote signals or barrier semaphores. Data moves between devices by JAX's collectives and lax.ppermute only.
A program may use at most 64 MiB of HBM per device.

v0:
```python
import math

import jax
import jax.numpy as jnp
from jax import lax
from jax.sharding import PartitionSpec as P

LX = 128
LY = 128
LZ = 64
LT = 8
KX = 32
KY = 32
KZ = 16
KT = 4
LZT = 512


keep_level = 6554
keep_scale = 1.0 / 0.9
gelu_cubic = 0.044715
mixer_one = -1640531535
mixer_two = -2048144789
mixer_three = -1028477387


def hartley_table(kept, length):
    wanted = jnp.arange(kept, dtype=jnp.int32)
    frequency = jnp.where(wanted < kept // 2, wanted, wanted + (length - kept))
    positions = jnp.arange(length, dtype=jnp.int32)
    residue = frequency[:, None] * positions[None, :] % length
    radians = residue.astype(jnp.float32) * (2.0 * math.pi / length)
    return (jnp.cos(radians) + jnp.sin(radians)) / math.sqrt(length)


def depth_table():
    depth_part = hartley_table(KZ, LZ)
    time_part = hartley_table(KT, LT)
    joined = depth_part[:, None, :, None] * time_part[None, :, None, :]
    return joined.reshape(KZ * KT, LZ * LT)


def scramble(hashed):
    hashed = jnp.bitwise_xor(hashed, lax.shift_right_logical(hashed, jnp.int32(16)))
    hashed = hashed * jnp.int32(mixer_two)
    hashed = jnp.bitwise_xor(hashed, lax.shift_right_logical(hashed, jnp.int32(13)))
    hashed = hashed * jnp.int32(mixer_three)
    return jnp.bitwise_xor(hashed, lax.shift_right_logical(hashed, jnp.int32(16)))


def dropout_keep(cell_index, hash_key):
    hashed = cell_index * jnp.int32(mixer_one) + hash_key[0]
    hashed = scramble(hashed)
    hashed = scramble(jnp.bitwise_xor(hashed, hash_key[1]))
    return jnp.bitwise_and(hashed, jnp.int32(65535)) >= keep_level


def gelu_slope(preact):
    factor = math.sqrt(2.0 / math.pi)
    tanh_value = jnp.tanh(factor * (preact + gelu_cubic * preact * preact * preact))
    return 0.5 * (1.0 + tanh_value) + 0.5 * preact * (1.0 - tanh_value * tanh_value) * factor * (
        1.0 + 3.0 * gelu_cubic * preact * preact
    )


def local(layer_input, cotangent, spectral_weight, bypass_weight, channel_bias, hash_key):
    highest = lax.Precision.HIGHEST
    slab_rows, slab_columns, channels, depth_cells = layer_input.shape
    column_devices = lax.axis_size("gy")
    row_offset = lax.axis_index("gx") * slab_rows
    column_offset = lax.axis_index("gy") * slab_columns
    across_table = hartley_table(KX, LX)
    down_table = lax.dynamic_slice_in_dim(hartley_table(KY, LY), column_offset, slab_columns, 1)
    depth_full = depth_table()
    depth_low = depth_full.T.astype(jnp.bfloat16)
    weight_modes = spectral_weight.astype(jnp.float32).reshape(
        spectral_weight.shape[0],
        spectral_weight.shape[1],
        spectral_weight.shape[2],
        channels,
        channels,
    )

    def forward_modes(source):
        depth_flat = jnp.dot(
            source.reshape(-1, depth_cells), depth_low, preferred_element_type=jnp.float32
        )
        partial_depth = depth_flat.reshape(slab_rows, slab_columns, channels, depth_low.shape[1])
        at_owner = lax.all_to_all(partial_depth, "gx", split_axis=3, concat_axis=0, tiled=True)
        swept = jnp.einsum("jx,xycm->jycm", across_table, at_owner, precision=highest)
        return lax.psum_scatter(
            jnp.einsum("ky,jycm->kmjc", down_table, swept, precision=highest),
            "gy",
            scatter_dimension=0,
            tiled=True,
        )

    def inverse_modes(mode_block):
        gathered = jnp.einsum(
            "ky,kmjc->jycm",
            down_table,
            lax.all_gather(mode_block, "gy", axis=0, tiled=True),
            precision=highest,
        )
        planes = jnp.einsum("jx,jycm->xycm", across_table, gathered, precision=highest)
        cell_modes = lax.all_to_all(planes, "gx", split_axis=0, concat_axis=3, tiled=True)
        flattened = jnp.dot(
            cell_modes.reshape(-1, cell_modes.shape[3]),
            depth_full,
            precision=highest,
            preferred_element_type=jnp.float32,
        )
        return flattened.reshape(slab_rows, slab_columns, channels, depth_cells)

    input_modes = forward_modes(layer_input)
    bypass = jnp.einsum(
        "xyct,cd->xydt", layer_input, bypass_weight, preferred_element_type=jnp.float32
    )
    row_ids = row_offset + jnp.arange(slab_rows, dtype=jnp.int32)
    column_ids = column_offset + jnp.arange(slab_columns, dtype=jnp.int32)
    channel_ids = jnp.arange(channels, dtype=jnp.int32)
    depth_ids = jnp.arange(depth_cells, dtype=jnp.int32)
    all_columns = slab_columns * column_devices
    cell_index = (
        (row_ids[:, None, None, None] * all_columns + column_ids[None, :, None, None]) * channels
        + channel_ids[None, None, :, None]
    ) * depth_cells + depth_ids[None, None, None, :]
    keep_mask = dropout_keep(cell_index, hash_key)
    mixed_modes = jnp.einsum("kmjc,kmjcd->kmjd", input_modes, weight_modes, precision=highest)
    spectral = inverse_modes(mixed_modes)
    preact = spectral + bypass + channel_bias[None, None, :, None]
    dpre = jnp.where(
        keep_mask, cotangent.astype(jnp.float32) * gelu_slope(preact) * keep_scale, 0.0
    ).astype(jnp.bfloat16)
    weight_local = jnp.einsum(
        "xyct,xydt->cd", layer_input, dpre, preferred_element_type=jnp.float32
    )
    bias_local = jnp.sum(dpre.astype(jnp.float32), axis=(0, 1, 3))
    weight_total, bias_total = lax.psum((weight_local, bias_local), ("gx", "gy"))
    norm_scale = 1.0 / math.sqrt(LX * LY * LZT)
    dpre_modes = forward_modes(dpre)
    grad_spectral = (input_modes[:, :, :, :, None] * dpre_modes[:, :, :, None, :]).reshape(
        spectral_weight.shape
    )
    backward_modes = jnp.einsum("kmjd,kmjcd->kmjc", dpre_modes, weight_modes, precision=highest)
    local_back = jnp.einsum(
        "xydt,cd->xyct", dpre, bypass_weight, preferred_element_type=jnp.float32
    )
    grad_input = (inverse_modes(backward_modes) + local_back).astype(jnp.bfloat16)
    return (grad_input, grad_spectral, weight_total * norm_scale, bias_total * norm_scale)


def solution(mesh):
    return jax.shard_map(
        local,
        mesh=mesh,
        in_specs=(
            P("gx", "gy", None, None),
            P("gx", "gy", None, None),
            P("gy", "gx", None, None),
            P(),
            P(),
            P(),
        ),
        out_specs=(P("gx", "gy", None, None), P("gy", "gx", None, None), P(), P()),
        check_vma=False,
    )
```

profile of v0, /device:TPU:1, one launch (start us, length us, event | category | flops | bytes accessed | tf_op | source)
XLA Modules:
  0.0 374.9 jit_solution(14677632297544402834)
XLA Ops:
  14.6 4.1 %copy.48 = f32[2,32,32,64]{2,1,0,3:T(8,128)} copy(f32[2,32,32,64]{3,2,1,0:T(8,128)} %bitcast.160) | data formatting | bytes 1048576 | tf_op jit(solution)/shard_map/reshape | solution.py:88
  21.8 15.4 %all-to-all-start = ((f32[64,1,2048]{2,1,0:T(1,128)}), f32[64,1,2048]{2,1,0:T(1,128)}, u32[]{:S(2)}, u32[]{:S(2)}) async-start(f32[64,1,2048]{2,1,0:T(1,128)} %reshape.306), calls=%async_computation | async-start | bytes 1048576 | tf_op jit(solution)/shard_map/all_to_all | solution.py:89
  37.6 16.5 %all-to-all-done = f32[64,1,2048]{2,1,0:T(1,128)} async-done(((f32[64,1,2048]{2,1,0:T(1,128)}), f32[64,1,2048]{2,1,0:T(1,128)}, u32[]{:S(2)}, u32[]{:S(2)}) %all-to-all-start) | async-done | bytes 524320 | tf_op jit(solution)/shard_map/all_to_all | solution.py:89
  54.6 3.7 reduce
  61.3 4.0 %fusion.20 = f32[32,32,32]{2,0,1:T(8,128)S(1)} fusion(f32[128,32,32]{2,1,0:T(8,128)} %bitcast.158, s32[32]{0:T(128)S(1)} %compare_select_fusion.2), kind=kOutput, calls=%fused_computation.32 | convolution fusion | flops 50397184 | bytes 655488 | tf_op jit(solution)/shard_map/jx,xycm->jycm/dot_general | solution.py:90
  69.6 3.7 reshape.278
  73.3 14.3 %reduce-scatter.3.cloned.1.call-done = f32[8,1,32,32]{3,2,1,0:T(8,128)} async-done(((f32[32,1,32,32]{3,2,1,0:T(8,128)}), f32[8,1,32,32]{3,2,1,0:T(8,128)}) %reduce-scatter.3.cloned.1.call-update) | async-done | bytes 32784 | tf_op jit(solution)/shard_map/reduce_scatter | solution.py:91
  87.6 3.4 fusion.87
  91.0 7.5 %all-gather = f32[32,32,32]{2,0,1:T(8,128)S(1)} all-gather(f32[8,32,32]{2,0,1:T(8,128)S(1)} %bitcast.165), channel_id=2, replica_groups=mesh['gx'=64,'gy'=4] {'gy'}, dimensions={0}, use_global_device_ids=true | all-gather | bytes 163840 | tf_op jit(solution)/shard_map/all_gather | solution.py:102
  105.2 3.8 %copy.53 = f32[128,32,32,1]{2,1,3,0:T(8,128)} copy(f32[128,32,32,1]{0,2,1,3:T(8,128)} %bitcast.162) | data formatting | bytes 1048576 | tf_op jit(solution)/shard_map/jx,jycm->xycm/dot_general | solution.py:105
  112.2 12.5 %all-to-all-start.1 = ((f32[64,1,2048]{2,1,0:T(1,128)}), f32[64,1,2048]{2,1,0:T(1,128)}, u32[]{:S(2)}, u32[]{:S(2)}) async-start(f32[64,1,2048]{2,1,0:T(1,128)} %reshape.308), calls=%async_computation.2 | async-start | bytes 1048576 | tf_op jit(solution)/shard_map/all_to_all | solution.py:106
  130.1 12.2 %all-to-all-done.1 = f32[64,1,2048]{2,1,0:T(1,128)} async-done(((f32[64,1,2048]{2,1,0:T(1,128)}), f32[64,1,2048]{2,1,0:T(1,128)}, u32[]{:S(2)}, u32[]{:S(2)}) %all-to-all-start.1) | async-done | bytes 524320 | tf_op jit(solution)/shard_map/all_to_all | solution.py:106
  149.9 3.6 fusion.24
  153.5 20.7 %convert_reduce_fusion = (f32[32]{0:T(128)S(1)}, bf16[2,32,32,512]{3,2,1,0:T(8,128)(2,1)S(1)}) fusion(f32[32]{0:T(128)S(1)} %copy-done.8, f32[2,32,32,512]{3,2,1,0:T(8,128)S(1)} %fusion.24, bf16[2,32,32,512]{3,2,1,0:T(8,128)(2,1)S(1)} %copy-done, bf16[32,32]{1,0:T(8,128)(2,1)S(1)} %copy-done.5, bf16[2,32,32,512]{3,2,1,0:T(8,128)(2,1)S(1)} %copy-done.7, ...), kind=kOutput, calls=%fused_computation.27 | convolution fusion | flops 117440480 | bytes 10496264 | tf_op jit(solution)/shard_map/xyct,cd->xydt/dot_general | solution.py:116
  181.6 23.8 %all_to_all.60 = f32[64,1,2048]{2,1,0:T(1,128)S(1)} all-to-all(f32[64,1,2048]{2,1,0:T(1,128)S(1)} %reshape.310), channel_id=1, replica_groups=mesh['gx'=64,'gy'=4] {'gx'}, dimensions={0} | all-to-all | bytes 1048576 | tf_op jit(solution)/shard_map/all_to_all | solution.py:89
  209.2 4.0 %fusion.18 = f32[32,32,32]{2,0,1:T(8,128)S(1)} fusion(f32[128,32,32]{2,1,0:T(8,128)} %bitcast.159, s32[32]{0:T(128)S(1)} %compare_select_fusion.2), kind=kOutput, calls=%fused_computation.30 | convolution fusion | flops 50397184 | bytes 655488 | tf_op jit(solution)/shard_map/jx,xycm->jycm/dot_general | solution.py:90
  215.6 18.2 %reduce-scatter.5.cloned.1.call-done = f32[8,1,32,32]{3,2,1,0:T(8,128)} async-done(((f32[32,1,32,32]{3,2,1,0:T(8,128)}), f32[8,1,32,32]{3,2,1,0:T(8,128)}) %reduce-scatter.5.cloned.1.call-update) | async-done | bytes 32784 | tf_op jit(solution)/shard_map/reduce_scatter | solution.py:91
  233.9 5.0 %fusion.88 = f32[8,32,1,32]{3,2,1,0:T(1,128)S(1)} fusion(f32[8,32,32,1]{2,3,1,0:T(1,128)} %bitcast.169, bf16[8,32,32,32]{3,2,1,0:T(8,128)(2,1)} %reshape.278), kind=kOutput, calls=%fused_computation.130 | convolution fusion | flops 3145728 | bytes 589824 | tf_op jit(solution)/shard_map/kmjd,kmjcd->kmjc/dot_general | solution.py:145
  239.0 7.3 %all-gather.1 = f32[32,32,32]{2,0,1:T(8,128)S(1)} all-gather(f32[8,32,32]{2,0,1:T(8,128)S(1)} %bitcast.166), channel_id=3, replica_groups=mesh['gx'=64,'gy'=4] {'gy'}, dimensions={0}, use_global_device_ids=true | all-gather | bytes 163840 | tf_op jit(solution)/shard_map/all_gather | solution.py:102
  251.4 3.3 reshape.312
  254.7 12.3 %all-to-all-start.3 = ((f32[64,1,2048]{2,1,0:T(1,128)}), f32[64,1,2048]{2,1,0:T(1,128)S(1)}, u32[]{:S(2)}, u32[]{:S(2)}) async-start(f32[64,1,2048]{2,1,0:T(1,128)} %reshape.312), calls=%async_computation.5 | async-start | bytes 1048576 | tf_op jit(solution)/shard_map/all_to_all | solution.py:106
  269.3 77.5 %all-reduce = (f32[32,32]{0,1:T(8,128)S(1)}, f32[32]{0:T(128)S(1)}) all-reduce(f32[32,32]{0,1:T(8,128)S(1)} %convolution_bitcast_fusion.5, f32[32]{0:T(128)S(1)} %get-tuple-element.26), channel_id=1, replica_groups=mesh['gx'=64,'gy'=4] {'gx','gy'}, use_global_device_ids=true, to_apply=%region_2.3 | all-reduce | flops 1056 | bytes 8448 | tf_op jit(solution)/shard_map/psum | solution.py:139
  351.1 4.6 %mul.399 = f32[8,1,32,1024]{3,2,1,0:T(8,128)} reshape(f32[8,32,32,32]{3,2,1,0:T(8,128)} %broadcast_multiply_fusion) | data formatting | bytes 2097152 | tf_op jit(solution)/shard_map/mul | solution.py:142
  362.2 3.6 fusion.22
  (74 shorter events, 75.3 us)
Async XLA Ops:
  7.2 3.6 copy-start
  21.8 32.3 %all-to-all-start = ((f32[64,1,2048]{2,1,0:T(1,128)}), f32[64,1,2048]{2,1,0:T(1,128)}, u32[]{:S(2)}, u32[]{:S(2)}) async-start(f32[64,1,2048]{2,1,0:T(1,128)} %reshape.306), calls=%async_computation | async-start | bytes 1048576 | tf_op jit(solution)/shard_map/all_to_all | solution.py:89
  37.2 50.4 %reduce-scatter.3.cloned.1.call-start = ((), (), s32[]{:S(2)}) async-start(), calls=%async_computation.6 | async-start | bytes 655360 | tf_op jit(solution)/shard_map/reduce_scatter | solution.py:91
  105.2 24.2 %copy-start.6 = (s32[2]{0:T(128)S(1)}, s32[2]{0:T(128)}, u32[]{:S(2)}) copy-start(s32[2]{0:T(128)} %param.11) | copy-start | bytes 28
  112.2 30.1 %all-to-all-start.1 = ((f32[64,1,2048]{2,1,0:T(1,128)}), f32[64,1,2048]{2,1,0:T(1,128)}, u32[]{:S(2)}, u32[]{:S(2)}) async-start(f32[64,1,2048]{2,1,0:T(1,128)} %reshape.308), calls=%async_computation.2 | async-start | bytes 1048576 | tf_op jit(solution)/shard_map/all_to_all | solution.py:106
  124.8 109.1 %reduce-scatter.5.cloned.1.call-start = ((), (), s32[]{:S(2)}) async-start(), calls=%async_computation.7 | async-start | bytes 655360 | tf_op jit(solution)/shard_map/reduce_scatter | solution.py:91
  147.3 6.2 %copy-start.5 = (bf16[32,32]{1,0:T(8,128)(2,1)S(1)}, bf16[32,32]{1,0:T(8,128)(2,1)}, u32[]{:S(2)}) copy-start(bf16[32,32]{1,0:T(8,128)(2,1)} %param.9) | copy-start | bytes 6148
  147.3 6.3 %copy-start.8 = (f32[32]{0:T(128)S(1)}, f32[32]{0:T(128)}, u32[]{:S(2)}) copy-start(f32[32]{0:T(128)} %param.10) | copy-start | bytes 388
  149.9 3.6 copy-start.7
  174.2 1.3 copy-start.1
  251.4 96.6 %copy-start.3 = (f32[8,1,32,32]{3,2,1,0:T(8,128)S(1)}, f32[8,1,32,32]{3,2,1,0:T(8,128)}, u32[]{:S(2)}) copy-start(f32[8,1,32,32]{3,2,1,0:T(8,128)} %reduce-scatter.3.cloned.1.call-done) | copy-start | bytes 98308
  251.4 96.6 %copy-start.4 = (f32[8,1,32,32]{3,2,1,0:T(8,128)S(1)}, f32[8,1,32,32]{3,2,1,0:T(8,128)}, u32[]{:S(2)}) copy-start(f32[8,1,32,32]{3,2,1,0:T(8,128)} %reduce-scatter.5.cloned.1.call-done) | copy-start | bytes 98308
  254.7 100.9 %all-to-all-start.3 = ((f32[64,1,2048]{2,1,0:T(1,128)}), f32[64,1,2048]{2,1,0:T(1,128)S(1)}, u32[]{:S(2)}, u32[]{:S(2)}) async-start(f32[64,1,2048]{2,1,0:T(1,128)} %reshape.312), calls=%async_computation.5 | async-start | bytes 1048576 | tf_op jit(solution)/shard_map/all_to_all | solution.py:106
  362.2 3.6 copy-start.2
Sparse Core Ops, SparseCore 0:
  69.7 17.8 reduce-scatter.2
  215.8 18.0 reduce-scatter.4
where the time goes:
time: 381 us; the launch traced here: 375 us
  blocking collectives  116 us (30%)
  local copies, waits for them, and re-layouts  65.8 us (17%)
  waiting for transfers between devices  61.3 us (16%)
  matrix products  60 us (16%)
  starting transfers between devices  40.8 us (11%)
  other arithmetic  16.3 us (4%)
  between operations  14.5 us (4%)
    psum x1, blocking collectives, local(): lax.psum((weight_local, bias_local), ('gx', 'gy'))  77.5 us
    reduce_scatter x2, waiting for transfers between devices, forward_modes(): lax.psum_scatter(jnp.einsum('ky,jycm->kmjc', down_table, swept, precision...  32.5 us
    all_to_all x2, starting transfers between devices, inverse_modes(): lax.all_to_all(planes, 'gx', split_axis=0, concat_axis=3, tiled=True)  24.9 us
    all_to_all x1, blocking collectives, forward_modes(): lax.all_to_all(partial_depth, 'gx', split_axis=3, concat_axis=0, tiled=True)  23.8 us
    unnamed x27, local copies, waits for them, and re-layouts  23.1 us
    dot_general x1, matrix products, local(): jnp.einsum('xyct,cd->xydt', layer_input, bypass_weight, preferred_element...  20.7 us
    all_to_all x1, waiting for transfers between devices, forward_modes(): lax.all_to_all(partial_depth, 'gx', split_axis=3, concat_axis=0, tiled=True)  16.5 us
    all_to_all x1, starting transfers between devices, forward_modes(): lax.all_to_all(partial_depth, 'gx', split_axis=3, concat_axis=0, tiled=True)  15.4 us
  transfers between devices with their start and end apart: 5, of which 4 were waited for; matrix products, arithmetic and copies ran while one was open for 5% of the time, Pallas kernels for 0%

commit v1 on v0

v1 whole, which is shorter than its diff:
```python
import functools
import math

import jax
import jax.numpy as jnp
import numpy as np
from jax import lax
from jax.experimental import pallas as pl
from jax.experimental.pallas import tpu as pltpu
from jax.sharding import PartitionSpec as P

LX = 128
LY = 128
LZ = 64
LT = 8
KX = 32
KY = 32
KZ = 16
KT = 4
C = 32
LZT = 512
KZT = 64
GX = 64
GY = 4
ROWS = 256
F32 = jnp.float32
BF16 = jnp.bfloat16
HIGHEST = lax.Precision.HIGHEST

keep_level = 6554
keep_scale = 1.0 / 0.9
gelu_cubic = 0.044715
mixer_one = -1640531535
mixer_two = -2048144789
mixer_three = -1028477387
norm_scale = 1.0 / math.sqrt(LX * LY * LZT)


def hartley_table(kept, length):
    wanted = np.arange(kept)
    frequency = np.where(wanted < kept // 2, wanted, wanted + (length - kept))
    residue = frequency[:, None] * np.arange(length)[None, :] % length
    radians = residue * (2.0 * math.pi / length)
    return ((np.cos(radians) + np.sin(radians)) / math.sqrt(length)).astype(np.float32)


def depth_table():
    joined = hartley_table(KZ, LZ)[:, None, :, None] * hartley_table(KT, LT)[None, :, None, :]
    return joined.reshape(KZT, LZT)


def split_table(table):
    high = table.astype(jnp.bfloat16)
    return high, (table - high.astype(np.float32)).astype(jnp.bfloat16)


def down_by_device():
    down = hartley_table(KY, LY)
    picked = []
    for q in range(GY):
        order = [
            ((side * 2 + (q % 2 + swap) % 2) * 8 + k)
            for swap in range(2)
            for side in range(2)
            for k in range(8)
        ]
        picked.append(down[order][:, q * 32 : (q + 1) * 32])
    return np.stack(picked)


def tables():
    down = down_by_device()
    spread = lambda t: np.repeat(t, C, axis=2)
    depth = depth_table()
    depth_high, depth_rest = split_table(depth)
    across = hartley_table(KX, LX)
    gather = np.concatenate([np.repeat(across[:, x::2], 2, axis=1) for x in range(2)], axis=1)
    scatter = np.concatenate([across[:, x::2].T for x in range(2)], axis=0)
    eye = np.eye(C, dtype=np.float32)
    return dict(
        down_cells=spread(down.transpose(0, 2, 1)),
        down_modes=spread(down),
        depth_low=depth_high,
        depth_stack=np.concatenate([depth_high, depth_high, depth_rest], axis=0),
        gather=gather,
        scatter=scatter,
        expand=np.concatenate([np.repeat(eye, C, axis=1)] * 2, axis=0).astype(jnp.bfloat16),
        tile4=np.concatenate([np.tile(eye, (1, 4))] * 2, axis=0).astype(jnp.bfloat16),
        fold4=np.concatenate([np.tile(eye, (4, 8))] * 2, axis=0).astype(jnp.bfloat16),
        fold32=np.tile(np.repeat(eye, C, axis=0), (1, 8)).astype(jnp.bfloat16),
        fold8=np.concatenate([np.tile(eye, (8, 1)), np.zeros((256, 96), np.float32)], axis=1),
    )


def halves(value):
    high = value.astype(BF16)
    return high, (value - high.astype(F32)).astype(BF16)


def mm(a, b):
    return jnp.dot(a, b, preferred_element_type=F32)


def mm_nt(a, b):
    return lax.dot_general(a, b, (((1,), (1,)), ((), ())), preferred_element_type=F32)


def mm_tn(a, b):
    return lax.dot_general(a, b, (((0,), (0,)), ((), ())), preferred_element_type=F32)


def build_spread(table_ref, high_ref, rest_ref):
    q = lax.axis_index("gy")
    shape = (C, 32 * C)
    mask = lax.broadcasted_iota(jnp.int32, shape, 0) == (
        lax.broadcasted_iota(jnp.int32, shape, 1) & (C - 1)
    )
    for row in range(32):
        line = table_ref[q, pl.ds(row, 1), :]
        value = jnp.where(mask, line, 0.0)
        high, rest = halves(value)
        high_ref[pl.ds(row * C, C), :] = high
        rest_ref[pl.ds(row * C, C), :] = rest


def times_spread(value, high_ref, rest_ref):
    high, rest = halves(value)
    return mm(high, high_ref[...]) + mm(rest, high_ref[...]) + mm(high, rest_ref[...])


def send_modes(modes, own_ref, other_ref, lines):
    for swap, ref in enumerate((own_ref, other_ref)):
        for side in range(2):
            for x in range(2):
                for half in range(2):
                    at = ((swap * 2 + side) * 2 + half) * 128
                    ref[pl.ds(side * lines + x * 2 + half, KZT, stride=2 * lines), :] = modes[
                        x * KZT : (x + 1) * KZT, at : at + 128
                    ]


def received_modes(own_ref, other_ref, lines):
    rows = []
    for x in range(2):
        parts = []
        for ref in (own_ref, other_ref):
            for side in range(2):
                for half in range(2):
                    parts.append(ref[pl.ds(side * lines + x * 2 + half, KZT, stride=2 * lines), :])
        rows.append(jnp.concatenate(parts, axis=1))
    return jnp.concatenate(rows, axis=0)


def block_mixing(weight_ref):
    weight = weight_ref[...].astype(F32)
    wide = jnp.concatenate([weight] * 8, axis=1)
    full = jnp.concatenate([wide] * 8, axis=0)
    shape = (ROWS, ROWS)
    same = (lax.broadcasted_iota(jnp.int32, shape, 0) >> 5) == (
        lax.broadcasted_iota(jnp.int32, shape, 1) >> 5
    )
    return jnp.where(same, full, 0.0)


def fill_inverse(own_ref, other_ref, lines, down_ref, high_ref, rest_ref, stack_ref):
    build_spread(down_ref, high_ref, rest_ref)
    cells = times_spread(received_modes(own_ref, other_ref, lines), high_ref, rest_ref)
    high, rest = halves(cells)
    for x in range(2):
        part = slice(x * KZT, (x + 1) * KZT)
        stack_ref[x, 0:KZT, :] = high[part]
        stack_ref[x, KZT : 2 * KZT, :] = rest[part]
        stack_ref[x, 2 * KZT : 3 * KZT, :] = high[part]


def forward_kernel(field, depth_low, down, own, other, flat, high, rest):
    step = pl.program_id(0)

    @pl.when(step == 0)
    def _():
        build_spread(down, high, rest)

    x, block = step // 4, step % 4
    flat[x, block] = mm_nt(depth_low[...], field[...])

    @pl.when(step == 7)
    def _():
        send_modes(times_spread(joined(flat), high, rest), own, other, 4)


def joined(flat):
    return jnp.concatenate(
        [jnp.concatenate([flat[x, block] for block in range(4)], axis=1) for x in range(2)], axis=0
    )


def scramble(hashed):
    hashed = jnp.bitwise_xor(hashed, lax.shift_right_logical(hashed, jnp.int32(16)))
    hashed = hashed * jnp.int32(mixer_two)
    hashed = jnp.bitwise_xor(hashed, lax.shift_right_logical(hashed, jnp.int32(13)))
    hashed = hashed * jnp.int32(mixer_three)
    return jnp.bitwise_xor(hashed, lax.shift_right_logical(hashed, jnp.int32(16)))


def dropout_kernel(key, cotangent, kept):
    step = pl.program_id(0)
    x, block = step // 4, step % 4
    plane = lax.axis_index("gx") * 2 + x
    column = lax.axis_index("gy") * 32 + block * 8
    first = (plane * LY + column) * (C * LZT)
    shape = (16, LZT)
    inside = (
        lax.broadcasted_iota(jnp.int32, shape, 0) * LZT + lax.broadcasted_iota(jnp.int32, shape, 1)
    ) * jnp.int32(mixer_one)

    def body(chunk, carry):
        start = (first + chunk * (16 * LZT)) * jnp.int32(mixer_one) + key[0]
        hashed = scramble(inside + start)
        hashed = scramble(jnp.bitwise_xor(hashed, key[1]))
        keep = jnp.bitwise_and(hashed, jnp.int32(65535)) >= keep_level
        rows = pl.ds(pl.multiple_of(chunk * 16, 16), 16)
        kept[rows, :] = jnp.where(keep, cotangent[rows, :].astype(F32), 0.0).astype(BF16)
        return carry

    lax.fori_loop(0, ROWS // 16, body, 0)


def gathered_modes(messages, gather, lines):
    slabs = [
        jnp.concatenate([messages[pl.ds(x * 2 + half, 128, stride=lines), :] for half in range(2)], axis=1)
        for x in range(2)
    ]
    return jnp.dot(gather[...], jnp.concatenate(slabs, axis=0), precision=HIGHEST, preferred_element_type=F32)


def by_mode(modes):
    return jnp.concatenate([modes[:, k * C : (k + 1) * C] for k in range(8)], axis=0)


def wide_halves(value):
    return jnp.concatenate(halves(value), axis=1)


def scatter_planes(repeated, scatter, out, lines):
    lane = lax.broadcasted_iota(jnp.int32, (KX, ROWS), 1) >> 5
    modes = jnp.zeros((KX, ROWS), F32)
    for k in range(8):
        modes = jnp.where(lane == k, repeated[k * KX : (k + 1) * KX, :], modes)
    planes = jnp.dot(scatter[...], modes, precision=HIGHEST, preferred_element_type=F32)
    for x in range(2):
        for half in range(2):
            piece = planes[x * GX : (x + 1) * GX, half * 128 : (half + 1) * 128]
            for side in range(2):
                out[pl.ds(side * lines + x * 2 + half, GX, stride=2 * lines), :] = piece


def mix_kernel(messages, weight, gather, scatter, expand, fold4, out, modes_out):
    modes = gathered_modes(messages, gather, 4)
    modes_out[...] = modes
    spread = mm(wide_halves(by_mode(modes)), expand[...])
    total = jnp.zeros((ROWS, 128), F32)
    for j in range(8):
        part = slice(j * 128, (j + 1) * 128)
        total = total + spread[:, part] * weight[:, part].astype(F32)
    repeated = mm(wide_halves(total), fold4[...])
    scatter_planes(repeated, scatter, out, 4)


def back_kernel(messages, modes, weight, gather, scatter, expand, tile4, fold32, out, grad):
    dmodes = wide_halves(by_mode(gathered_modes(messages, gather, 5)))
    tiled = mm(dmodes, tile4[...])
    spread = mm(wide_halves(by_mode(modes[...])), expand[...])
    repeated = jnp.zeros((ROWS, ROWS), F32)
    for j in range(8):
        part = slice(j * 128, (j + 1) * 128)
        grad[:, part] = spread[:, part] * tiled
        high, rest = halves(weight[:, part].astype(F32) * tiled)
        repeated = repeated + mm(high, fold32[part, :]) + mm(rest, fold32[part, :])
    scatter_planes(repeated, scatter, out, 5)
    total = jnp.sum(messages[pl.ds(4, 128, stride=5), :], axis=0, keepdims=True)
    out[pl.ds(4, 128, stride=5), :] = jnp.broadcast_to(total, (128, 128))


def gelu_slope(preact):
    factor = math.sqrt(2.0 / math.pi)
    square = preact * preact
    tanh_value = jnp.tanh(preact * (factor + (factor * gelu_cubic) * square))
    rest = preact * (0.5 * factor + (1.5 * factor * gelu_cubic) * square)
    return 0.5 + 0.5 * tanh_value + rest * (1.0 - tanh_value * tanh_value)


def middle_kernel(
    own_in, other_in, field, kept, bias, bypass, depth_stack, depth_low, down_modes, down_cells, fold8,
    dpre, own, other,
    high_in, rest_in, high, rest, stack, mixing, preact, flat, sums, bias_sums,
):
    step = pl.program_id(0)
    x, block = step // 4, step % 4

    @pl.when(step == 0)
    def _():
        fill_inverse(own_in, other_in, 4, down_modes, high_in, rest_in, stack)
        build_spread(down_cells, high, rest)
        mixing[...] = jnp.transpose(block_mixing(bypass)).astype(BF16)
        sums[...] = jnp.zeros_like(sums)
        bias_sums[...] = jnp.zeros_like(bias_sums)

    columns = pl.ds(pl.multiple_of(block * ROWS, ROWS), ROWS)
    preact[...] = mm_tn(stack[x, :, columns], depth_stack[...]) + mm(mixing[...], field[...])

    def body(chunk, carry):
        rows = pl.ds(pl.multiple_of(chunk * 16, 16), 16)
        shift = bias[pl.ds(pl.multiple_of((chunk % 2) * 16, 16), 16), :]
        slope = gelu_slope(preact[rows, :] + shift)
        dpre[rows, :] = (kept[rows, :].astype(F32) * slope * keep_scale).astype(BF16)
        return carry

    lax.fori_loop(0, ROWS // 16, body, 0)
    flat[x, block] = mm_nt(depth_low[...], dpre[...])
    sums[...] += mm_nt(field[...], dpre[...])
    bias_sums[...] += mm_nt(jnp.ones((16, LZT), BF16), dpre[...])

    @pl.when(step == 7)
    def _():
        send_modes(times_spread(joined(flat), high, rest), own, other, 5)
        lane = lax.broadcasted_iota(jnp.int32, (C, ROWS), 1) >> 5
        picked = jnp.zeros((C, ROWS), F32)
        for k in range(8):
            picked = jnp.where(lane == k, sums[k * C : (k + 1) * C, :], picked)
        both = jnp.concatenate([picked, bias_sums[...], jnp.zeros((16, ROWS), F32)], axis=0)
        folded = jnp.dot(both, fold8[...], precision=HIGHEST, preferred_element_type=F32)
        for side in range(2):
            own[pl.ds(side * 5 + 4, KZT, stride=10), :] = folded
            other[pl.ds(side * 5 + 4, KZT, stride=10), :] = jnp.zeros((KZT, 128), F32)


def last_kernel(
    own_in, other_in, dpre, bypass, depth_stack, down_modes,
    grad, grad_weight, grad_bias,
    high_in, rest_in, stack, mixing,
):
    step = pl.program_id(0)
    x, block = step // 4, step % 4

    @pl.when(step == 0)
    def _():
        fill_inverse(own_in, other_in, 5, down_modes, high_in, rest_in, stack)
        mixing[...] = block_mixing(bypass).astype(BF16)
        total = own_in[pl.ds(4, KZT, stride=10), :] + other_in[pl.ds(4, KZT, stride=10), :]
        total = total * norm_scale
        grad_weight[...] = total[0:C, 0:C]
        grad_bias[...] = total[C : C + 8, 0:C]

    columns = pl.ds(pl.multiple_of(block * ROWS, ROWS), ROWS)
    grad[...] = (mm_tn(stack[x, :, columns], depth_stack[...]) + mm(mixing[...], dpre[...])).astype(BF16)


def whole(shape):
    return pl.BlockSpec(shape, lambda *_: (0,) * len(shape))


def rows_block():
    return pl.BlockSpec((ROWS, LZT), lambda i: (i, 0))


SMEM = pl.BlockSpec(memory_space=pltpu.SMEM)
PARAMS = pltpu.CompilerParams(vmem_limit_bytes=48 * 1024 * 1024)


def like(*shape, dtype=F32):
    return jax.ShapeDtypeStruct(shape, dtype)


def call(kernel, name, grid, ins, outs, scratch, out_shape):
    return pl.pallas_call(
        kernel,
        name=name,
        grid=grid,
        in_specs=ins,
        out_specs=outs,
        out_shape=out_shape,
        scratch_shapes=scratch,
        compiler_params=PARAMS,
    )


def swap_cores(value):
    return lax.ppermute(value, "gy", [(i, i ^ 1) for i in range(GY)])


def exchange(messages, lines):
    groups = [[(g * 2 + side) * 2 + core for g in range(GX) for side in range(2)] for core in range(2)]
    shaped = messages.reshape(128, 1, lines * 128)
    moved = lax.all_to_all(
        shaped, ("gx", "gy"), split_axis=0, concat_axis=0, tiled=True, axis_index_groups=groups
    )
    return moved.reshape(128 * lines, 128)


def local(layer_input, cotangent, spectral_weight, bypass_weight, channel_bias, hash_key):
    table = {name: jnp.asarray(value) for name, value in tables().items()}
    field = layer_input.reshape(-1, LZT)
    weight = spectral_weight.reshape(ROWS, C * C)
    square = lambda: pltpu.VMEM((1024, 1024), BF16)
    flat = pltpu.VMEM((2, 4, KZT, ROWS), F32)
    stack = pltpu.VMEM((2, 3 * KZT, 1024), BF16)

    own, other = call(
        forward_kernel,
        "forward",
        (8,),
        [rows_block(), whole((KZT, LZT)), whole((GY, 32, 1024))],
        [whole((512, 128))] * 2,
        [flat, square(), square()],
        [like(512, 128)] * 2,
    )(field, table["depth_low"], table["down_cells"])
    messages = exchange(own + swap_cores(other), 4)

    kept = call(
        dropout_kernel, "dropout", (8,), [SMEM, rows_block()], rows_block(), [], like(2048, LZT, dtype=BF16)
    )(hash_key, cotangent.reshape(-1, LZT))

    planes, modes = call(
        mix_kernel,
        "mix",
        (1,),
        [whole((512, 128)), whole((ROWS, 1024)), whole((32, 256)), whole((128, 32)), whole((64, 1024)), whole((256, 256))],
        [whole((512, 128)), whole((KX, ROWS))],
        [],
        [like(512, 128), like(KX, ROWS)],
    )(messages, weight, table["gather"], table["scatter"], table["expand"], table["fold4"])
    own_cells = exchange(planes, 4)
    other_cells = swap_cores(own_cells)

    wide_bias = jnp.broadcast_to(channel_bias[:, None], (C, LZT))
    dpre, own, other = call(
        middle_kernel,
        "middle",
        (8,),
        [
            whole((512, 128)), whole((512, 128)), rows_block(), rows_block(), whole((C, LZT)), whole((C, C)),
            whole((192, LZT)), whole((KZT, LZT)), whole((GY, 32, 1024)), whole((GY, 32, 1024)), whole((256, 128)),
        ],
        [rows_block(), whole((640, 128)), whole((640, 128))],
        [
            square(), square(), square(), square(), stack,
            pltpu.VMEM((ROWS, ROWS), BF16), pltpu.VMEM((ROWS, LZT), F32), flat,
            pltpu.VMEM((ROWS, ROWS), F32), pltpu.VMEM((16, ROWS), F32),
        ],
        [like(2048, LZT, dtype=BF16), like(640, 128), like(640, 128)],
    )(
        own_cells, other_cells, field, kept, wide_bias, bypass_weight,
        table["depth_stack"], table["depth_low"], table["down_modes"], table["down_cells"], table["fold8"],
    )
    messages = exchange(own + swap_cores(other), 5)

    planes, grad_spectral = call(
        back_kernel,
        "back",
        (1,),
        [
            whole((640, 128)), whole((KX, ROWS)), whole((ROWS, 1024)), whole((32, 256)), whole((128, 32)),
            whole((64, 1024)), whole((64, 128)), whole((1024, 256)),
        ],
        [whole((640, 128)), whole((ROWS, 1024))],
        [],
        [like(640, 128), like(ROWS, 1024)],
    )(
        messages, modes, weight, table["gather"], table["scatter"], table["expand"], table["tile4"], table["fold32"]
    )
    own_cells = exchange(planes, 5)
    other_cells = swap_cores(own_cells)

    grad_input, grad_weight, grad_bias = call(
        last_kernel,
        "last",
        (8,),
        [whole((640, 128)), whole((640, 128)), rows_block(), whole((C, C)), whole((192, LZT)), whole((GY, 32, 1024))],
        [rows_block(), whole((C, C)), whole((8, C))],
        [square(), square(), stack, pltpu.VMEM((ROWS, ROWS), BF16)],
        [like(2048, LZT, dtype=BF16), like(C, C), like(8, C)],
    )(own_cells, other_cells, dpre, bypass_weight, table["depth_stack"], table["down_modes"])
    return (
        grad_input.reshape(layer_input.shape),
        grad_spectral.reshape(spectral_weight.shape),
        grad_weight,
        grad_bias[0],
    )


def solution(mesh):
    return jax.shard_map(
        local,
        mesh=mesh,
        in_specs=(
            P("gx", "gy", None, None),
            P("gx", "gy", None, None),
            P("gy", "gx", None, None),
            P(),
            P(),
            P(),
        ),
        out_specs=(P("gx", "gy", None, None), P("gy", "gx", None, None), P(), P()),
        check_vma=False,
    )
```

time: 381 us -> 138 us (0.36); the launches traced: 375 us -> 138 us
  local copies, waits for them, and re-layouts: 65.8 us -> 5.45 us
  matrix products: 60 us -> 0 us
  waiting for transfers between devices: 61.3 us -> 4.03 us
  blocking collectives: 116 us -> 84.4 us
  Pallas kernels: 0 us -> 31.2 us
  starting transfers between devices: 40.8 us -> 11.7 us
  other arithmetic: 16.3 us -> 0.07 us
  between operations: 14.5 us -> 0.85 us
    psum x1 -> x0, blocking collectives: 77.5 us -> none  [local(): lax.psum((weight_local, bias_local), ('gx', 'gy'))]
    all_to_all x1 -> x4, blocking collectives: 23.8 us -> 84.4 us  [exchange(): lax.all_to_all(shaped, ('gx', 'gy'), split_axis=0, concat_axis=0, tiled=T...]
    dot_general x15 -> x0, matrix products: 56.7 us -> none  [the longest x1 20.7 us: local(): jnp.einsum('xyct,cd->xydt', layer_input, bypass_weight, preferred_element...]
    all_to_all x3 -> x0, starting transfers between devices: 40.2 us -> none  [the longest x2 24.9 us: inverse_modes(): lax.all_to_all(planes, 'gx', split_axis=0, concat_axis=3, tiled=True)]
    reduce_scatter x2 -> x0, waiting for transfers between devices: 32.5 us -> none  [forward_modes(): lax.psum_scatter(jnp.einsum('ky,jycm->kmjc', down_table, swept, precision...]
    pallas_call x0 -> x6, Pallas kernels: none -> 31.2 us  [the longest x1 14 us: local(): call(middle_kernel, 'middle', (8,), [whole((512, 128)), whole((512, 128))...]
    all_to_all x3 -> x0, waiting for transfers between devices: 28.7 us -> none  [the longest x1 16.5 us: forward_modes(): lax.all_to_all(partial_depth, 'gx', split_axis=3, concat_axis=0, tiled=True)]
    unnamed x27 -> x40, local copies, waits for them, and re-layouts: 23.1 us -> 4.87 us
  transfers between devices with their start and end apart: 5 -> 4, of which waited for: 4 -> 3; matrix products, arithmetic and copies ran while one was open for 5% -> 0% of each run, Pallas kernels for 0% -> 3%
where the time goes in v1:
time: 138 us
  blocking collectives  84.4 us (61%)
  Pallas kernels  31.2 us (23%)
  starting transfers between devices  11.7 us (8%)
  local copies, waits for them, and re-layouts  5.45 us (4%)
  waiting for transfers between devices  4.03 us (3%)
    all_to_all x4, blocking collectives, exchange(): lax.all_to_all(shaped, ('gx', 'gy'), split_axis=0, concat_axis=0, tiled=T...  84.4 us
    pallas_call x1, Pallas kernels, local(): call(middle_kernel, 'middle', (8,), [whole((512, 128)), whole((512, 128))...  14 us
    ppermute x4, starting transfers between devices, swap_cores(): return lax.ppermute(value, 'gy', [(i, i ^ 1) for i in range(GY)])  11.7 us
    pallas_call x1, Pallas kernels, local(): call(last_kernel, 'last', (8,), [whole((640, 128)), whole((640, 128)), ro...  5.73 us
    unnamed x40, local copies, waits for them, and re-layouts  4.87 us
    pallas_call x1, Pallas kernels, local(): call(dropout_kernel, 'dropout', (8,), [SMEM, rows_block()], rows_block(),...  4.68 us
    ppermute x4, waiting for transfers between devices, swap_cores(): return lax.ppermute(value, 'gy', [(i, i ^ 1) for i in range(GY)])  4.03 us
    pallas_call x1, Pallas kernels, local(): call(forward_kernel, 'forward', (8,), [rows_block(), whole((KZT, LZT)), w...  3.41 us
  transfers between devices with their start and end apart: 4, of which 3 were waited for; matrix products, arithmetic and copies ran while one was open for 0% of the time, Pallas kernels for 3%

profile of v1, /device:TPU:1, one launch (start us, length us, event | category | flops | bytes accessed | tf_op | source)
XLA Modules:
  0.0 137.7 jit_solution(3142616804638556336)
XLA Ops:
  0.6 1.6 %copy-done = bf16[2,32,32,512]{3,2,1,0:T(8,128)(2,1)S(1)} copy-done((bf16[2,32,32,512]{3,2,1,0:T(8,128)(2,1)S(1)}, bf16[2,32,32,512]{3,2,1,0:T(8,128)(2,1)}, u32[]{:S(2)}) %copy-start) | copy-done | bytes 2097176
  2.2 1.0 copy-done.5
  3.3 0.8 copy-done.11
  4.1 0.0 copy-start.15
  4.1 3.4 %forward.1 = (f32[512,128]{1,0:T(8,128)S(1)}, f32[512,128]{1,0:T(8,128)S(1)}) custom-call(bf16[2048,512]{1,0:T(8,128)(2,1)S(1)} %bitcast.18, bf16[64,512]{1,0:T(8,128)(2,1)S(1)} %copy-done.11, f32[4,32,1024]{2,1,0:T(8,128)S(1)} %copy-done.5), custom_call_target="tpu_custom_call" | custom-call | tf_op jit(solution)/shard_map/forward/pallas_call | solution.py:408
  7.6 3.3 %collective-permute-start = (f32[512,128]{1,0:T(8,128)S(1)}, f32[512,128]{1,0:T(8,128)S(1)}, u32[]{:S(2)}, u32[]{:S(2)}) collective-permute-start(f32[512,128]{1,0:T(8,128)S(1)} %get-tuple-element.17), channel_id=1, source_target_pairs={{0,1},{1,0},{2,3},{3,2},{4,5},{5,4},{6,7},{7,6},{8,9},{9,8},{10,11... | collective-permute-start | bytes 786440 | tf_op jit(solution)/shard_map/ppermute | solution.py:388
  10.9 1.2 collective-permute-done
  12.1 26.5 %all_to_all.20 = f32[128,1,512]{2,1,0:T(1,128)S(1)} all-to-all(f32[128,1,512]{2,1,0:T(1,128)S(1)} %bitcast.31), channel_id=1, replica_groups={{0,2,4,6,8,10,12,14,16,18,20,22,24,26,28,30,32,34,36,38,40,42,44,46,48,..., dimensions={0} | all-to-all | bytes 524288 | tf_op jit(solution)/shard_map/all_to_all | solution.py:394
  38.6 1.3 mix.1
  40.0 18.7 %all_to_all.21 = f32[128,1,512]{2,1,0:T(1,128)S(1)} all-to-all(f32[128,1,512]{2,1,0:T(1,128)S(1)} %bitcast.29), channel_id=1, replica_groups={{0,2,4,6,8,10,12,14,16,18,20,22,24,26,28,30,32,34,36,38,40,42,44,46,48,..., dimensions={0} | all-to-all | bytes 524288 | tf_op jit(solution)/shard_map/all_to_all | solution.py:394
  58.7 3.7 %collective-permute-start.1 = (f32[512,128]{1,0:T(8,128)S(1)}, f32[512,128]{1,0:T(8,128)S(1)}, u32[]{:S(2)}, u32[]{:S(2)}) collective-permute-start(f32[512,128]{1,0:T(8,128)S(1)} %bitcast.25), channel_id=1, source_target_pairs={{0,1},{1,0},{2,3},{3,2},{4,5},{5,4},{6,7},{7,6},{8,9},{9,8},{10,11... | collective-permute-start | bytes 786440 | tf_op jit(solution)/shard_map/ppermute | solution.py:388
  62.4 4.7 %dropout.1.kept = bf16[2048,512]{1,0:T(8,128)(2,1)S(1)} custom-call(s32[2]{0:T(128)S(1)} %copy-done.18, bf16[2048,512]{1,0:T(8,128)(2,1)S(1)} %bitcast.21), custom_call_target="tpu_custom_call" | custom-call | tf_op jit(solution)/shard_map/dropout/pallas_call | solution.py:419
  67.1 1.3 copy-done.1
  68.4 0.1 broadcast_in_dim.2.bias
  68.6 14.0 %middle.1 = (bf16[2048,512]{1,0:T(8,128)(2,1)S(1)}, f32[640,128]{1,0:T(8,128)S(1)}, f32[640,128]{1,0:T(8,128)S(1)}) custom-call(f32[512,128]{1,0:T(8,128)S(1)} %bitcast.26, f32[512,128]{1,0:T(8,128)S(1)} %collective-permute-done.1.other_in, bf16[2048,512]{1,0:T(8,128)(2,1)} %bitcast.17, bf16[2048,512]{1,0:T(8,128)(2,1)} %copy-done.1, ...), custom_call_target="tpu_custom_call" | custom-call | tf_op jit(solution)/shard_map/middle/pallas_call | solution.py:436
  82.6 0.1 collective-permute-start.2
  82.7 1.6 %collective-permute-done.2 = f32[640,128]{1,0:T(8,128)S(1)} collective-permute-done((f32[640,128]{1,0:T(8,128)S(1)}, f32[640,128]{1,0:T(8,128)S(1)}, u32[]{:S(2)}, u32[]{:S(2)}) %collective-permute-start.2) | collective-permute-done | bytes 327712 | tf_op jit(solution)/shard_map/ppermute | solution.py:388
  84.4 20.3 %all_to_all.22 = f32[128,1,640]{2,1,0:T(1,128)S(1)} all-to-all(f32[128,1,640]{2,1,0:T(1,128)S(1)} %bitcast.30), channel_id=1, replica_groups={{0,2,4,6,8,10,12,14,16,18,20,22,24,26,28,30,32,34,36,38,40,42,44,46,48,..., dimensions={0} | all-to-all | bytes 655360 | tf_op jit(solution)/shard_map/all_to_all | solution.py:394
  104.7 2.0 %back.1 = (f32[640,128]{1,0:T(8,128)S(1)}, f32[256,1024]{1,0:T(8,128)}) custom-call(f32[640,128]{1,0:T(8,128)S(1)} %bitcast.22, f32[32,256]{1,0:T(8,128)S(1)} %get-tuple-element.21.modes, bf16[256,1024]{1,0:T(8,128)(2,1)S(1)} %bitcast.20, f32[32,256]{1,0:T(8,128)S(1)} %copy-done.15, f32[128,32]{1,0:T(8,128)S(1)} %copy-done.10, ...), custom_call_target="tpu_custom_call" | custom-call | tf_op jit(solution)/shard_map/back/pallas_call | solution.py:457
  106.8 18.8 %all_to_all.23 = f32[128,1,640]{2,1,0:T(1,128)S(1)} all-to-all(f32[128,1,640]{2,1,0:T(1,128)S(1)} %bitcast.28), channel_id=1, replica_groups={{0,2,4,6,8,10,12,14,16,18,20,22,24,26,28,30,32,34,36,38,40,42,44,46,48,..., dimensions={0} | all-to-all | bytes 655360 | tf_op jit(solution)/shard_map/all_to_all | solution.py:394
  125.6 4.6 %collective-permute-start.3 = (f32[640,128]{1,0:T(8,128)S(1)}, f32[640,128]{1,0:T(8,128)S(1)}, u32[]{:S(2)}, u32[]{:S(2)}) collective-permute-start(f32[640,128]{1,0:T(8,128)S(1)} %bitcast.23), channel_id=1, source_target_pairs={{0,1},{1,0},{2,3},{3,2},{4,5},{5,4},{6,7},{7,6},{8,9},{9,8},{10,11... | collective-permute-start | bytes 983048 | tf_op jit(solution)/shard_map/ppermute | solution.py:388
  130.2 1.3 collective-permute-done.3.other_in
  131.5 5.7 %last.1 = (bf16[2048,512]{1,0:T(8,128)(2,1)}, f32[32,32]{1,0:T(8,128)}, f32[8,32]{1,0:T(8,128)S(1)}) custom-call(f32[640,128]{1,0:T(8,128)S(1)} %bitcast.24, f32[640,128]{1,0:T(8,128)S(1)} %collective-permute-done.3.other_in, bf16[2048,512]{1,0:T(8,128)(2,1)S(1)} %get-tuple-element.23.dpre, bf16[32,32]{1,0:T(8,128)(2,1)S(1)} %copy-done.16, ...), custom_call_target="tpu_custom_call" | custom-call | tf_op jit(solution)/shard_map/last/pallas_call | solution.py:474
  137.2 0.5 slice_bitcast_fusion
  (38 shorter events, 0.2 us)
Async XLA Ops:
  0.6 1.6 %copy-start = (bf16[2,32,32,512]{3,2,1,0:T(8,128)(2,1)S(1)}, bf16[2,32,32,512]{3,2,1,0:T(8,128)(2,1)}, u32[]{:S(2)}) copy-start(bf16[2,32,32,512]{3,2,1,0:T(8,128)(2,1)} %param.17) | copy-start | bytes 6291460
  2.2 1.0 copy-start.5
  3.3 0.8 copy-start.11
  4.1 34.5 %copy-start.2 = (bf16[8,1,32,1024]{3,2,1,0:T(8,128)(2,1)S(1)}, bf16[8,1,32,1024]{3,2,1,0:T(8,128)(2,1)}, u32[]{:S(2)}) copy-start(bf16[8,1,32,1024]{3,2,1,0:T(8,128)(2,1)} %param.19) | copy-start | bytes 1572868
  4.1 34.5 %copy-start.9 = (bf16[64,1024]{1,0:T(8,128)(2,1)S(1)}, bf16[64,1024]{1,0:T(8,128)(2,1)}, u32[]{:S(2)}) copy-start(bf16[64,1024]{1,0:T(8,128)(2,1)} %constant.28.clone.expand) | copy-start | bytes 393220
  4.1 34.5 %copy-start.10 = (f32[128,32]{1,0:T(8,128)S(1)}, f32[128,32]{1,0:T(8,128)}, u32[]{:S(2)}) copy-start(f32[128,32]{1,0:T(8,128)} %constant.27.clone.scatter) | copy-start | bytes 49156
  4.1 34.5 %copy-start.14 = (bf16[256,256]{1,0:T(8,128)(2,1)S(1)}, bf16[256,256]{1,0:T(8,128)(2,1)}, u32[]{:S(2)}) copy-start(bf16[256,256]{1,0:T(8,128)(2,1)} %constant.30.clone.fold4) | copy-start | bytes 393220
  4.1 34.5 %copy-start.15 = (f32[32,256]{1,0:T(8,128)S(1)}, f32[32,256]{1,0:T(8,128)}, u32[]{:S(2)}) copy-start(f32[32,256]{1,0:T(8,128)} %constant.26.clone.gather) | copy-start | bytes 98308
  7.6 54.8 %copy-start.3 = (bf16[2,32,32,512]{3,2,1,0:T(8,128)(2,1)S(1)}, bf16[2,32,32,512]{3,2,1,0:T(8,128)(2,1)}, u32[]{:S(2)}) copy-start(bf16[2,32,32,512]{3,2,1,0:T(8,128)(2,1)} %param.18) | copy-start | bytes 6291460
  7.6 54.8 %copy-start.18 = (s32[2]{0:T(128)S(1)}, s32[2]{0:T(128)}, u32[]{:S(2)}) copy-start(s32[2]{0:T(128)} %key.1) | copy-start | bytes 28
  7.6 4.5 %collective-permute-start = (f32[512,128]{1,0:T(8,128)S(1)}, f32[512,128]{1,0:T(8,128)S(1)}, u32[]{:S(2)}, u32[]{:S(2)}) collective-permute-start(f32[512,128]{1,0:T(8,128)S(1)} %get-tuple-element.17), channel_id=1, source_target_pairs={{0,1},{1,0},{2,3},{3,2},{4,5},{5,4},{6,7},{7,6},{8,9},{9,8},{10,11... | collective-permute-start | bytes 786440 | tf_op jit(solution)/shard_map/ppermute | solution.py:388
  58.7 9.8 %collective-permute-start.1 = (f32[512,128]{1,0:T(8,128)S(1)}, f32[512,128]{1,0:T(8,128)S(1)}, u32[]{:S(2)}, u32[]{:S(2)}) collective-permute-start(f32[512,128]{1,0:T(8,128)S(1)} %bitcast.25), channel_id=1, source_target_pairs={{0,1},{1,0},{2,3},{3,2},{4,5},{5,4},{6,7},{7,6},{8,9},{9,8},{10,11... | collective-permute-start | bytes 786440 | tf_op jit(solution)/shard_map/ppermute | solution.py:388
  62.4 6.1 %copy-start.19 = (f32[32]{0:T(128)S(1)}, f32[32]{0:T(128)}, u32[]{:S(2)}) copy-start(f32[32]{0:T(128)} %param.21) | copy-start | bytes 388
  62.4 6.2 %copy-start.4 = (f32[4,32,1024]{2,1,0:T(8,128)S(1)}, f32[4,32,1024]{2,1,0:T(8,128)}, u32[]{:S(2)}) copy-start(f32[4,32,1024]{2,1,0:T(8,128)} %constant.23.clone.down_modes) | copy-start | bytes 1572868
  62.4 6.2 %copy-start.6 = (f32[4,32,1024]{2,1,0:T(8,128)S(1)}, f32[4,32,1024]{2,1,0:T(8,128)}, u32[]{:S(2)}) copy-start(f32[4,32,1024]{2,1,0:T(8,128)} %constant.22.clone.down.down_cells) | copy-start | bytes 1572868
  62.4 6.2 %copy-start.7 = (bf16[192,512]{1,0:T(8,128)(2,1)S(1)}, bf16[192,512]{1,0:T(8,128)(2,1)}, u32[]{:S(2)}) copy-start(bf16[192,512]{1,0:T(8,128)(2,1)} %constant.25.clone.depth_stack) | copy-start | bytes 589828
  62.4 6.1 %copy-start.12 = (bf16[64,512]{1,0:T(8,128)(2,1)S(1)}, bf16[64,512]{1,0:T(8,128)(2,1)}, u32[]{:S(2)}) copy-start(bf16[64,512]{1,0:T(8,128)(2,1)} %constant.24.clone.depth_low) | copy-start | bytes 196612
  62.4 6.1 %copy-start.13 = (f32[256,128]{1,0:T(8,128)S(1)}, f32[256,128]{1,0:T(8,128)}, u32[]{:S(2)}) copy-start(f32[256,128]{1,0:T(8,128)} %constant.32.clone.fold8) | copy-start | bytes 393220
  62.4 6.1 %copy-start.16 = (bf16[32,32]{1,0:T(8,128)(2,1)S(1)}, bf16[32,32]{1,0:T(8,128)(2,1)}, u32[]{:S(2)}) copy-start(bf16[32,32]{1,0:T(8,128)(2,1)} %bypass.3) | copy-start | bytes 6148
  67.1 1.3 copy-start.1
  68.6 36.2 %copy-start.8 = (bf16[1024,256]{1,0:T(8,128)(2,1)S(1)}, bf16[1024,256]{1,0:T(8,128)(2,1)}, u32[]{:S(2)}) copy-start(bf16[1024,256]{1,0:T(8,128)(2,1)} %constant.31.clone.fold32) | copy-start | bytes 1572868
  68.6 36.2 %copy-start.17 = (bf16[64,128]{1,0:T(8,128)(2,1)S(1)}, bf16[64,128]{1,0:T(8,128)(2,1)}, u32[]{:S(2)}) copy-start(bf16[64,128]{1,0:T(8,128)(2,1)} %constant.29.clone.tile4) | copy-start | bytes 49156
  82.6 1.7 %collective-permute-start.2 = (f32[640,128]{1,0:T(8,128)S(1)}, f32[640,128]{1,0:T(8,128)S(1)}, u32[]{:S(2)}, u32[]{:S(2)}) collective-permute-start(f32[640,128]{1,0:T(8,128)S(1)} %get-tuple-element.20), channel_id=1, source_target_pairs={{0,1},{1,0},{2,3},{3,2},{4,5},{5,4},{6,7},{7,6},{8,9},{9,8},{10,11... | collective-permute-start | bytes 983048 | tf_op jit(solution)/shard_map/ppermute | solution.py:388
  125.6 5.9 %collective-permute-start.3 = (f32[640,128]{1,0:T(8,128)S(1)}, f32[640,128]{1,0:T(8,128)S(1)}, u32[]{:S(2)}, u32[]{:S(2)}) collective-permute-start(f32[640,128]{1,0:T(8,128)S(1)} %bitcast.23), channel_id=1, source_target_pairs={{0,1},{1,0},{2,3},{3,2},{4,5},{5,4},{6,7},{7,6},{8,9},{9,8},{10,11... | collective-permute-start | bytes 983048 | tf_op jit(solution)/shard_map/ppermute | solution.py:388

commit v2 on v1

v2 whole, which is shorter than its diff:
```python
import math

import jax
import jax.numpy as jnp
import numpy as np
from jax import lax
from jax.experimental import pallas as pl
from jax.experimental.pallas import tpu as pltpu
from jax.sharding import PartitionSpec as P

LX = 128
LY = 128
LZ = 64
LT = 8
KX = 32
KY = 32
KZ = 16
KT = 4
C = 32
LZT = 512
KZT = 64
GX = 64
GY = 4
ROWS = 256
F32 = jnp.float32
BF16 = jnp.bfloat16
HIGHEST = lax.Precision.HIGHEST

keep_level = 6554
keep_scale = 1.0 / 0.9
gelu_cubic = 0.044715
mixer_one = -1640531535
mixer_two = -2048144789
mixer_three = -1028477387
norm_scale = 1.0 / math.sqrt(LX * LY * LZT)


def hartley_table(kept, length):
    wanted = np.arange(kept)
    frequency = np.where(wanted < kept // 2, wanted, wanted + (length - kept))
    residue = frequency[:, None] * np.arange(length)[None, :] % length
    radians = residue * (2.0 * math.pi / length)
    return ((np.cos(radians) + np.sin(radians)) / math.sqrt(length)).astype(np.float32)


def depth_table():
    joined = hartley_table(KZ, LZ)[:, None, :, None] * hartley_table(KT, LT)[None, :, None, :]
    return joined.reshape(KZT, LZT)


def split_table(table):
    high = table.astype(jnp.bfloat16)
    return high, (table - high.astype(np.float32)).astype(jnp.bfloat16)


def down_by_device():
    down = hartley_table(KY, LY)
    picked = []
    for q in range(GY):
        order = [
            ((side * 2 + (q % 2 + swap) % 2) * 8 + k)
            for swap in range(2)
            for side in range(2)
            for k in range(8)
        ]
        picked.append(down[order][:, q * 32 : (q + 1) * 32])
    return np.stack(picked)


def tables():
    down = down_by_device()
    pair = lambda t: np.concatenate(split_table(t), axis=1)
    depth = depth_table()
    depth_high, depth_rest = split_table(depth)
    across = hartley_table(KX, LX)
    gather = np.concatenate([np.repeat(across[:, x::2], 2, axis=1) for x in range(2)], axis=1)
    scatter = np.concatenate([across[:, x::2] for x in range(2)], axis=1)
    ones = np.concatenate([np.ones((3, LZT)), np.zeros((13, LZT))]).astype(jnp.bfloat16)
    return dict(
        down_cells=pair(down.transpose(0, 2, 1)),
        down_modes=pair(down),
        depth=np.concatenate([depth_high, depth_high, depth_rest, ones], axis=0),
        across=np.concatenate([gather, scatter], axis=1),
    )


def halves(value):
    high = value.astype(BF16)
    return high, (value - high.astype(F32)).astype(BF16)


def mm(a, b):
    return jnp.dot(a, b, preferred_element_type=F32)


def mm_nt(a, b):
    return lax.dot_general(a, b, (((1,), (1,)), ((), ())), preferred_element_type=F32)


def mm_tn(a, b):
    return lax.dot_general(a, b, (((0,), (0,)), ((), ())), preferred_element_type=F32)


def same(shape, rows, columns):
    row_ids = lax.broadcasted_iota(jnp.int32, shape, 0)
    column_ids = lax.broadcasted_iota(jnp.int32, shape, 1)
    return rows(row_ids) == columns(column_ids)


def ones_where(shape, rows, columns, dtype=BF16):
    return jnp.where(same(shape, rows, columns), 1.0, 0.0).astype(dtype)


def channel(index):
    return index & (C - 1)


def group(index):
    return index >> 5


def build_spread(table_ref, wide_ref, high_ref, rest_ref):
    wide_ref[...] = mm(table_ref[lax.axis_index("gy")], ones_where((C, 32 * C), lambda i: i, group))
    mask = same((C, 32 * C), lambda i: i, channel)
    for row in range(32):
        high_ref[row * C : (row + 1) * C, :] = jnp.where(mask, wide_ref[row : row + 1, :], 0.0).astype(BF16)
        rest_ref[row * C : (row + 1) * C, :] = jnp.where(mask, wide_ref[32 + row : 33 + row, :], 0.0).astype(BF16)


def start_copies(pairs, sems):
    copies = [pltpu.make_async_copy(source, target, sems.at[i]) for i, (source, target) in enumerate(pairs)]
    for copy in copies:
        copy.start()
    return copies


def times_spread(value, high_ref, rest_ref):
    high, rest = halves(value)
    return mm(high, high_ref[...]) + mm(rest, high_ref[...]) + mm(high, rest_ref[...])


def send_modes(modes, own_ref, other_ref, lines):
    for swap, ref in enumerate((own_ref, other_ref)):
        for side in range(2):
            for x in range(2):
                for half in range(2):
                    at = ((swap * 2 + side) * 2 + half) * 128
                    ref[pl.ds(side * lines + x * 2 + half, KZT, stride=2 * lines), :] = modes[
                        x * KZT : (x + 1) * KZT, at : at + 128
                    ]


def received_modes(own_ref, other_ref, lines):
    rows = []
    for x in range(2):
        parts = []
        for ref in (own_ref, other_ref):
            for side in range(2):
                for half in range(2):
                    parts.append(ref[pl.ds(side * lines + x * 2 + half, KZT, stride=2 * lines), :])
        rows.append(jnp.concatenate(parts, axis=1))
    return jnp.concatenate(rows, axis=0)


def block_mixing(weight_ref):
    weight = weight_ref[...].astype(F32)
    wide = jnp.concatenate([weight] * 8, axis=1)
    full = jnp.concatenate([wide] * 8, axis=0)
    return jnp.where(same((ROWS, ROWS), group, group), full, 0.0)


def fill_inverse(own_ref, other_ref, lines, high_ref, rest_ref, stack_ref):
    cells = times_spread(received_modes(own_ref, other_ref, lines), high_ref, rest_ref)
    high, rest = halves(cells)
    for x in range(2):
        part = slice(x * KZT, (x + 1) * KZT)
        stack_ref[x, 0:KZT, :] = high[part]
        stack_ref[x, KZT : 2 * KZT, :] = rest[part]
        stack_ref[x, 2 * KZT : 3 * KZT, :] = high[part]


def block_rows(i):
    return slice(i * ROWS, (i + 1) * ROWS)


def block_pairs(source, target):
    return [(source.at[pl.ds(i * ROWS, ROWS)], target.at[pl.ds(i * ROWS, ROWS)]) for i in range(8)]


def forward_kernel(field_in, depth_in, down_in, own, other, field, depth, down, wide, high, rest, flat, sems):
    copies = start_copies(
        [(down_in, down), (depth_in.at[pl.ds(0, KZT)], depth)] + block_pairs(field_in, field), sems
    )
    copies[0].wait()
    build_spread(down, wide, high, rest)
    copies[1].wait()
    for i in range(8):
        copies[2 + i].wait()
        flat[i // 4, i % 4] = mm_nt(depth[...], field[block_rows(i), :])
    send_modes(times_spread(joined(flat), high, rest), own, other, 4)


def joined(flat):
    return jnp.concatenate(
        [jnp.concatenate([flat[x, block] for block in range(4)], axis=1) for x in range(2)], axis=0
    )


def scramble(hashed):
    hashed = jnp.bitwise_xor(hashed, lax.shift_right_logical(hashed, jnp.int32(16)))
    hashed = hashed * jnp.int32(mixer_two)
    hashed = jnp.bitwise_xor(hashed, lax.shift_right_logical(hashed, jnp.int32(13)))
    hashed = hashed * jnp.int32(mixer_three)
    return jnp.bitwise_xor(hashed, lax.shift_right_logical(hashed, jnp.int32(16)))


def prepare_kernel(key, cotangent_in, kept_out, cotangent, kept, in_sems, out_sems):
    arriving = start_copies(block_pairs(cotangent_in, cotangent), in_sems)
    leaving = [pltpu.make_async_copy(source, target, out_sems.at[i]) for i, (source, target) in enumerate(block_pairs(kept, kept_out))]
    origin = (lax.axis_index("gx") * 2 * LY + lax.axis_index("gy") * 32) * (C * LZT)
    shape = (16, LZT)
    inside = (
        lax.broadcasted_iota(jnp.int32, shape, 0) * LZT + lax.broadcasted_iota(jnp.int32, shape, 1)
    ) * jnp.int32(mixer_one)
    for i in range(8):
        first = origin + ((i // 4) * LY + (i % 4) * 8) * (C * LZT)
        arriving[i].wait()

        def body(chunk, carry):
            for part in range(4):
                at = chunk * 64 + part * 16
                start = (first + at * LZT) * jnp.int32(mixer_one) + key[0]
                hashed = scramble(inside + start)
                hashed = scramble(jnp.bitwise_xor(hashed, key[1]))
                keep = jnp.bitwise_and(hashed, jnp.int32(65535)) >= keep_level
                rows = pl.ds(pl.multiple_of(i * ROWS + at, 16), 16)
                kept[rows, :] = jnp.where(keep, cotangent[rows, :].astype(F32), 0.0).astype(BF16)
            return carry

        lax.fori_loop(0, 4, body, 0)
        leaving[i].start()
    for copy in leaving:
        copy.wait()


def gathered_modes(messages, across, lines):
    slabs = [
        jnp.concatenate([messages[pl.ds(x * 2 + half, 128, stride=lines), :] for half in range(2)], axis=1)
        for x in range(2)
    ]
    slabs = jnp.concatenate(slabs, axis=0)
    return jnp.dot(across[:, 0:256], slabs, precision=HIGHEST, preferred_element_type=F32)


def by_mode(modes):
    return jnp.concatenate([modes[:, k * C : (k + 1) * C] for k in range(8)], axis=0)


def wide_halves(value):
    return jnp.concatenate(halves(value), axis=1)


def scatter_planes(repeated, across, out, lines):
    lane = lax.broadcasted_iota(jnp.int32, (KX, ROWS), 1) >> 5
    modes = jnp.zeros((KX, ROWS), F32)
    for k in range(8):
        modes = jnp.where(lane == k, repeated[k * KX : (k + 1) * KX, :], modes)
    planes = lax.dot_general(
        across[:, 256:384], modes, (((0,), (0,)), ((), ())), precision=HIGHEST, preferred_element_type=F32
    )
    for x in range(2):
        for half in range(2):
            piece = planes[x * GX : (x + 1) * GX, half * 128 : (half + 1) * 128]
            for side in range(2):
                out[pl.ds(side * lines + x * 2 + half, GX, stride=2 * lines), :] = piece


def mix_kernel(messages, weight, across, out, modes_out):
    modes = gathered_modes(messages, across, 4)
    modes_out[...] = modes
    spread = mm(wide_halves(by_mode(modes)), ones_where((2 * C, C * C), channel, group))
    total = jnp.zeros((ROWS, 128), F32)
    for j in range(8):
        part = slice(j * 128, (j + 1) * 128)
        total = total + spread[:, part] * weight[:, part].astype(F32)
    repeated = mm(wide_halves(total), ones_where((256, 256), channel, channel))
    scatter_planes(repeated, across, out, 4)


def back_kernel(messages, modes, weight, across, out, grad_out, grad, sems):
    dmodes = wide_halves(by_mode(gathered_modes(messages, across, 5)))
    tiled = mm(dmodes, ones_where((2 * C, 128), channel, channel))
    spread = mm(wide_halves(by_mode(modes[...])), ones_where((2 * C, C * C), channel, group))
    repeated = jnp.zeros((ROWS, ROWS), F32)
    leaving = []
    for j in range(8):
        part = slice(j * 128, (j + 1) * 128)
        grad[:, part] = spread[:, part] * tiled
        copy = pltpu.make_async_copy(
            grad.at[:, pl.ds(j * 128, 128)], grad_out.at[:, pl.ds(j * 128, 128)], sems.at[j]
        )
        copy.start()
        leaving.append(copy)
        high, rest = halves(weight[:, part].astype(F32) * tiled)
        fold = ones_where((128, 256), lambda i: group(i) + 4 * j, channel)
        repeated = repeated + mm(high, fold) + mm(rest, fold)
    scatter_planes(repeated, across, out, 5)
    total = jnp.sum(messages[pl.ds(4, 128, stride=5), :], axis=0, keepdims=True)
    out[pl.ds(4, 128, stride=5), :] = jnp.broadcast_to(total, (128, 128))
    for copy in leaving:
        copy.wait()


def gelu_slope(preact):
    factor = math.sqrt(2.0 / math.pi)
    square = preact * preact
    tanh_value = jnp.tanh(preact * (factor + (factor * gelu_cubic) * square))
    rest = preact * (0.5 * factor + (1.5 * factor * gelu_cubic) * square)
    return 0.5 + 0.5 * tanh_value + rest * (1.0 - tanh_value * tanh_value)


def middle_kernel(
    own_in, other_in, bias, bypass, field_in, kept_in, depth_in, modes_in, cells_in,
    own, other, dpre_out,
    field, kept, dpre, depth, down_modes, down_cells, wide, high_in, rest_in, high, rest,
    stack, mixing, preact_even, preact_odd, flat, sums, bias_sums, in_sems, out_sems,
):
    small = [(modes_in, down_modes), (depth_in, depth), (cells_in, down_cells)]
    pairs = [pair for both in zip(block_pairs(field_in, field), block_pairs(kept_in, kept)) for pair in both]
    copies = start_copies(small + pairs, in_sems)
    leaving = [
        pltpu.make_async_copy(source, target, out_sems.at[i])
        for i, (source, target) in enumerate(block_pairs(dpre, dpre_out))
    ]
    mixing[...] = jnp.transpose(block_mixing(bypass)).astype(BF16)
    sums[...] = jnp.zeros_like(sums)
    bias_sums[...] = jnp.zeros_like(bias_sums)
    copies[0].wait()
    build_spread(down_modes, wide, high_in, rest_in)
    fill_inverse(own_in, other_in, 4, high_in, rest_in, stack)
    first = bias[...]
    bias_high, bias_left = halves(first)
    bias_rest, bias_last = halves(first - bias_high.astype(F32))
    lines = jnp.concatenate([bias_high, bias_rest, bias_last], axis=0).astype(F32)
    lines = jnp.concatenate([lines, jnp.zeros((13, C), F32)], axis=0).astype(BF16)
    wide_bias = mm(lines, ones_where((C, 32 * C), lambda i: i, channel)).astype(BF16)
    for x in range(2):
        stack[x, 3 * KZT : 3 * KZT + 16, :] = wide_bias
    copies[1].wait()
    preacts = (preact_even, preact_odd)

    def linear(i):
        copies[3 + 2 * i].wait()
        spectral = mm_tn(stack[i // 4, :, block_rows(i % 4)], depth[...])
        preacts[i % 2][...] = spectral + mm(mixing[...], field[block_rows(i), :])

    def activate(i):
        copies[4 + 2 * i].wait()
        for chunk in range(ROWS // 16):
            rows = slice(i * ROWS + chunk * 16, i * ROWS + chunk * 16 + 16)
            slope = gelu_slope(preacts[i % 2][chunk * 16 : chunk * 16 + 16, :])
            dpre[rows, :] = (kept[rows, :].astype(F32) * slope * keep_scale).astype(BF16)
        leaving[i].start()

    def reduce(i):
        part = dpre[block_rows(i), :]
        flat[i // 4, i % 4] = mm_nt(depth[0:KZT, :], part)
        sums[...] += mm_nt(field[block_rows(i), :], part)
        bias_sums[...] += mm_nt(jnp.ones((16, LZT), BF16), part)

    linear(0)
    copies[2].wait()
    build_spread(down_cells, wide, high, rest)
    for i in range(8):
        if i < 7:
            linear(i + 1)
        activate(i)
        reduce(i)

    send_modes(times_spread(joined(flat), high, rest), own, other, 5)
    lane = lax.broadcasted_iota(jnp.int32, (C, ROWS), 1) >> 5
    picked = jnp.zeros((C, ROWS), F32)
    for k in range(8):
        picked = jnp.where(lane == k, sums[k * C : (k + 1) * C, :], picked)
    both = jnp.concatenate([picked, bias_sums[...], jnp.zeros((16, ROWS), F32)], axis=0)
    fold = ones_where((ROWS, 128), channel, lambda i: i, F32)
    folded = jnp.dot(both, fold, precision=HIGHEST, preferred_element_type=F32)
    for side in range(2):
        own[pl.ds(side * 5 + 4, KZT, stride=10), :] = folded
        other[pl.ds(side * 5 + 4, KZT, stride=10), :] = jnp.zeros((KZT, 128), F32)
    for copy in leaving:
        copy.wait()


def last_kernel(
    own_in, other_in, bypass, dpre_in, depth_in, modes_in,
    grad_out, grad_weight, grad_bias,
    dpre, grad, depth, down_modes, wide, high_in, rest_in, stack, mixing, in_sems, out_sems,
):
    copies = start_copies([(modes_in, down_modes), (depth_in.at[pl.ds(0, 3 * KZT)], depth)] + block_pairs(dpre_in, dpre), in_sems)
    leaving = [
        pltpu.make_async_copy(source, target, out_sems.at[i])
        for i, (source, target) in enumerate(block_pairs(grad, grad_out))
    ]
    mixing[...] = block_mixing(bypass).astype(BF16)
    copies[0].wait()
    build_spread(down_modes, wide, high_in, rest_in)
    fill_inverse(own_in, other_in, 5, high_in, rest_in, stack)
    copies[1].wait()
    for i in range(8):
        copies[2 + i].wait()
        spectral = mm_tn(stack[i // 4, :, block_rows(i % 4)], depth[...])
        grad[block_rows(i), :] = (spectral + mm(mixing[...], dpre[block_rows(i), :])).astype(BF16)
        leaving[i].start()
    total = own_in[pl.ds(4, KZT, stride=10), :] + other_in[pl.ds(4, KZT, stride=10), :]
    total = total * norm_scale
    grad_weight[...] = total[0:C, 0:C]
    grad_bias[...] = total[C : C + 8, 0:C]
    for copy in leaving:
        copy.wait()


HELD = pl.BlockSpec(memory_space=pltpu.VMEM)
FAR = pl.BlockSpec(memory_space=pltpu.HBM)
SMEM = pl.BlockSpec(memory_space=pltpu.SMEM)
PARAMS = pltpu.CompilerParams(vmem_limit_bytes=24 * 1024 * 1024)


def like(*shape, dtype=F32):
    return jax.ShapeDtypeStruct(shape, dtype)


def call(kernel, name, ins, outs, out_shape, scratch=(), cost=None):
    return pl.pallas_call(
        kernel,
        name=name,
        in_specs=ins,
        out_specs=outs,
        out_shape=out_shape,
        scratch_shapes=list(scratch),
        compiler_params=PARAMS,
        cost_estimate=cost,
    )


def swap_cores(value):
    return lax.ppermute(value, "gy", [(i, i ^ 1) for i in range(GY)])


def exchange(messages, lines):
    groups = [[(g * 2 + side) * 2 + core for g in range(GX) for side in range(2)] for core in range(2)]
    shaped = messages.reshape(128, 1, lines * 128)
    moved = lax.all_to_all(
        shaped, ("gx", "gy"), split_axis=0, concat_axis=0, tiled=True, axis_index_groups=groups
    )
    return moved.reshape(128 * lines, 128)


def far(value):
    return pltpu.with_memory_space_constraint(value, pltpu.HBM)


def local(layer_input, cotangent, spectral_weight, bypass_weight, channel_bias, hash_key):
    table = {name: jnp.asarray(value) for name, value in tables().items()}
    across = table["across"]
    depth, down_cells, down_modes = (far(table[name]) for name in ("depth", "down_cells", "down_modes"))
    weight = spectral_weight.reshape(ROWS, C * C)
    field = far(layer_input.reshape(-1, LZT))
    field_far = pltpu.HBM((2048, LZT), BF16)
    held = lambda *shape, dtype=BF16: pltpu.VMEM(shape, dtype)
    sems = lambda count: pltpu.SemaphoreType.DMA((count,))
    field_held = held(2048, LZT)
    square = held(1024, 1024)
    flat = held(2, 4, KZT, ROWS, dtype=F32)
    stack = held(2, 3 * KZT + 16, 1024)
    last_stack = held(2, 3 * KZT, 1024)
    mixing = held(ROWS, ROWS)
    down = held(GY, 64, 32)
    wide = held(64, 1024, dtype=F32)
    depth_held = held(3 * KZT + 16, LZT)

    own, other = call(
        forward_kernel,
        "forward",
        [FAR] * 3,
        [HELD] * 2,
        [like(512, 128)] * 2,
        [field_held, held(KZT, LZT), down, wide, square, square, flat, sems(10)],
    )(field, depth, down_cells)
    messages = exchange(own + swap_cores(other), 4)

    kept = call(
        prepare_kernel,
        "prepare",
        [SMEM, FAR],
        FAR,
        field_far,
        [field_held, field_held, sems(8), sems(8)],
        pl.CostEstimate(flops=10**10, bytes_accessed=2 * 10**7, transcendentals=0),
    )(hash_key, far(cotangent.reshape(-1, LZT)))
    messages, kept = lax.optimization_barrier((messages, kept))

    planes, modes = call(mix_kernel, "mix", [HELD] * 3, [HELD] * 2, [like(512, 128), like(KX, ROWS)])(
        messages, weight, across
    )
    own_cells = exchange(planes, 4)
    other_cells = swap_cores(own_cells)

    preact = held(ROWS, LZT, dtype=F32)
    own, other, dpre = call(
        middle_kernel,
        "middle",
        [HELD] * 4 + [FAR] * 5,
        [HELD, HELD, FAR],
        [like(640, 128), like(640, 128), field_far],
        [
            field_held, field_held, field_held, depth_held, down, down, wide, square, square, square, square,
            stack, mixing, preact, preact, flat, held(ROWS, ROWS, dtype=F32), held(16, ROWS, dtype=F32),
            sems(19), sems(8),
        ],
    )(
        own_cells, other_cells, channel_bias.reshape(1, C), bypass_weight, field, far(kept), depth,
        down_modes, down_cells,
    )
    messages = exchange(own + swap_cores(other), 5)

    planes, grad_spectral = call(
        back_kernel,
        "back",
        [HELD] * 4,
        [HELD, FAR],
        [like(640, 128), pltpu.HBM((ROWS, 1024), F32)],
        [held(ROWS, 1024, dtype=F32), sems(8)],
    )(messages, modes, weight, across)
    own_cells = exchange(planes, 5)
    other_cells = swap_cores(own_cells)

    grad_input, grad_weight, grad_bias = call(
        last_kernel,
        "last",
        [HELD] * 3 + [FAR] * 3,
        [FAR, HELD, HELD],
        [field_far, like(C, C), like(8, C)],
        [
            field_held, field_held, held(3 * KZT, LZT), down, wide, square, square, last_stack, mixing,
            sems(10), sems(8),
        ],
    )(own_cells, other_cells, bypass_weight, far(dpre), depth, down_modes)
    return (
        grad_input.reshape(layer_input.shape),
        grad_spectral.reshape(spectral_weight.shape),
        grad_weight,
        grad_bias[0],
    )


def solution(mesh):
    return jax.shard_map(
        local,
        mesh=mesh,
        in_specs=(
            P("gx", "gy", None, None),
            P("gx", "gy", None, None),
            P("gy", "gx", None, None),
            P(),
            P(),
            P(),
        ),
        out_specs=(P("gx", "gy", None, None), P("gy", "gx", None, None), P(), P()),
        check_vma=False,
    )
```

time: 138 us -> 127 us (0.920)
  blocking collectives: 84.4 us -> 57.7 us
  starting transfers between devices: 11.7 us -> 25.8 us
  waiting for transfers between devices: 4.03 us -> 12 us
  local copies, waits for them, and re-layouts: 5.45 us -> 0.54 us
  Pallas kernels: 31.2 us -> 29.2 us
    all_to_all x4 -> x3, blocking collectives: 84.4 us -> 57.7 us  [exchange(): lax.all_to_all(shaped, ('gx', 'gy'), split_axis=0, concat_axis=0, tiled=T...]
    all_to_all x0 -> x1, starting transfers between devices: none -> 13.8 us  [exchange(): lax.all_to_all(shaped, ('gx', 'gy'), split_axis=0, concat_axis=0, tiled=T...]
    all_to_all x0 -> x1, waiting for transfers between devices: none -> 7.14 us  [exchange(): lax.all_to_all(shaped, ('gx', 'gy'), split_axis=0, concat_axis=0, tiled=T...]
    unnamed x40 -> x10, local copies, waits for them, and re-layouts: 4.87 us -> 0.03 us
    pallas_call x6, Pallas kernels: 31.2 us -> 29.2 us  [the longest x1 10 us: local(): call(middle_kernel, 'middle', [HELD] * 4 + [FAR] * 5, [HELD, HELD, FAR],...]
  transfers between devices with their start and end apart: 4 -> 5, of which waited for: 3 -> 5; matrix products, arithmetic and copies ran while one was open for 0% -> 0% of each run, Pallas kernels for 3% -> 5%
where the time goes in v2:
time: 127 us
  blocking collectives  57.7 us (45%)
  Pallas kernels  29.2 us (23%)
  starting transfers between devices  25.8 us (20%)
  waiting for transfers between devices  12 us (9%)
    all_to_all x3, blocking collectives, exchange(): lax.all_to_all(shaped, ('gx', 'gy'), split_axis=0, concat_axis=0, tiled=T...  57.7 us
    all_to_all x1, starting transfers between devices, exchange(): lax.all_to_all(shaped, ('gx', 'gy'), split_axis=0, concat_axis=0, tiled=T...  13.8 us
    ppermute x4, starting transfers between devices, swap_cores(): return lax.ppermute(value, 'gy', [(i, i ^ 1) for i in range(GY)])  12.1 us
    pallas_call x1, Pallas kernels, local(): call(middle_kernel, 'middle', [HELD] * 4 + [FAR] * 5, [HELD, HELD, FAR],...  10 us
    all_to_all x1, waiting for transfers between devices, exchange(): lax.all_to_all(shaped, ('gx', 'gy'), split_axis=0, concat_axis=0, tiled=T...  7.14 us
    pallas_call x1, Pallas kernels, local(): call(last_kernel, 'last', [HELD] * 3 + [FAR] * 3, [FAR, HELD, HELD], [fie...  5.91 us
    pallas_call x1, Pallas kernels, local(): call(prepare_kernel, 'prepare', [SMEM, FAR], FAR, field_far, [field_held,...  5.73 us
    ppermute x4, waiting for transfers between devices, swap_cores(): return lax.ppermute(value, 'gy', [(i, i ^ 1) for i in range(GY)])  4.84 us
  transfers between devices with their start and end apart: 5, of which 5 were waited for; matrix products, arithmetic and copies ran while one was open for 0% of the time, Pallas kernels for 5%

profile of v2, /device:TPU:1, one launch (start us, length us, event | category | flops | bytes accessed | tf_op | source)
XLA Modules:
  0.0 126.8 jit_solution(14144156666711014023)
XLA Ops:
  0.6 4.1 %forward.1 = (f32[512,128]{1,0:T(8,128)S(1)}, f32[512,128]{1,0:T(8,128)S(1)}) custom-call(bf16[2048,512]{1,0:T(8,128)(2,1)} %bitcast.29, bf16[208,512]{1,0:T(8,128)(2,1)} %constant.10.clone.depth_in, bf16[4,64,32]{2,1,0:T(8,128)(2,1)} %constant.8.clone.down_in.cells_in), custom_call_target="tpu_custom_call" | custom-call | tf_op jit(solution)/shard_map/forward/pallas_call | solution.py:482
  4.8 3.3 %collective-permute-start = (f32[512,128]{1,0:T(8,128)S(1)}, f32[512,128]{1,0:T(8,128)S(1)}, u32[]{:S(2)}, u32[]{:S(2)}) collective-permute-start(f32[512,128]{1,0:T(8,128)S(1)} %get-tuple-element.19), channel_id=1, source_target_pairs={{0,1},{1,0},{2,3},{3,2},{4,5},{5,4},{6,7},{7,6},{8,9},{9,8},{10,11... | collective-permute-start | bytes 786440 | tf_op jit(solution)/shard_map/ppermute | solution.py:447
  8.1 1.2 collective-permute-done
  9.3 0.7 add.6
  10.0 13.8 %all-to-all-start = ((f32[128,1,512]{2,1,0:T(1,128)}), f32[128,1,512]{2,1,0:T(1,128)S(1)}, u32[]{:S(2)}, u32[]{:S(2)}) async-start(f32[128,1,512]{2,1,0:T(1,128)} %bitcast.1), calls=%async_computation | async-start | bytes 524288 | tf_op jit(solution)/shard_map/all_to_all | solution.py:453
  23.8 0.0 copy-start
  23.8 0.0 copy-start.1
  23.8 0.0 copy-start.2
  23.8 5.7 %prepare.1.kept_in = bf16[2048,512]{1,0:T(8,128)(2,1)} custom-call(s32[2]{0:T(128)S(1)} %copy-done.4, bf16[2048,512]{1,0:T(8,128)(2,1)} %bitcast.32), custom_call_target="tpu_custom_call" | custom-call | flops 10000000000 | bytes 20000000 | tf_op jit(solution)/shard_map/prepare/pallas_call | solution.py:492
  29.6 7.1 %all-to-all-done = f32[128,1,512]{2,1,0:T(1,128)S(1)} async-done(((f32[128,1,512]{2,1,0:T(1,128)}), f32[128,1,512]{2,1,0:T(1,128)S(1)}, u32[]{:S(2)}, u32[]{:S(2)}) %all-to-all-start) | async-done | bytes 262176 | tf_op jit(solution)/shard_map/all_to_all | solution.py:453
  36.7 1.3 %mix.1 = (f32[512,128]{1,0:T(8,128)S(1)}, f32[32,256]{1,0:T(8,128)S(1)}) custom-call(f32[512,128]{1,0:T(8,128)S(1)} %bitcast.23, bf16[256,1024]{1,0:T(8,128)(2,1)S(1)} %bitcast.18, f32[32,384]{1,0:T(8,128)S(1)} %copy-done.1), custom_call_target="tpu_custom_call" | custom-call | tf_op jit(solution)/shard_map/mix/pallas_call | solution.py:503
  38.1 18.7 %all_to_all.20 = f32[128,1,512]{2,1,0:T(1,128)S(1)} all-to-all(f32[128,1,512]{2,1,0:T(1,128)S(1)} %bitcast.27), channel_id=1, replica_groups={{0,2,4,6,8,10,12,14,16,18,20,22,24,26,28,30,32,34,36,38,40,42,44,46,48,..., dimensions={0} | all-to-all | bytes 524288 | tf_op jit(solution)/shard_map/all_to_all | solution.py:453
  56.7 3.7 %collective-permute-start.1 = (f32[512,128]{1,0:T(8,128)S(1)}, f32[512,128]{1,0:T(8,128)S(1)}, u32[]{:S(2)}, u32[]{:S(2)}) collective-permute-start(f32[512,128]{1,0:T(8,128)S(1)} %bitcast.24), channel_id=1, source_target_pairs={{0,1},{1,0},{2,3},{3,2},{4,5},{5,4},{6,7},{7,6},{8,9},{9,8},{10,11... | collective-permute-start | bytes 786440 | tf_op jit(solution)/shard_map/ppermute | solution.py:447
  60.4 1.2 collective-permute-done.1.other_in
  61.6 10.0 %middle.1 = (f32[640,128]{1,0:T(8,128)S(1)}, f32[640,128]{1,0:T(8,128)S(1)}, bf16[2048,512]{1,0:T(8,128)(2,1)}) custom-call(f32[512,128]{1,0:T(8,128)S(1)} %bitcast.25, f32[512,128]{1,0:T(8,128)S(1)} %collective-permute-done.1.other_in, f32[1,32]{1,0:T(1,128)S(1)} %bitcast.28, bf16[32,32]{1,0:T(8,128)(2,1)S(1)} %copy-done.2, bf16[2048,512]{1,0:T(8,128)(2,1)} %bitcast.30, ...), custom_call_target="tpu_custom_call" | custom-call | tf_op jit(solution)/shard_map/middle/pallas_call | solution.py:510
  71.6 0.5 collective-permute-start.2
  72.1 1.3 collective-permute-done.2
  73.4 19.9 %all_to_all.21 = f32[128,1,640]{2,1,0:T(1,128)S(1)} all-to-all(f32[128,1,640]{2,1,0:T(1,128)S(1)} %bitcast.31), channel_id=1, replica_groups={{0,2,4,6,8,10,12,14,16,18,20,22,24,26,28,30,32,34,36,38,40,42,44,46,48,..., dimensions={0} | all-to-all | bytes 655360 | tf_op jit(solution)/shard_map/all_to_all | solution.py:453
  93.3 2.1 %back.1 = (f32[640,128]{1,0:T(8,128)S(1)}, f32[256,1024]{1,0:T(8,128)}) custom-call(f32[640,128]{1,0:T(8,128)S(1)} %bitcast.22, f32[32,256]{1,0:T(8,128)S(1)} %get-tuple-element.25.modes, bf16[256,1024]{1,0:T(8,128)(2,1)S(1)} %bitcast.19, f32[32,384]{1,0:T(8,128)S(1)} %copy-done.1), custom_call_target="tpu_custom_call" | custom-call | tf_op jit(solution)/shard_map/back/pallas_call | solution.py:527
  95.4 19.1 %all_to_all.22 = f32[128,1,640]{2,1,0:T(1,128)S(1)} all-to-all(f32[128,1,640]{2,1,0:T(1,128)S(1)} %bitcast.26), channel_id=1, replica_groups={{0,2,4,6,8,10,12,14,16,18,20,22,24,26,28,30,32,34,36,38,40,42,44,46,48,..., dimensions={0} | all-to-all | bytes 655360 | tf_op jit(solution)/shard_map/all_to_all | solution.py:453
  114.5 4.6 %collective-permute-start.3 = (f32[640,128]{1,0:T(8,128)S(1)}, f32[640,128]{1,0:T(8,128)S(1)}, u32[]{:S(2)}, u32[]{:S(2)}) collective-permute-start(f32[640,128]{1,0:T(8,128)S(1)} %bitcast.20), channel_id=1, source_target_pairs={{0,1},{1,0},{2,3},{3,2},{4,5},{5,4},{6,7},{7,6},{8,9},{9,8},{10,11... | collective-permute-start | bytes 983048 | tf_op jit(solution)/shard_map/ppermute | solution.py:447
  119.1 1.3 collective-permute-done.3.other_in
  120.4 5.9 %last.1 = (bf16[2048,512]{1,0:T(8,128)(2,1)}, f32[32,32]{1,0:T(8,128)}, f32[8,32]{1,0:T(8,128)S(1)}) custom-call(f32[640,128]{1,0:T(8,128)S(1)} %bitcast.21, f32[640,128]{1,0:T(8,128)S(1)} %collective-permute-done.3.other_in, bf16[32,32]{1,0:T(8,128)(2,1)S(1)} %copy-done.2, bf16[2048,512]{1,0:T(8,128)(2,1)} %get-tuple-element.27.dpre_in, ...), custom_call_target="tpu_custom_call" | custom-call | tf_op jit(solution)/shard_map/last/pallas_call | solution.py:538
  126.3 0.5 slice_bitcast_fusion
  (8 shorter events, 0.1 us)
Async XLA Ops:
  0.6 23.2 %copy-start.4 = (s32[2]{0:T(128)S(1)}, s32[2]{0:T(128)}, u32[]{:S(2)}) copy-start(s32[2]{0:T(128)} %key.1) | copy-start | bytes 28
  4.8 4.5 %collective-permute-start = (f32[512,128]{1,0:T(8,128)S(1)}, f32[512,128]{1,0:T(8,128)S(1)}, u32[]{:S(2)}, u32[]{:S(2)}) collective-permute-start(f32[512,128]{1,0:T(8,128)S(1)} %get-tuple-element.19), channel_id=1, source_target_pairs={{0,1},{1,0},{2,3},{3,2},{4,5},{5,4},{6,7},{7,6},{8,9},{9,8},{10,11... | collective-permute-start | bytes 786440 | tf_op jit(solution)/shard_map/ppermute | solution.py:447
  10.0 26.7 %all-to-all-start = ((f32[128,1,512]{2,1,0:T(1,128)}), f32[128,1,512]{2,1,0:T(1,128)S(1)}, u32[]{:S(2)}, u32[]{:S(2)}) async-start(f32[128,1,512]{2,1,0:T(1,128)} %bitcast.1), calls=%async_computation | async-start | bytes 524288 | tf_op jit(solution)/shard_map/all_to_all | solution.py:453
  23.8 12.9 %copy-start = (bf16[8,1,32,1024]{3,2,1,0:T(8,128)(2,1)S(1)}, bf16[8,1,32,1024]{3,2,1,0:T(8,128)(2,1)}, u32[]{:S(2)}) copy-start(bf16[8,1,32,1024]{3,2,1,0:T(8,128)(2,1)} %param.12) | copy-start | bytes 1572868
  23.8 12.9 %copy-start.1 = (f32[32,384]{1,0:T(8,128)S(1)}, f32[32,384]{1,0:T(8,128)}, u32[]{:S(2)}) copy-start(f32[32,384]{1,0:T(8,128)} %constant.11.clone.across) | copy-start | bytes 147460
  23.8 37.8 %copy-start.2 = (bf16[32,32]{1,0:T(8,128)(2,1)S(1)}, bf16[32,32]{1,0:T(8,128)(2,1)}, u32[]{:S(2)}) copy-start(bf16[32,32]{1,0:T(8,128)(2,1)} %bypass.3) | copy-start | bytes 6148
  23.8 37.8 %copy-start.3 = (f32[32]{0:T(128)S(1)}, f32[32]{0:T(128)}, u32[]{:S(2)}) copy-start(f32[32]{0:T(128)} %param.14) | copy-start | bytes 388
  56.7 4.8 %collective-permute-start.1 = (f32[512,128]{1,0:T(8,128)S(1)}, f32[512,128]{1,0:T(8,128)S(1)}, u32[]{:S(2)}, u32[]{:S(2)}) collective-permute-start(f32[512,128]{1,0:T(8,128)S(1)} %bitcast.24), channel_id=1, source_target_pairs={{0,1},{1,0},{2,3},{3,2},{4,5},{5,4},{6,7},{7,6},{8,9},{9,8},{10,11... | collective-permute-start | bytes 786440 | tf_op jit(solution)/shard_map/ppermute | solution.py:447
  71.6 1.7 %collective-permute-start.2 = (f32[640,128]{1,0:T(8,128)S(1)}, f32[640,128]{1,0:T(8,128)S(1)}, u32[]{:S(2)}, u32[]{:S(2)}) collective-permute-start(f32[640,128]{1,0:T(8,128)S(1)} %get-tuple-element.24), channel_id=1, source_target_pairs={{0,1},{1,0},{2,3},{3,2},{4,5},{5,4},{6,7},{7,6},{8,9},{9,8},{10,11... | collective-permute-start | bytes 983048 | tf_op jit(solution)/shard_map/ppermute | solution.py:447
  114.5 5.9 %collective-permute-start.3 = (f32[640,128]{1,0:T(8,128)S(1)}, f32[640,128]{1,0:T(8,128)S(1)}, u32[]{:S(2)}, u32[]{:S(2)}) collective-permute-start(f32[640,128]{1,0:T(8,128)S(1)} %bitcast.20), channel_id=1, source_target_pairs={{0,1},{1,0},{2,3},{3,2},{4,5},{5,4},{6,7},{7,6},{8,9},{9,8},{10,11... | collective-permute-start | bytes 983048 | tf_op jit(solution)/shard_map/ppermute | solution.py:447

commit v3 on v2

--- a/solution.py
+++ b/solution.py
@@ -69,7 +69,7 @@
 
 def tables():
     down = down_by_device()
-    pair = lambda t: np.concatenate(split_table(t), axis=1)
+    low = lambda t: t.astype(jnp.bfloat16)
     depth = depth_table()
     depth_high, depth_rest = split_table(depth)
     across = hartley_table(KX, LX)
@@ -77,8 +77,8 @@
     scatter = np.concatenate([across[:, x::2] for x in range(2)], axis=1)
     ones = np.concatenate([np.ones((3, LZT)), np.zeros((13, LZT))]).astype(jnp.bfloat16)
     return dict(
-        down_cells=pair(down.transpose(0, 2, 1)),
-        down_modes=pair(down),
+        down_cells=low(down.transpose(0, 2, 1)),
+        down_modes=low(down),
         depth=np.concatenate([depth_high, depth_high, depth_rest, ones], axis=0),
         across=np.concatenate([gather, scatter], axis=1),
     )
@@ -119,12 +119,20 @@
     return index >> 5
 
 
-def build_spread(table_ref, wide_ref, high_ref, rest_ref):
-    wide_ref[...] = mm(table_ref[lax.axis_index("gy")], ones_where((C, 32 * C), lambda i: i, group))
-    mask = same((C, 32 * C), lambda i: i, channel)
-    for row in range(32):
-        high_ref[row * C : (row + 1) * C, :] = jnp.where(mask, wide_ref[row : row + 1, :], 0.0).astype(BF16)
-        rest_ref[row * C : (row + 1) * C, :] = jnp.where(mask, wide_ref[32 + row : 33 + row, :], 0.0).astype(BF16)
+def widen(table_ref):
+    return mm(table_ref[lax.axis_index("gy")], ones_where((C, 32 * C), lambda i: i, group))
+
+
+def fill_spread(wide_ref, columns, target_ref, first=0, count=32):
+    mask = same((C, columns.stop - columns.start), lambda i: i, channel)
+    for row in range(count):
+        line = wide_ref[first + row : first + row + 1, columns]
+        target_ref[row * C : (row + 1) * C, :] = jnp.where(mask, line, 0.0).astype(BF16)
+
+
+OWN = slice(0, 512)
+OTHER = slice(512, 1024)
+ALL = slice(0, 1024)
 
 
 def start_copies(pairs, sems):
@@ -134,30 +142,24 @@
     return copies
 
 
-def times_spread(value, high_ref, rest_ref):
-    high, rest = halves(value)
-    return mm(high, high_ref[...]) + mm(rest, high_ref[...]) + mm(high, rest_ref[...])
-
-
-def send_modes(modes, own_ref, other_ref, lines):
-    for swap, ref in enumerate((own_ref, other_ref)):
-        for side in range(2):
-            for x in range(2):
-                for half in range(2):
-                    at = ((swap * 2 + side) * 2 + half) * 128
-                    ref[pl.ds(side * lines + x * 2 + half, KZT, stride=2 * lines), :] = modes[
-                        x * KZT : (x + 1) * KZT, at : at + 128
-                    ]
-
-
-def received_modes(own_ref, other_ref, lines):
+def send_modes(modes, ref, lines):
+    for side in range(2):
+        for x in range(2):
+            for half in range(2):
+                at = (side * 2 + half) * 128
+                ref[pl.ds(side * lines + x * 2 + half, KZT, stride=2 * lines), :] = modes[
+                    x * KZT : (x + 1) * KZT, at : at + 128
+                ]
+
+
+def received_modes(ref, lines):
     rows = []
     for x in range(2):
-        parts = []
-        for ref in (own_ref, other_ref):
-            for side in range(2):
-                for half in range(2):
-                    parts.append(ref[pl.ds(side * lines + x * 2 + half, KZT, stride=2 * lines), :])
+        parts = [
+            ref[pl.ds(side * lines + x * 2 + half, KZT, stride=2 * lines), :]
+            for side in range(2)
+            for half in range(2)
+        ]
         rows.append(jnp.concatenate(parts, axis=1))
     return jnp.concatenate(rows, axis=0)
 
@@ -169,8 +171,7 @@
     return jnp.where(same((ROWS, ROWS), group, group), full, 0.0)
 
 
-def fill_inverse(own_ref, other_ref, lines, high_ref, rest_ref, stack_ref):
-    cells = times_spread(received_modes(own_ref, other_ref, lines), high_ref, rest_ref)
+def fill_stack(cells, stack_ref):
     high, rest = halves(cells)
     for x in range(2):
         part = slice(x * KZT, (x + 1) * KZT)
@@ -187,17 +188,26 @@
     return [(source.at[pl.ds(i * ROWS, ROWS)], target.at[pl.ds(i * ROWS, ROWS)]) for i in range(8)]
 
 
-def forward_kernel(field_in, depth_in, down_in, own, other, field, depth, down, wide, high, rest, flat, sems):
+def forward_kernel(field_in, depth_in, down_in, other, cells, wide, field, depth, down, spread, flat, sems):
     copies = start_copies(
         [(down_in, down), (depth_in.at[pl.ds(0, KZT)], depth)] + block_pairs(field_in, field), sems
     )
     copies[0].wait()
-    build_spread(down, wide, high, rest)
+    wide[...] = widen(down)
+    fill_spread(wide, OTHER, spread)
     copies[1].wait()
-    for i in range(8):
-        copies[2 + i].wait()
-        flat[i // 4, i % 4] = mm_nt(depth[...], field[block_rows(i), :])
-    send_modes(times_spread(joined(flat), high, rest), own, other, 4)
+    for first in (0, 4):
+        for i in range(first, first + 4):
+            copies[2 + i].wait()
+        for i in range(first, first + 4):
+            flat[i // 4, i % 4] = mm_nt(depth[...], field[block_rows(i), :])
+    cells[...] = joined(flat).astype(BF16)
+    send_modes(mm(cells[...], spread[...]), other, 4)
+
+
+def forward_own_kernel(cells, wide, own, spread):
+    fill_spread(wide, OWN, spread)
+    send_modes(mm(cells[...], spread[...]), own, 4)
 
 
 def joined(flat):
@@ -287,28 +297,18 @@
     scatter_planes(repeated, across, out, 4)
 
 
-def back_kernel(messages, modes, weight, across, out, grad_out, grad, sems):
-    dmodes = wide_halves(by_mode(gathered_modes(messages, across, 5)))
-    tiled = mm(dmodes, ones_where((2 * C, 128), channel, channel))
-    spread = mm(wide_halves(by_mode(modes[...])), ones_where((2 * C, C * C), channel, group))
+def back_kernel(messages, weight, across, out, dmodes_out):
+    dmodes = gathered_modes(messages, across, 5)
+    dmodes_out[...] = dmodes
+    tiled = mm(wide_halves(by_mode(dmodes)), ones_where((2 * C, 128), channel, channel))
     repeated = jnp.zeros((ROWS, ROWS), F32)
-    leaving = []
     for j in range(8):
-        part = slice(j * 128, (j + 1) * 128)
-        grad[:, part] = spread[:, part] * tiled
-        copy = pltpu.make_async_copy(
-            grad.at[:, pl.ds(j * 128, 128)], grad_out.at[:, pl.ds(j * 128, 128)], sems.at[j]
-        )
-        copy.start()
-        leaving.append(copy)
-        high, rest = halves(weight[:, part].astype(F32) * tiled)
+        high, rest = halves(weight[:, j * 128 : (j + 1) * 128].astype(F32) * tiled)
         fold = ones_where((128, 256), lambda i: group(i) + 4 * j, channel)
         repeated = repeated + mm(high, fold) + mm(rest, fold)
     scatter_planes(repeated, across, out, 5)
     total = jnp.sum(messages[pl.ds(4, 128, stride=5), :], axis=0, keepdims=True)
     out[pl.ds(4, 128, stride=5), :] = jnp.broadcast_to(total, (128, 128))
-    for copy in leaving:
-        copy.wait()
 
 
 def gelu_slope(preact):
@@ -319,65 +319,99 @@
     return 0.5 + 0.5 * tanh_value + rest * (1.0 - tanh_value * tanh_value)
 
 
+def invert_own(own_in, lines, down_modes, part, spread_other, wide, spread):
+    wide[...] = widen(down_modes)
+    fill_spread(wide, ALL, spread, 0, 16)
+    part[...] = mm(received_modes(own_in, lines).astype(BF16), spread[...])
+    fill_spread(wide, ALL, spread_other, 16, 16)
+
+
+def middle_own_kernel(
+    own_in, field_in, kept_in, depth_in, modes_in, cells_in,
+    part, spread_other, spread_cells, field, kept, depth,
+    down_modes, down_cells, wide, wide_cells, spread, sems,
+):
+    copies = start_copies(
+        [(modes_in, down_modes), (cells_in, down_cells), (depth_in, depth)]
+        + block_pairs(field_in, field)
+        + block_pairs(kept_in, kept),
+        sems,
+    )
+    copies[0].wait()
+    copies[1].wait()
+    invert_own(own_in, 4, down_modes, part, spread_other, wide, spread)
+    wide_cells[...] = widen(down_cells)
+    fill_spread(wide_cells, ALL, spread_cells)
+    for copy in copies[2:]:
+        copy.wait()
+
+
 def middle_kernel(
-    own_in, other_in, bias, bypass, field_in, kept_in, depth_in, modes_in, cells_in,
-    own, other, dpre_out,
-    field, kept, dpre, depth, down_modes, down_cells, wide, high_in, rest_in, high, rest,
-    stack, mixing, preact_even, preact_odd, flat, sums, bias_sums, in_sems, out_sems,
+    other_in, part, spread_other, spread_cells, field, kept, depth, bias, bypass,
+    other, cells, sums, bias_sums, dpre_out,
+    dpre_even, dpre_odd, stack, mixing, preact_even, preact_odd, flat, sems,
 ):
-    small = [(modes_in, down_modes), (depth_in, depth), (cells_in, down_cells)]
-    pairs = [pair for both in zip(block_pairs(field_in, field), block_pairs(kept_in, kept)) for pair in both]
-    copies = start_copies(small + pairs, in_sems)
-    leaving = [
-        pltpu.make_async_copy(source, target, out_sems.at[i])
-        for i, (source, target) in enumerate(block_pairs(dpre, dpre_out))
-    ]
     mixing[...] = jnp.transpose(block_mixing(bypass)).astype(BF16)
     sums[...] = jnp.zeros_like(sums)
     bias_sums[...] = jnp.zeros_like(bias_sums)
-    copies[0].wait()
-    build_spread(down_modes, wide, high_in, rest_in)
-    fill_inverse(own_in, other_in, 4, high_in, rest_in, stack)
+    inverted = part[...] + mm(received_modes(other_in, 4).astype(BF16), spread_other[...])
+    fill_stack(inverted, stack)
     first = bias[...]
-    bias_high, bias_left = halves(first)
+    bias_high = first.astype(BF16)
     bias_rest, bias_last = halves(first - bias_high.astype(F32))
     lines = jnp.concatenate([bias_high, bias_rest, bias_last], axis=0).astype(F32)
     lines = jnp.concatenate([lines, jnp.zeros((13, C), F32)], axis=0).astype(BF16)
     wide_bias = mm(lines, ones_where((C, 32 * C), lambda i: i, channel)).astype(BF16)
     for x in range(2):
         stack[x, 3 * KZT : 3 * KZT + 16, :] = wide_bias
-    copies[1].wait()
     preacts = (preact_even, preact_odd)
+    dpres = (dpre_even, dpre_odd)
+
+    def leaving(i):
+        rows = pl.ds((i // 2) * ROWS, ROWS)
+        return pltpu.make_async_copy(dpres[i % 2].at[rows], dpre_out.at[pl.ds(i * ROWS, ROWS)], sems.at[i])
+
+    def held_rows(i):
+        return slice((i // 2) * ROWS, (i // 2 + 1) * ROWS)
 
     def linear(i):
-        copies[3 + 2 * i].wait()
         spectral = mm_tn(stack[i // 4, :, block_rows(i % 4)], depth[...])
         preacts[i % 2][...] = spectral + mm(mixing[...], field[block_rows(i), :])
 
     def activate(i):
-        copies[4 + 2 * i].wait()
         for chunk in range(ROWS // 16):
             rows = slice(i * ROWS + chunk * 16, i * ROWS + chunk * 16 + 16)
+            at = (i // 2) * ROWS + chunk * 16
             slope = gelu_slope(preacts[i % 2][chunk * 16 : chunk * 16 + 16, :])
-            dpre[rows, :] = (kept[rows, :].astype(F32) * slope * keep_scale).astype(BF16)
-        leaving[i].start()
+            dpres[i % 2][at : at + 16, :] = (kept[rows, :].astype(F32) * slope * keep_scale).astype(BF16)
 
     def reduce(i):
-        part = dpre[block_rows(i), :]
-        flat[i // 4, i % 4] = mm_nt(depth[0:KZT, :], part)
-        sums[...] += mm_nt(field[block_rows(i), :], part)
-        bias_sums[...] += mm_nt(jnp.ones((16, LZT), BF16), part)
+        block = dpres[i % 2][held_rows(i), :]
+        flat[i // 4, i % 4] = mm_nt(depth[0:KZT, :], block)
+        sums[...] += mm_nt(field[block_rows(i), :], block)
+        bias_sums[...] += mm_nt(jnp.ones((16, LZT), BF16), block)
 
     linear(0)
-    copies[2].wait()
-    build_spread(down_cells, wide, high, rest)
-    for i in range(8):
+    for i in range(9):
+        if i > 0:
+            leaving(i - 1).start()
         if i < 7:
             linear(i + 1)
-        activate(i)
-        reduce(i)
-
-    send_modes(times_spread(joined(flat), high, rest), own, other, 5)
+        if i > 0:
+            reduce(i - 1)
+        if i < 8:
+            activate(i)
+
+    cells[...] = joined(flat).astype(BF16)
+    send_modes(mm(cells[...], spread_cells[:, OTHER]), other, 5)
+    for side in range(2):
+        other[pl.ds(side * 5 + 4, KZT, stride=10), :] = jnp.zeros((KZT, 128), F32)
+    for i in range(8):
+        leaving(i).wait()
+
+
+def middle_send_kernel(cells, spread_cells, sums, bias_sums, own):
+    send_modes(mm(cells[...], spread_cells[:, OWN]), own, 5)
     lane = lax.broadcasted_iota(jnp.int32, (C, ROWS), 1) >> 5
     picked = jnp.zeros((C, ROWS), F32)
     for k in range(8):
@@ -387,36 +421,52 @@
     folded = jnp.dot(both, fold, precision=HIGHEST, preferred_element_type=F32)
     for side in range(2):
         own[pl.ds(side * 5 + 4, KZT, stride=10), :] = folded
-        other[pl.ds(side * 5 + 4, KZT, stride=10), :] = jnp.zeros((KZT, 128), F32)
-    for copy in leaving:
+
+
+def last_own_kernel(
+    own_in, modes, dmodes, dpre_in, depth_in, modes_in,
+    part, spread_other, dpre, depth, grad_out,
+    down_modes, wide, spread, grad, sems, out_sems,
+):
+    copies = start_copies(
+        [(modes_in, down_modes), (depth_in.at[pl.ds(0, 3 * KZT)], depth)] + block_pairs(dpre_in, dpre), sems
+    )
+    tiled = mm(wide_halves(by_mode(dmodes[...])), ones_where((2 * C, 128), channel, channel))
+    expanded = mm(wide_halves(by_mode(modes[...])), ones_where((2 * C, C * C), channel, group))
+    for j in range(8):
+        grad[:, j * 128 : (j + 1) * 128] = expanded[:, j * 128 : (j + 1) * 128] * tiled
+    leaving = pltpu.make_async_copy(grad, grad_out, out_sems.at[0])
+    leaving.start()
+    copies[0].wait()
+    invert_own(own_in, 5, down_modes, part, spread_other, wide, spread)
+    for copy in copies[1:]:
         copy.wait()
+    leaving.wait()
 
 
 def last_kernel(
-    own_in, other_in, bypass, dpre_in, depth_in, modes_in,
+    own_in, other_in, part, spread_other, dpre, depth, bypass,
     grad_out, grad_weight, grad_bias,
-    dpre, grad, depth, down_modes, wide, high_in, rest_in, stack, mixing, in_sems, out_sems,
+    grad, stack, mixing, sems,
 ):
-    copies = start_copies([(modes_in, down_modes), (depth_in.at[pl.ds(0, 3 * KZT)], depth)] + block_pairs(dpre_in, dpre), in_sems)
-    leaving = [
-        pltpu.make_async_copy(source, target, out_sems.at[i])
-        for i, (source, target) in enumerate(block_pairs(grad, grad_out))
-    ]
     mixing[...] = block_mixing(bypass).astype(BF16)
-    copies[0].wait()
-    build_spread(down_modes, wide, high_in, rest_in)
-    fill_inverse(own_in, other_in, 5, high_in, rest_in, stack)
-    copies[1].wait()
-    for i in range(8):
-        copies[2 + i].wait()
-        spectral = mm_tn(stack[i // 4, :, block_rows(i % 4)], depth[...])
-        grad[block_rows(i), :] = (spectral + mm(mixing[...], dpre[block_rows(i), :])).astype(BF16)
-        leaving[i].start()
+    inverted = part[...] + mm(received_modes(other_in, 5).astype(BF16), spread_other[...])
+    fill_stack(inverted, stack)
     total = own_in[pl.ds(4, KZT, stride=10), :] + other_in[pl.ds(4, KZT, stride=10), :]
     total = total * norm_scale
     grad_weight[...] = total[0:C, 0:C]
-    grad_bias[...] = total[C : C + 8, 0:C]
-    for copy in leaving:
+    grad_bias[...] = total[C : C + 1, 0:C]
+    copies = [
+        pltpu.make_async_copy(source, target, sems.at[i])
+        for i, (source, target) in enumerate(block_pairs(grad, grad_out))
+    ]
+    for first in range(0, 8, 2):
+        for i in (first, first + 1):
+            spectral = mm_tn(stack[i // 4, :, block_rows(i % 4)], depth[...])
+            grad[block_rows(i), :] = (spectral + mm(mixing[...], dpre[block_rows(i), :])).astype(BF16)
+        copies[first].start()
+        copies[first + 1].start()
+    for copy in copies:
         copy.wait()
 
 
@@ -424,6 +474,10 @@
 FAR = pl.BlockSpec(memory_space=pltpu.HBM)
 SMEM = pl.BlockSpec(memory_space=pltpu.SMEM)
 PARAMS = pltpu.CompilerParams(vmem_limit_bytes=24 * 1024 * 1024)
+
+
+SHORT = pl.CostEstimate(flops=2 * 10**9, bytes_accessed=4 * 10**6, transcendentals=0)
+LONG = pl.CostEstimate(flops=10**10, bytes_accessed=2 * 10**7, transcendentals=0)
 
 
 def like(*shape, dtype=F32):
@@ -470,33 +524,33 @@
     held = lambda *shape, dtype=BF16: pltpu.VMEM(shape, dtype)
     sems = lambda count: pltpu.SemaphoreType.DMA((count,))
     field_held = held(2048, LZT)
-    square = held(1024, 1024)
     flat = held(2, 4, KZT, ROWS, dtype=F32)
-    stack = held(2, 3 * KZT + 16, 1024)
-    last_stack = held(2, 3 * KZT, 1024)
     mixing = held(ROWS, ROWS)
-    down = held(GY, 64, 32)
-    wide = held(64, 1024, dtype=F32)
-    depth_held = held(3 * KZT + 16, LZT)
-
-    own, other = call(
+    down = held(GY, 32, 32)
+    wide = held(32, 1024, dtype=F32)
+    half_rows = held(512, 1024)
+    half_columns = held(1024, 512)
+    part_like = like(128, 1024)
+    cells_like = like(128, 1024, dtype=BF16)
+    spread_like = like(512, 1024, dtype=BF16)
+    field_like = like(2048, LZT, dtype=BF16)
+
+    other, cells, wide_cells = call(
         forward_kernel,
         "forward",
         [FAR] * 3,
-        [HELD] * 2,
-        [like(512, 128)] * 2,
-        [field_held, held(KZT, LZT), down, wide, square, square, flat, sems(10)],
+        [HELD] * 3,
+        [like(512, 128), cells_like, like(32, 1024)],
+        [field_held, held(KZT, LZT), down, half_columns, flat, sems(10)],
     )(field, depth, down_cells)
-    messages = exchange(own + swap_cores(other), 4)
+    arriving = swap_cores(other)
+    own = call(forward_own_kernel, "forward_own", [HELD] * 2, HELD, like(512, 128), [half_columns], cost=SHORT)(
+        cells, wide_cells
+    )
+    messages = exchange(own + arriving, 4)
 
     kept = call(
-        prepare_kernel,
-        "prepare",
-        [SMEM, FAR],
-        FAR,
-        field_far,
-        [field_held, field_held, sems(8), sems(8)],
-        pl.CostEstimate(flops=10**10, bytes_accessed=2 * 10**7, transcendentals=0),
+        prepare_kernel, "prepare", [SMEM, FAR], FAR, field_far, [field_held, field_held, sems(8), sems(8)], cost=LONG
     )(hash_key, far(cotangent.reshape(-1, LZT)))
     messages, kept = lax.optimization_barrier((messages, kept))
 
@@ -505,52 +559,66 @@
     )
     own_cells = exchange(planes, 4)
     other_cells = swap_cores(own_cells)
+    part, spread_other, spread_cells, field_near, kept_near, depth_near = call(
+        middle_own_kernel,
+        "middle_own",
+        [HELD] + [FAR] * 5,
+        [HELD] * 6,
+        [
+            part_like, spread_like, like(1024, 1024, dtype=BF16), field_like, field_like,
+            like(3 * KZT + 16, LZT, dtype=BF16),
+        ],
+        [down, down, wide, wide, half_rows, sems(19)],
+        SHORT,
+    )(own_cells, field, far(kept), depth, down_modes, down_cells)
 
     preact = held(ROWS, LZT, dtype=F32)
-    own, other, dpre = call(
+    half_field = held(1024, LZT)
+    other, cells, sums, bias_sums, dpre = call(
         middle_kernel,
         "middle",
-        [HELD] * 4 + [FAR] * 5,
-        [HELD, HELD, FAR],
-        [like(640, 128), like(640, 128), field_far],
-        [
-            field_held, field_held, field_held, depth_held, down, down, wide, square, square, square, square,
-            stack, mixing, preact, preact, flat, held(ROWS, ROWS, dtype=F32), held(16, ROWS, dtype=F32),
-            sems(19), sems(8),
-        ],
+        [HELD] * 9,
+        [HELD] * 4 + [FAR],
+        [like(640, 128), cells_like, like(ROWS, ROWS), like(16, ROWS), field_far],
+        [half_field, half_field, held(2, 3 * KZT + 16, 1024), mixing, preact, preact, flat, sems(8)],
     )(
-        own_cells, other_cells, channel_bias.reshape(1, C), bypass_weight, field, far(kept), depth,
-        down_modes, down_cells,
-    )
-    messages = exchange(own + swap_cores(other), 5)
-
-    planes, grad_spectral = call(
-        back_kernel,
-        "back",
-        [HELD] * 4,
-        [HELD, FAR],
-        [like(640, 128), pltpu.HBM((ROWS, 1024), F32)],
-        [held(ROWS, 1024, dtype=F32), sems(8)],
-    )(messages, modes, weight, across)
+        other_cells, part, spread_other, spread_cells, field_near, kept_near, depth_near,
+        channel_bias.reshape(1, C), bypass_weight,
+    )
+    arriving = swap_cores(other)
+    own = call(middle_send_kernel, "middle_send", [HELD] * 4, HELD, like(640, 128), cost=SHORT)(
+        cells, spread_cells, sums, bias_sums
+    )
+    messages = exchange(own + arriving, 5)
+
+    planes, dmodes = call(back_kernel, "back", [HELD] * 3, [HELD] * 2, [like(640, 128), like(KX, ROWS)])(
+        messages, weight, across
+    )
     own_cells = exchange(planes, 5)
     other_cells = swap_cores(own_cells)
+    part, spread_other, dpre_near, depth_near, grad_spectral = call(
+        last_own_kernel,
+        "last_own",
+        [HELD] * 3 + [FAR] * 3,
+        [HELD] * 4 + [FAR],
+        [part_like, spread_like, field_like, like(3 * KZT, LZT, dtype=BF16), pltpu.HBM((ROWS, 1024), F32)],
+        [down, wide, half_rows, held(ROWS, 1024, dtype=F32), sems(10), sems(1)],
+        SHORT,
+    )(own_cells, modes, dmodes, far(dpre), depth, down_modes)
 
     grad_input, grad_weight, grad_bias = call(
         last_kernel,
         "last",
-        [HELD] * 3 + [FAR] * 3,
+        [HELD] * 7,
         [FAR, HELD, HELD],
-        [field_far, like(C, C), like(8, C)],
-        [
-            field_held, field_held, held(3 * KZT, LZT), down, wide, square, square, last_stack, mixing,
-            sems(10), sems(8),
-        ],
-    )(own_cells, other_cells, bypass_weight, far(dpre), depth, down_modes)
+        [field_far, like(C, C), like(1, C)],
+        [field_held, held(2, 3 * KZT, 1024), mixing, sems(8)],
+    )(own_cells, other_cells, part, spread_other, dpre_near, depth_near, bypass_weight)
     return (
         grad_input.reshape(layer_input.shape),
         grad_spectral.reshape(spectral_weight.shape),
         grad_weight,
-        grad_bias[0],
+        grad_bias.reshape(C),
     )
 
 

time: 127 us -> 119 us (0.937)
  Pallas kernels: 29.2 us -> 24.4 us
  waiting for transfers between devices: 12 us -> 9.2 us
    pallas_call x4 -> x8, Pallas kernels: 22.2 us -> 17.4 us  [the longest x1 4.78 us: local(): call(middle_kernel, 'middle', [HELD] * 9, [HELD] * 4 + [FAR], [like(640,...]
    ppermute x4, waiting for transfers between devices: 4.84 us -> 2.04 us  [swap_cores(): return lax.ppermute(value, 'gy', [(i, i ^ 1) for i in range(GY)])]
  transfers between devices with their start and end apart: 5 -> 5, of which waited for: 5 -> 3; matrix products, arithmetic and copies ran while one was open for 0% -> 0% of each run, Pallas kernels for 5% -> 9%
where the time goes in v3:
time: 119 us
  blocking collectives  57.7 us (48%)
  starting transfers between devices  25.5 us (21%)
  Pallas kernels  24.4 us (21%)
  waiting for transfers between devices  9.2 us (8%)
    all_to_all x3, blocking collectives, exchange(): lax.all_to_all(shaped, ('gx', 'gy'), split_axis=0, concat_axis=0, tiled=T...  57.7 us
    all_to_all x1, starting transfers between devices, exchange(): lax.all_to_all(shaped, ('gx', 'gy'), split_axis=0, concat_axis=0, tiled=T...  13.8 us
    ppermute x4, starting transfers between devices, swap_cores(): return lax.ppermute(value, 'gy', [(i, i ^ 1) for i in range(GY)])  11.7 us
    all_to_all x1, waiting for transfers between devices, exchange(): lax.all_to_all(shaped, ('gx', 'gy'), split_axis=0, concat_axis=0, tiled=T...  7.16 us
    pallas_call x1, Pallas kernels, local(): call(prepare_kernel, 'prepare', [SMEM, FAR], FAR, field_far, [field_held,...  5.73 us
    pallas_call x1, Pallas kernels, local(): call(middle_kernel, 'middle', [HELD] * 9, [HELD] * 4 + [FAR], [like(640,...  4.78 us
    pallas_call x1, Pallas kernels, local(): call(last_kernel, 'last', [HELD] * 7, [FAR, HELD, HELD], [field_far, like...  2.9 us
    pallas_call x1, Pallas kernels, local(): call(middle_own_kernel, 'middle_own', [HELD] + [FAR] * 5, [HELD] * 6, [pa...  2.44 us
  transfers between devices with their start and end apart: 5, of which 3 were waited for; matrix products, arithmetic and copies ran while one was open for 0% of the time, Pallas kernels for 9%

profile of v3, /device:TPU:1, one launch (start us, length us, event | category | flops | bytes accessed | tf_op | source)
XLA Modules:
  0.0 118.5 jit_solution(10296470886074943196)
XLA Ops:
  0.6 2.4 %forward.1 = (f32[512,128]{1,0:T(8,128)S(1)}, bf16[128,1024]{1,0:T(8,128)(2,1)S(1)}, f32[32,1024]{1,0:T(8,128)S(1)}) custom-call(bf16[2048,512]{1,0:T(8,128)(2,1)} %bitcast.29, bf16[208,512]{1,0:T(8,128)(2,1)} %constant.10.clone.depth_in, bf16[4,32,32]{2,1,0:T(8,128)(2,1)} %constant.8.clone.down_in.cells_in), custom_call_target="tpu_custom_call" | custom-call | tf_op jit(solution)/shard_map/forward/pallas_call | solution.py:538
  3.1 3.3 %collective-permute-start = (f32[512,128]{1,0:T(8,128)S(1)}, f32[512,128]{1,0:T(8,128)S(1)}, u32[]{:S(2)}, u32[]{:S(2)}) collective-permute-start(f32[512,128]{1,0:T(8,128)S(1)} %get-tuple-element.34), channel_id=1, source_target_pairs={{0,1},{1,0},{2,3},{3,2},{4,5},{5,4},{6,7},{7,6},{8,9},{9,8},{10,11... | collective-permute-start | bytes 786440 | tf_op jit(solution)/shard_map/ppermute | solution.py:501
  6.4 0.3 forward_own.1
  6.7 0.8 collective-permute-done
  7.6 0.7 add.6
  8.3 13.8 %all-to-all-start = ((f32[128,1,512]{2,1,0:T(1,128)}), f32[128,1,512]{2,1,0:T(1,128)S(1)}, u32[]{:S(2)}, u32[]{:S(2)}) async-start(f32[128,1,512]{2,1,0:T(1,128)} %bitcast.1), calls=%async_computation | async-start | bytes 524288 | tf_op jit(solution)/shard_map/all_to_all | solution.py:507
  22.1 0.0 copy-start
  22.1 0.0 copy-start.1
  22.1 5.7 %prepare.1.kept_in = bf16[2048,512]{1,0:T(8,128)(2,1)} custom-call(s32[2]{0:T(128)S(1)} %copy-done.4, bf16[2048,512]{1,0:T(8,128)(2,1)} %bitcast.32), custom_call_target="tpu_custom_call" | custom-call | flops 10000000000 | bytes 20000000 | tf_op jit(solution)/shard_map/prepare/pallas_call | solution.py:552
  27.8 7.2 %all-to-all-done = f32[128,1,512]{2,1,0:T(1,128)S(1)} async-done(((f32[128,1,512]{2,1,0:T(1,128)}), f32[128,1,512]{2,1,0:T(1,128)S(1)}, u32[]{:S(2)}, u32[]{:S(2)}) %all-to-all-start) | async-done | bytes 262176 | tf_op jit(solution)/shard_map/all_to_all | solution.py:507
  35.0 1.3 %mix.1 = (f32[512,128]{1,0:T(8,128)S(1)}, f32[32,256]{1,0:T(8,128)S(1)}) custom-call(f32[512,128]{1,0:T(8,128)S(1)} %bitcast.23, bf16[256,1024]{1,0:T(8,128)(2,1)S(1)} %bitcast.17, f32[32,384]{1,0:T(8,128)S(1)} %copy-done.1), custom_call_target="tpu_custom_call" | custom-call | tf_op jit(solution)/shard_map/mix/pallas_call | solution.py:557
  36.3 18.7 %all_to_all.20 = f32[128,1,512]{2,1,0:T(1,128)S(1)} all-to-all(f32[128,1,512]{2,1,0:T(1,128)S(1)} %bitcast.27), channel_id=1, replica_groups={{0,2,4,6,8,10,12,14,16,18,20,22,24,26,28,30,32,34,36,38,40,42,44,46,48,..., dimensions={0} | all-to-all | bytes 524288 | tf_op jit(solution)/shard_map/all_to_all | solution.py:507
  55.0 3.7 %collective-permute-start.1 = (f32[512,128]{1,0:T(8,128)S(1)}, f32[512,128]{1,0:T(8,128)S(1)}, u32[]{:S(2)}, u32[]{:S(2)}) collective-permute-start(f32[512,128]{1,0:T(8,128)S(1)} %bitcast.25), channel_id=1, source_target_pairs={{0,1},{1,0},{2,3},{3,2},{4,5},{5,4},{6,7},{7,6},{8,9},{9,8},{10,11... | collective-permute-start | bytes 786440 | tf_op jit(solution)/shard_map/ppermute | solution.py:501
  58.7 2.4 %middle_own.1 = (f32[128,1024]{1,0:T(8,128)S(1)}, bf16[512,1024]{1,0:T(8,128)(2,1)S(1)}, bf16[1024,1024]{1,0:T(8,128)(2,1)S(1)}, bf16[2048,512]{1,0:T(8,128)(2,1...) custom-call(f32[512,128]{1,0:T(8,128)S(1)} %bitcast.26, bf16[2048,512]{1,0:T(8,128)(2,1)} %bitcast.30, ...), custom_call_target="tpu_custom_call" | custom-call | flops 2000000000 | bytes 4000000 | tf_op jit(solution)/shard_map/middle_own/pallas_call | solution.py:562
  61.2 4.8 %middle.1 = (f32[640,128]{1,0:T(8,128)S(1)}, bf16[128,1024]{1,0:T(8,128)(2,1)S(1)}, f32[256,256]{1,0:T(8,128)S(1)}, f32[16,256]{1,0:T(8,128)S(1)}, bf16[2048,512]{1,0:T(8,128)(2,1)}) custom-call(f32[512,128]{1,0:T(8,128)S(1)} %collective-permute-done.1.other_in, f32[128,1024]{1,0:T(8,128)S(1)} %get-tuple-element.38.part, ...), custom_call_target="tpu_custom_call" | custom-call | tf_op jit(solution)/shard_map/middle/pallas_call | solution.py:577
  66.0 0.1 collective-permute-start.2
  66.1 0.4 middle_send.1
  66.5 1.2 %collective-permute-done.2 = f32[640,128]{1,0:T(8,128)S(1)} collective-permute-done((f32[640,128]{1,0:T(8,128)S(1)}, f32[640,128]{1,0:T(8,128)S(1)}, u32[]{:S(2)}, u32[]{:S(2)}) %collective-permute-start.2) | collective-permute-done | bytes 327712 | tf_op jit(solution)/shard_map/ppermute | solution.py:501
  67.7 20.2 %all_to_all.21 = f32[128,1,640]{2,1,0:T(1,128)S(1)} all-to-all(f32[128,1,640]{2,1,0:T(1,128)S(1)} %bitcast.31), channel_id=1, replica_groups={{0,2,4,6,8,10,12,14,16,18,20,22,24,26,28,30,32,34,36,38,40,42,44,46,48,..., dimensions={0} | all-to-all | bytes 655360 | tf_op jit(solution)/shard_map/all_to_all | solution.py:507
  87.9 1.9 %back.1 = (f32[640,128]{1,0:T(8,128)S(1)}, f32[32,256]{1,0:T(8,128)S(1)}) custom-call(f32[640,128]{1,0:T(8,128)S(1)} %bitcast.22, bf16[256,1024]{1,0:T(8,128)(2,1)S(1)} %bitcast.18, f32[32,384]{1,0:T(8,128)S(1)} %copy-done.1), custom_call_target="tpu_custom_call" | custom-call | tf_op jit(solution)/shard_map/back/pallas_call | solution.py:594
  89.8 18.8 %all_to_all.22 = f32[128,1,640]{2,1,0:T(1,128)S(1)} all-to-all(f32[128,1,640]{2,1,0:T(1,128)S(1)} %bitcast.24), channel_id=1, replica_groups={{0,2,4,6,8,10,12,14,16,18,20,22,24,26,28,30,32,34,36,38,40,42,44,46,48,..., dimensions={0} | all-to-all | bytes 655360 | tf_op jit(solution)/shard_map/all_to_all | solution.py:507
  108.6 4.6 %collective-permute-start.3 = (f32[640,128]{1,0:T(8,128)S(1)}, f32[640,128]{1,0:T(8,128)S(1)}, u32[]{:S(2)}, u32[]{:S(2)}) collective-permute-start(f32[640,128]{1,0:T(8,128)S(1)} %bitcast.19), channel_id=1, source_target_pairs={{0,1},{1,0},{2,3},{3,2},{4,5},{5,4},{6,7},{7,6},{8,9},{9,8},{10,11... | collective-permute-start | bytes 983048 | tf_op jit(solution)/shard_map/ppermute | solution.py:501
  113.2 2.3 %last_own.1 = (f32[128,1024]{1,0:T(8,128)S(1)}, bf16[512,1024]{1,0:T(8,128)(2,1)S(1)}, bf16[2048,512]{1,0:T(8,128)(2,1)S(1)}, bf16[192,512]{1,0:T(8,128)(2,1)S(1)}, f32[256,1024]{1,0:T(8,128)}) custom-call(f32[640,128]{1,0:T(8,128)S(1)} %bitcast.20, f32[32,256]{1,0:T(8,128)S(1)} %get-tuple-element.49.modes, f32[32,256]{1,0:T(8,128)S(1)} %get-tuple-element.50.dmodes, ...), custom_call_target="tpu_custom_call" | custom-call | flops 2000000000 | bytes 4000000 | tf_op jit(solution)/shard_map/last_own/pallas_call | solution.py:599
  115.5 2.9 %last.1 = (bf16[2048,512]{1,0:T(8,128)(2,1)}, f32[32,32]{1,0:T(8,128)}, f32[1,32]{1,0:T(1,128)}) custom-call(f32[640,128]{1,0:T(8,128)S(1)} %bitcast.21, f32[640,128]{1,0:T(8,128)S(1)} %collective-permute-done.3.other_in, f32[128,1024]{1,0:T(8,128)S(1)} %get-tuple-element.52.part, bf16[512,1024]{1,0:T(8,128)(2,1)S(1)} %get-tuple-element.53.spread_other, ...), custom_call_target="tpu_custom_call" | custom-call | tf_op jit(solution)/shard_map/last/pallas_call | solution.py:609
  (11 shorter events, 0.1 us)
Async XLA Ops:
  3.1 4.5 %collective-permute-start = (f32[512,128]{1,0:T(8,128)S(1)}, f32[512,128]{1,0:T(8,128)S(1)}, u32[]{:S(2)}, u32[]{:S(2)}) collective-permute-start(f32[512,128]{1,0:T(8,128)S(1)} %get-tuple-element.34), channel_id=1, source_target_pairs={{0,1},{1,0},{2,3},{3,2},{4,5},{5,4},{6,7},{7,6},{8,9},{9,8},{10,11... | collective-permute-start | bytes 786440 | tf_op jit(solution)/shard_map/ppermute | solution.py:501
  6.4 15.7 %copy-start.4 = (s32[2]{0:T(128)S(1)}, s32[2]{0:T(128)}, u32[]{:S(2)}) copy-start(s32[2]{0:T(128)} %key.1) | copy-start | bytes 28
  8.3 26.7 %all-to-all-start = ((f32[128,1,512]{2,1,0:T(1,128)}), f32[128,1,512]{2,1,0:T(1,128)S(1)}, u32[]{:S(2)}, u32[]{:S(2)}) async-start(f32[128,1,512]{2,1,0:T(1,128)} %bitcast.1), calls=%async_computation | async-start | bytes 524288 | tf_op jit(solution)/shard_map/all_to_all | solution.py:507
  22.1 12.9 %copy-start = (bf16[8,1,32,1024]{3,2,1,0:T(8,128)(2,1)S(1)}, bf16[8,1,32,1024]{3,2,1,0:T(8,128)(2,1)}, u32[]{:S(2)}) copy-start(bf16[8,1,32,1024]{3,2,1,0:T(8,128)(2,1)} %param.12) | copy-start | bytes 1572868
  22.1 12.9 %copy-start.1 = (f32[32,384]{1,0:T(8,128)S(1)}, f32[32,384]{1,0:T(8,128)}, u32[]{:S(2)}) copy-start(f32[32,384]{1,0:T(8,128)} %constant.11.clone.across) | copy-start | bytes 147460
  55.0 6.1 %copy-start.2 = (bf16[32,32]{1,0:T(8,128)(2,1)S(1)}, bf16[32,32]{1,0:T(8,128)(2,1)}, u32[]{:S(2)}) copy-start(bf16[32,32]{1,0:T(8,128)(2,1)} %bypass.3) | copy-start | bytes 6148
  55.0 6.1 %copy-start.3 = (f32[32]{0:T(128)S(1)}, f32[32]{0:T(128)}, u32[]{:S(2)}) copy-start(f32[32]{0:T(128)} %param.14) | copy-start | bytes 388
  55.0 6.1 %collective-permute-start.1 = (f32[512,128]{1,0:T(8,128)S(1)}, f32[512,128]{1,0:T(8,128)S(1)}, u32[]{:S(2)}, u32[]{:S(2)}) collective-permute-start(f32[512,128]{1,0:T(8,128)S(1)} %bitcast.25), channel_id=1, source_target_pairs={{0,1},{1,0},{2,3},{3,2},{4,5},{5,4},{6,7},{7,6},{8,9},{9,8},{10,11... | collective-permute-start | bytes 786440 | tf_op jit(solution)/shard_map/ppermute | solution.py:501
  66.0 1.7 %collective-permute-start.2 = (f32[640,128]{1,0:T(8,128)S(1)}, f32[640,128]{1,0:T(8,128)S(1)}, u32[]{:S(2)}, u32[]{:S(2)}) collective-permute-start(f32[640,128]{1,0:T(8,128)S(1)} %get-tuple-element.47), channel_id=1, source_target_pairs={{0,1},{1,0},{2,3},{3,2},{4,5},{5,4},{6,7},{7,6},{8,9},{9,8},{10,11... | collective-permute-start | bytes 983048 | tf_op jit(solution)/shard_map/ppermute | solution.py:501
  108.6 6.9 %collective-permute-start.3 = (f32[640,128]{1,0:T(8,128)S(1)}, f32[640,128]{1,0:T(8,128)S(1)}, u32[]{:S(2)}, u32[]{:S(2)}) collective-permute-start(f32[640,128]{1,0:T(8,128)S(1)} %bitcast.19), channel_id=1, source_target_pairs={{0,1},{1,0},{2,3},{3,2},{4,5},{5,4},{6,7},{7,6},{8,9},{9,8},{10,11... | collective-permute-start | bytes 983048 | tf_op jit(solution)/shard_map/ppermute | solution.py:501

commit v4 on v3

--- a/solution.py
+++ b/solution.py
@@ -75,12 +75,15 @@
     across = hartley_table(KX, LX)
     gather = np.concatenate([np.repeat(across[:, x::2], 2, axis=1) for x in range(2)], axis=1)
     scatter = np.concatenate([across[:, x::2] for x in range(2)], axis=1)
+    scatter_high, scatter_rest = split_table(scatter)
+    scatter_stack = np.concatenate([scatter_high, scatter_high, scatter_rest], axis=0).T.copy()
     ones = np.concatenate([np.ones((3, LZT)), np.zeros((13, LZT))]).astype(jnp.bfloat16)
     return dict(
         down_cells=low(down.transpose(0, 2, 1)),
         down_modes=low(down),
         depth=np.concatenate([depth_high, depth_high, depth_rest, ones], axis=0),
-        across=np.concatenate([gather, scatter], axis=1),
+        gather=np.concatenate(split_table(gather), axis=0),
+        scatter=scatter_stack,
     )
 
 
@@ -196,10 +199,10 @@
     wide[...] = widen(down)
     fill_spread(wide, OTHER, spread)
     copies[1].wait()
-    for first in (0, 4):
-        for i in range(first, first + 4):
+    for first in (0, 2, 4, 6):
+        for i in range(first, first + 2):
             copies[2 + i].wait()
-        for i in range(first, first + 4):
+        for i in range(first, first + 2):
             flat[i // 4, i % 4] = mm_nt(depth[...], field[block_rows(i), :])
     cells[...] = joined(flat).astype(BF16)
     send_modes(mm(cells[...], spread[...]), other, 4)
@@ -224,9 +227,8 @@
     return jnp.bitwise_xor(hashed, lax.shift_right_logical(hashed, jnp.int32(16)))
 
 
-def prepare_kernel(key, cotangent_in, kept_out, cotangent, kept, in_sems, out_sems):
+def prepare_kernel(key, cotangent_in, kept, cotangent, in_sems):
     arriving = start_copies(block_pairs(cotangent_in, cotangent), in_sems)
-    leaving = [pltpu.make_async_copy(source, target, out_sems.at[i]) for i, (source, target) in enumerate(block_pairs(kept, kept_out))]
     origin = (lax.axis_index("gx") * 2 * LY + lax.axis_index("gy") * 32) * (C * LZT)
     shape = (16, LZT)
     inside = (
@@ -248,18 +250,16 @@
             return carry
 
         lax.fori_loop(0, 4, body, 0)
-        leaving[i].start()
-    for copy in leaving:
-        copy.wait()
-
-
-def gathered_modes(messages, across, lines):
+
+
+def gathered_modes(messages, gather, lines):
     slabs = [
         jnp.concatenate([messages[pl.ds(x * 2 + half, 128, stride=lines), :] for half in range(2)], axis=1)
         for x in range(2)
     ]
-    slabs = jnp.concatenate(slabs, axis=0)
-    return jnp.dot(across[:, 0:256], slabs, precision=HIGHEST, preferred_element_type=F32)
+    high, rest = halves(jnp.concatenate(slabs, axis=0))
+    both = mm(gather[...], high)
+    return both[0:KX] + both[KX : 2 * KX] + mm(gather[0:KX, :], rest)
 
 
 def by_mode(modes):
@@ -270,14 +270,13 @@
     return jnp.concatenate(halves(value), axis=1)
 
 
-def scatter_planes(repeated, across, out, lines):
+def scatter_planes(repeated, scatter, out, lines):
     lane = lax.broadcasted_iota(jnp.int32, (KX, ROWS), 1) >> 5
     modes = jnp.zeros((KX, ROWS), F32)
     for k in range(8):
         modes = jnp.where(lane == k, repeated[k * KX : (k + 1) * KX, :], modes)
-    planes = lax.dot_general(
-        across[:, 256:384], modes, (((0,), (0,)), ((), ())), precision=HIGHEST, preferred_element_type=F32
-    )
+    high, rest = halves(modes)
+    planes = mm(scatter[...], jnp.concatenate([high, rest, high], axis=0))
     for x in range(2):
         for half in range(2):
             piece = planes[x * GX : (x + 1) * GX, half * 128 : (half + 1) * 128]
@@ -285,8 +284,8 @@
                 out[pl.ds(side * lines + x * 2 + half, GX, stride=2 * lines), :] = piece
 
 
-def mix_kernel(messages, weight, across, out, modes_out):
-    modes = gathered_modes(messages, across, 4)
+def mix_kernel(messages, weight, gather, scatter, out, modes_out):
+    modes = gathered_modes(messages, gather, 4)
     modes_out[...] = modes
     spread = mm(wide_halves(by_mode(modes)), ones_where((2 * C, C * C), channel, group))
     total = jnp.zeros((ROWS, 128), F32)
@@ -294,11 +293,11 @@
         part = slice(j * 128, (j + 1) * 128)
         total = total + spread[:, part] * weight[:, part].astype(F32)
     repeated = mm(wide_halves(total), ones_where((256, 256), channel, channel))
-    scatter_planes(repeated, across, out, 4)
-
-
-def back_kernel(messages, weight, across, out, dmodes_out):
-    dmodes = gathered_modes(messages, across, 5)
+    scatter_planes(repeated, scatter, out, 4)
+
+
+def back_kernel(messages, weight, gather, scatter, out, dmodes_out):
+    dmodes = gathered_modes(messages, gather, 5)
     dmodes_out[...] = dmodes
     tiled = mm(wide_halves(by_mode(dmodes)), ones_where((2 * C, 128), channel, channel))
     repeated = jnp.zeros((ROWS, ROWS), F32)
@@ -306,17 +305,18 @@
         high, rest = halves(weight[:, j * 128 : (j + 1) * 128].astype(F32) * tiled)
         fold = ones_where((128, 256), lambda i: group(i) + 4 * j, channel)
         repeated = repeated + mm(high, fold) + mm(rest, fold)
-    scatter_planes(repeated, across, out, 5)
+    scatter_planes(repeated, scatter, out, 5)
     total = jnp.sum(messages[pl.ds(4, 128, stride=5), :], axis=0, keepdims=True)
     out[pl.ds(4, 128, stride=5), :] = jnp.broadcast_to(total, (128, 128))
 
 
-def gelu_slope(preact):
+def scaled_slope(preact):
     factor = math.sqrt(2.0 / math.pi)
     square = preact * preact
     tanh_value = jnp.tanh(preact * (factor + (factor * gelu_cubic) * square))
-    rest = preact * (0.5 * factor + (1.5 * factor * gelu_cubic) * square)
-    return 0.5 + 0.5 * tanh_value + rest * (1.0 - tanh_value * tanh_value)
+    half = 0.5 * keep_scale
+    rest = preact * (half * factor + (half * 3.0 * factor * gelu_cubic) * square)
+    return (1.0 + tanh_value) * (half + rest * (1.0 - tanh_value))
 
 
 def invert_own(own_in, lines, down_modes, part, spread_other, wide, spread):
@@ -327,14 +327,13 @@
 
 
 def middle_own_kernel(
-    own_in, field_in, kept_in, depth_in, modes_in, cells_in,
-    part, spread_other, spread_cells, field, kept, depth,
+    own_in, field_in, depth_in, modes_in, cells_in,
+    part, spread_other, spread_cells, field, depth,
     down_modes, down_cells, wide, wide_cells, spread, sems,
 ):
     copies = start_copies(
         [(modes_in, down_modes), (cells_in, down_cells), (depth_in, depth)]
-        + block_pairs(field_in, field)
-        + block_pairs(kept_in, kept),
+        + [(field_in.at[pl.ds(i * ROWS, ROWS)], field.at[i, pl.ds(KZT, ROWS)]) for i in range(8)],
         sems,
     )
     copies[0].wait()
@@ -342,14 +341,18 @@
     invert_own(own_in, 4, down_modes, part, spread_other, wide, spread)
     wide_cells[...] = widen(down_cells)
     fill_spread(wide_cells, ALL, spread_cells)
-    for copy in copies[2:]:
+    copies[2].wait()
+    for i in range(8):
+        field[i, 0:KZT, :] = depth[0:KZT, :]
+        field[i, KZT + ROWS :, :] = jnp.ones((16, LZT), BF16)
+    for copy in copies[3:]:
         copy.wait()
 
 
 def middle_kernel(
     other_in, part, spread_other, spread_cells, field, kept, depth, bias, bypass,
-    other, cells, sums, bias_sums, dpre_out,
-    dpre_even, dpre_odd, stack, mixing, preact_even, preact_odd, flat, sems,
+    other, cells, sums, bias_sums, dpre,
+    stack, mixing, preact_even, preact_odd, flat,
 ):
     mixing[...] = jnp.transpose(block_mixing(bypass)).astype(BF16)
     sums[...] = jnp.zeros_like(sums)
@@ -365,36 +368,25 @@
     for x in range(2):
         stack[x, 3 * KZT : 3 * KZT + 16, :] = wide_bias
     preacts = (preact_even, preact_odd)
-    dpres = (dpre_even, dpre_odd)
-
-    def leaving(i):
-        rows = pl.ds((i // 2) * ROWS, ROWS)
-        return pltpu.make_async_copy(dpres[i % 2].at[rows], dpre_out.at[pl.ds(i * ROWS, ROWS)], sems.at[i])
-
-    def held_rows(i):
-        return slice((i // 2) * ROWS, (i // 2 + 1) * ROWS)
 
     def linear(i):
         spectral = mm_tn(stack[i // 4, :, block_rows(i % 4)], depth[...])
-        preacts[i % 2][...] = spectral + mm(mixing[...], field[block_rows(i), :])
+        preacts[i % 2][...] = spectral + mm(mixing[...], field[i, KZT : KZT + ROWS, :])
 
     def activate(i):
         for chunk in range(ROWS // 16):
             rows = slice(i * ROWS + chunk * 16, i * ROWS + chunk * 16 + 16)
-            at = (i // 2) * ROWS + chunk * 16
-            slope = gelu_slope(preacts[i % 2][chunk * 16 : chunk * 16 + 16, :])
-            dpres[i % 2][at : at + 16, :] = (kept[rows, :].astype(F32) * slope * keep_scale).astype(BF16)
+            slope = scaled_slope(preacts[i % 2][chunk * 16 : chunk * 16 + 16, :])
+            dpre[rows, :] = (kept[rows, :].astype(F32) * slope).astype(BF16)
 
     def reduce(i):
-        block = dpres[i % 2][held_rows(i), :]
-        flat[i // 4, i % 4] = mm_nt(depth[0:KZT, :], block)
-        sums[...] += mm_nt(field[block_rows(i), :], block)
-        bias_sums[...] += mm_nt(jnp.ones((16, LZT), BF16), block)
+        found = mm_nt(field[i], dpre[block_rows(i), :])
+        flat[i // 4, i % 4] = found[0:KZT]
+        sums[...] += found[KZT : KZT + ROWS]
+        bias_sums[...] += found[KZT + ROWS :]
 
     linear(0)
     for i in range(9):
-        if i > 0:
-            leaving(i - 1).start()
         if i < 7:
             linear(i + 1)
         if i > 0:
@@ -406,8 +398,6 @@
     send_modes(mm(cells[...], spread_cells[:, OTHER]), other, 5)
     for side in range(2):
         other[pl.ds(side * 5 + 4, KZT, stride=10), :] = jnp.zeros((KZT, 128), F32)
-    for i in range(8):
-        leaving(i).wait()
 
 
 def middle_send_kernel(cells, spread_cells, sums, bias_sums, own):
@@ -424,12 +414,12 @@
 
 
 def last_own_kernel(
-    own_in, modes, dmodes, dpre_in, depth_in, modes_in,
-    part, spread_other, dpre, depth, grad_out,
+    own_in, modes, dmodes, depth_in, modes_in,
+    part, spread_other, depth, grad_out,
     down_modes, wide, spread, grad, sems, out_sems,
 ):
     copies = start_copies(
-        [(modes_in, down_modes), (depth_in.at[pl.ds(0, 3 * KZT)], depth)] + block_pairs(dpre_in, dpre), sems
+        [(modes_in, down_modes), (depth_in.at[pl.ds(0, 3 * KZT)], depth)], sems
     )
     tiled = mm(wide_halves(by_mode(dmodes[...])), ones_where((2 * C, 128), channel, channel))
     expanded = mm(wide_halves(by_mode(modes[...])), ones_where((2 * C, C * C), channel, group))
@@ -516,7 +506,7 @@
 
 def local(layer_input, cotangent, spectral_weight, bypass_weight, channel_bias, hash_key):
     table = {name: jnp.asarray(value) for name, value in tables().items()}
-    across = table["across"]
+    gather, scatter = table["gather"], table["scatter"]
     depth, down_cells, down_modes = (far(table[name]) for name in ("depth", "down_cells", "down_modes"))
     weight = spectral_weight.reshape(ROWS, C * C)
     field = far(layer_input.reshape(-1, LZT))
@@ -550,39 +540,38 @@
     messages = exchange(own + arriving, 4)
 
     kept = call(
-        prepare_kernel, "prepare", [SMEM, FAR], FAR, field_far, [field_held, field_held, sems(8), sems(8)], cost=LONG
+        prepare_kernel, "prepare", [SMEM, FAR], HELD, field_like, [field_held, sems(8)], cost=LONG
     )(hash_key, far(cotangent.reshape(-1, LZT)))
     messages, kept = lax.optimization_barrier((messages, kept))
 
-    planes, modes = call(mix_kernel, "mix", [HELD] * 3, [HELD] * 2, [like(512, 128), like(KX, ROWS)])(
-        messages, weight, across
+    planes, modes = call(mix_kernel, "mix", [HELD] * 4, [HELD] * 2, [like(512, 128), like(KX, ROWS)])(
+        messages, weight, gather, scatter
     )
     own_cells = exchange(planes, 4)
     other_cells = swap_cores(own_cells)
-    part, spread_other, spread_cells, field_near, kept_near, depth_near = call(
+    part, spread_other, spread_cells, field_near, depth_near = call(
         middle_own_kernel,
         "middle_own",
-        [HELD] + [FAR] * 5,
-        [HELD] * 6,
+        [HELD] + [FAR] * 4,
+        [HELD] * 5,
         [
-            part_like, spread_like, like(1024, 1024, dtype=BF16), field_like, field_like,
+            part_like, spread_like, like(1024, 1024, dtype=BF16), like(8, KZT + ROWS + 16, LZT, dtype=BF16),
             like(3 * KZT + 16, LZT, dtype=BF16),
         ],
-        [down, down, wide, wide, half_rows, sems(19)],
+        [down, down, wide, wide, half_rows, sems(11)],
         SHORT,
-    )(own_cells, field, far(kept), depth, down_modes, down_cells)
+    )(own_cells, field, depth, down_modes, down_cells)
 
     preact = held(ROWS, LZT, dtype=F32)
-    half_field = held(1024, LZT)
     other, cells, sums, bias_sums, dpre = call(
         middle_kernel,
         "middle",
         [HELD] * 9,
-        [HELD] * 4 + [FAR],
-        [like(640, 128), cells_like, like(ROWS, ROWS), like(16, ROWS), field_far],
-        [half_field, half_field, held(2, 3 * KZT + 16, 1024), mixing, preact, preact, flat, sems(8)],
+        [HELD] * 5,
+        [like(640, 128), cells_like, like(ROWS, ROWS), like(16, ROWS), field_like],
+        [held(2, 3 * KZT + 16, 1024), mixing, preact, preact, flat],
     )(
-        other_cells, part, spread_other, spread_cells, field_near, kept_near, depth_near,
+        other_cells, part, spread_other, spread_cells, field_near, kept, depth_near,
         channel_bias.reshape(1, C), bypass_weight,
     )
     arriving = swap_cores(other)
@@ -591,20 +580,20 @@
     )
     messages = exchange(own + arriving, 5)
 
-    planes, dmodes = call(back_kernel, "back", [HELD] * 3, [HELD] * 2, [like(640, 128), like(KX, ROWS)])(
-        messages, weight, across
+    planes, dmodes = call(back_kernel, "back", [HELD] * 4, [HELD] * 2, [like(640, 128), like(KX, ROWS)])(
+        messages, weight, gather, scatter
     )
     own_cells = exchange(planes, 5)
     other_cells = swap_cores(own_cells)
-    part, spread_other, dpre_near, depth_near, grad_spectral = call(
+    part, spread_other, depth_near, grad_spectral = call(
         last_own_kernel,
         "last_own",
-        [HELD] * 3 + [FAR] * 3,
-        [HELD] * 4 + [FAR],
-        [part_like, spread_like, field_like, like(3 * KZT, LZT, dtype=BF16), pltpu.HBM((ROWS, 1024), F32)],
+        [HELD] * 3 + [FAR] * 2,
+        [HELD] * 3 + [FAR],
+        [part_like, spread_like, like(3 * KZT, LZT, dtype=BF16), pltpu.HBM((ROWS, 1024), F32)],
         [down, wide, half_rows, held(ROWS, 1024, dtype=F32), sems(10), sems(1)],
         SHORT,
-    )(own_cells, modes, dmodes, far(dpre), depth, down_modes)
+    )(own_cells, modes, dmodes, depth, down_modes)
 
     grad_input, grad_weight, grad_bias = call(
         last_kernel,
@@ -613,7 +602,7 @@
         [FAR, HELD, HELD],
         [field_far, like(C, C), like(1, C)],
         [field_held, held(2, 3 * KZT, 1024), mixing, sems(8)],
-    )(own_cells, other_cells, part, spread_other, dpre_near, depth_near, bypass_weight)
+    )(own_cells, other_cells, part, spread_other, dpre, depth_near, bypass_weight)
     return (
         grad_input.reshape(layer_input.shape),
         grad_spectral.reshape(spectral_weight.shape),

time: 119 us -> 116 us (0.975)
  Pallas kernels: 24.4 us -> 20.5 us
    pallas_call x6, Pallas kernels: 18.4 us -> 14.3 us  [the longest x1 4.95 us: local(): call(prepare_kernel, 'prepare', [SMEM, FAR], HELD, field_like, [field_hel...]
  transfers between devices with their start and end apart: 5 -> 5, of which waited for: 3 -> 3; matrix products, arithmetic and copies ran while one was open for 0% -> 0% of each run, Pallas kernels for 9% -> 8%
where the time goes in v4:
time: 116 us
  blocking collectives  57.7 us (50%)
  starting transfers between devices  25.7 us (22%)
  Pallas kernels  20.5 us (18%)
  waiting for transfers between devices  9.98 us (9%)
    all_to_all x3, blocking collectives, exchange(): lax.all_to_all(shaped, ('gx', 'gy'), split_axis=0, concat_axis=0, tiled=T...  57.7 us
    all_to_all x1, starting transfers between devices, exchange(): lax.all_to_all(shaped, ('gx', 'gy'), split_axis=0, concat_axis=0, tiled=T...  13.8 us
    ppermute x4, starting transfers between devices, swap_cores(): return lax.ppermute(value, 'gy', [(i, i ^ 1) for i in range(GY)])  11.9 us
    all_to_all x1, waiting for transfers between devices, exchange(): lax.all_to_all(shaped, ('gx', 'gy'), split_axis=0, concat_axis=0, tiled=T...  7.94 us
    pallas_call x1, Pallas kernels, local(): call(prepare_kernel, 'prepare', [SMEM, FAR], HELD, field_like, [field_hel...  4.95 us
    pallas_call x1, Pallas kernels, local(): call(middle_kernel, 'middle', [HELD] * 9, [HELD] * 5, [like(640, 128), ce...  3.5 us
    pallas_call x1, Pallas kernels, local(): call(last_kernel, 'last', [HELD] * 7, [FAR, HELD, HELD], [field_far, like...  2.92 us
    pallas_call x1, Pallas kernels, local(): call(forward_kernel, 'forward', [FAR] * 3, [HELD] * 3, [like(512, 128), c...  2.52 us
  transfers between devices with their start and end apart: 5, of which 3 were waited for; matrix products, arithmetic and copies ran while one was open for 0% of the time, Pallas kernels for 8%

profile of v4, /device:TPU:1, one launch (start us, length us, event | category | flops | bytes accessed | tf_op | source)
XLA Modules:
  0.0 115.5 jit_solution(8991206727160731395)
XLA Ops:
  0.6 2.5 %forward.1 = (f32[512,128]{1,0:T(8,128)S(1)}, bf16[128,1024]{1,0:T(8,128)(2,1)S(1)}, f32[32,1024]{1,0:T(8,128)S(1)}) custom-call(bf16[2048,512]{1,0:T(8,128)(2,1)} %bitcast.29, bf16[208,512]{1,0:T(8,128)(2,1)} %constant.12.clone.depth_in, bf16[4,32,32]{2,1,0:T(8,128)(2,1)} %constant.10.clone.down_in.cells_in), custom_call_target="tpu_custom_call" | custom-call | tf_op jit(solution)/shard_map/forward/pallas_call | solution.py:528
  3.2 3.3 %collective-permute-start = (f32[512,128]{1,0:T(8,128)S(1)}, f32[512,128]{1,0:T(8,128)S(1)}, u32[]{:S(2)}, u32[]{:S(2)}) collective-permute-start(f32[512,128]{1,0:T(8,128)S(1)} %get-tuple-element.32), channel_id=1, source_target_pairs={{0,1},{1,0},{2,3},{3,2},{4,5},{5,4},{6,7},{7,6},{8,9},{9,8},{10,11... | collective-permute-start | bytes 786440 | tf_op jit(solution)/shard_map/ppermute | solution.py:491
  6.5 0.3 forward_own.1
  6.8 0.8 collective-permute-done
  7.6 0.7 add.6
  8.4 13.8 %all-to-all-start = ((f32[128,1,512]{2,1,0:T(1,128)}), f32[128,1,512]{2,1,0:T(1,128)S(1)}, u32[]{:S(2)}, u32[]{:S(2)}) async-start(f32[128,1,512]{2,1,0:T(1,128)} %bitcast.1), calls=%async_computation | async-start | bytes 524288 | tf_op jit(solution)/shard_map/all_to_all | solution.py:497
  22.2 0.0 copy-start.1
  22.2 0.0 copy-start.2
  22.2 4.9 %prepare.1.kept = bf16[2048,512]{1,0:T(8,128)(2,1)S(1)} custom-call(s32[2]{0:T(128)S(1)} %copy-done.5, bf16[2048,512]{1,0:T(8,128)(2,1)} %bitcast.32), custom_call_target="tpu_custom_call" | custom-call | flops 10000000000 | bytes 20000000 | tf_op jit(solution)/shard_map/prepare/pallas_call | solution.py:542
  27.2 7.9 %all-to-all-done = f32[128,1,512]{2,1,0:T(1,128)S(1)} async-done(((f32[128,1,512]{2,1,0:T(1,128)}), f32[128,1,512]{2,1,0:T(1,128)S(1)}, u32[]{:S(2)}, u32[]{:S(2)}) %all-to-all-start) | async-done | bytes 262176 | tf_op jit(solution)/shard_map/all_to_all | solution.py:497
  35.1 0.9 mix.1
  36.0 18.7 %all_to_all.20 = f32[128,1,512]{2,1,0:T(1,128)S(1)} all-to-all(f32[128,1,512]{2,1,0:T(1,128)S(1)} %bitcast.27), channel_id=1, replica_groups={{0,2,4,6,8,10,12,14,16,18,20,22,24,26,28,30,32,34,36,38,40,42,44,46,48,..., dimensions={0} | all-to-all | bytes 524288 | tf_op jit(solution)/shard_map/all_to_all | solution.py:497
  54.7 3.7 %collective-permute-start.1 = (f32[512,128]{1,0:T(8,128)S(1)}, f32[512,128]{1,0:T(8,128)S(1)}, u32[]{:S(2)}, u32[]{:S(2)}) collective-permute-start(f32[512,128]{1,0:T(8,128)S(1)} %bitcast.25), channel_id=1, source_target_pairs={{0,1},{1,0},{2,3},{3,2},{4,5},{5,4},{6,7},{7,6},{8,9},{9,8},{10,11... | collective-permute-start | bytes 786440 | tf_op jit(solution)/shard_map/ppermute | solution.py:491
  58.4 1.9 %middle_own.1 = (f32[128,1024]{1,0:T(8,128)S(1)}, bf16[512,1024]{1,0:T(8,128)(2,1)S(1)}, bf16[1024,1024]{1,0:T(8,128)(2,1)S(1)}, bf16[8,336,512]{2,1,0:T(8,128)(2,1)S(1)}, bf16[208,512]{1,0:T(8,128)(2,1)S(1)}) custom-call(f32[512,128]{1,0:T(8,128)S(1)} %bitcast.26, bf16[2048,512]{1,0:T(8,128)(2,1)} %bitcast.30, bf16[208,512]{1,0:T(8,128)(2,1)} %constant.12.clone.depth_in, ...), custom_call_target="tpu_custom_call" | custom-call | flops 2000000000 | bytes 4000000 | tf_op jit(solution)/shard_map/middle_own/pallas_call | solution.py:552
  60.4 3.5 %middle.1 = (f32[640,128]{1,0:T(8,128)S(1)}, bf16[128,1024]{1,0:T(8,128)(2,1)S(1)}, f32[256,256]{1,0:T(8,128)S(1)}, f32[16,256]{1,0:T(8,128)S(1)}, bf16[2048,512]{1,0:T(8,128)(2,1)S(1)}) custom-call(f32[512,128]{1,0:T(8,128)S(1)} %collective-permute-done.1.other_in, f32[128,1024]{1,0:T(8,128)S(1)} %get-tuple-element.35.part, ...), custom_call_target="tpu_custom_call" | custom-call | tf_op jit(solution)/shard_map/middle/pallas_call | solution.py:566
  63.9 0.3 collective-permute-start.2
  64.2 0.4 middle_send.1
  64.6 1.2 %collective-permute-done.2 = f32[640,128]{1,0:T(8,128)S(1)} collective-permute-done((f32[640,128]{1,0:T(8,128)S(1)}, f32[640,128]{1,0:T(8,128)S(1)}, u32[]{:S(2)}, u32[]{:S(2)}) %collective-permute-start.2) | collective-permute-done | bytes 327712 | tf_op jit(solution)/shard_map/ppermute | solution.py:491
  65.8 20.1 %all_to_all.21 = f32[128,1,640]{2,1,0:T(1,128)S(1)} all-to-all(f32[128,1,640]{2,1,0:T(1,128)S(1)} %bitcast.31), channel_id=1, replica_groups={{0,2,4,6,8,10,12,14,16,18,20,22,24,26,28,30,32,34,36,38,40,42,44,46,48,..., dimensions={0} | all-to-all | bytes 655360 | tf_op jit(solution)/shard_map/all_to_all | solution.py:497
  86.0 1.4 %back.1 = (f32[640,128]{1,0:T(8,128)S(1)}, f32[32,256]{1,0:T(8,128)S(1)}) custom-call(f32[640,128]{1,0:T(8,128)S(1)} %bitcast.22, bf16[256,1024]{1,0:T(8,128)(2,1)S(1)} %bitcast.18, bf16[64,256]{1,0:T(8,128)(2,1)S(1)} %copy-done.2, bf16[128,96]{1,0:T(8,128)(2,1)S(1)} %copy-done.1), custom_call_target="tpu_custom_call" | custom-call | tf_op jit(solution)/shard_map/back/pallas_call | solution.py:583
  87.3 18.8 %all_to_all.22 = f32[128,1,640]{2,1,0:T(1,128)S(1)} all-to-all(f32[128,1,640]{2,1,0:T(1,128)S(1)} %bitcast.24), channel_id=1, replica_groups={{0,2,4,6,8,10,12,14,16,18,20,22,24,26,28,30,32,34,36,38,40,42,44,46,48,..., dimensions={0} | all-to-all | bytes 655360 | tf_op jit(solution)/shard_map/all_to_all | solution.py:497
  106.2 4.6 %collective-permute-start.3 = (f32[640,128]{1,0:T(8,128)S(1)}, f32[640,128]{1,0:T(8,128)S(1)}, u32[]{:S(2)}, u32[]{:S(2)}) collective-permute-start(f32[640,128]{1,0:T(8,128)S(1)} %bitcast.19), channel_id=1, source_target_pairs={{0,1},{1,0},{2,3},{3,2},{4,5},{5,4},{6,7},{7,6},{8,9},{9,8},{10,11... | collective-permute-start | bytes 983048 | tf_op jit(solution)/shard_map/ppermute | solution.py:491
  110.8 1.7 %last_own.1 = (f32[128,1024]{1,0:T(8,128)S(1)}, bf16[512,1024]{1,0:T(8,128)(2,1)S(1)}, bf16[192,512]{1,0:T(8,128)(2,1)S(1)}, f32[256,1024]{1,0:T(8,128)}) custom-call(f32[640,128]{1,0:T(8,128)S(1)} %bitcast.20, f32[32,256]{1,0:T(8,128)S(1)} %get-tuple-element.46.modes, f32[32,256]{1,0:T(8,128)S(1)} %get-tuple-element.47.dmodes, ...), custom_call_target="tpu_custom_call" | custom-call | flops 2000000000 | bytes 4000000 | tf_op jit(solution)/shard_map/last_own/pallas_call | solution.py:588
  112.5 2.9 %last.1 = (bf16[2048,512]{1,0:T(8,128)(2,1)}, f32[32,32]{1,0:T(8,128)}, f32[1,32]{1,0:T(1,128)}) custom-call(f32[640,128]{1,0:T(8,128)S(1)} %bitcast.21, f32[640,128]{1,0:T(8,128)S(1)} %collective-permute-done.3.other_in, f32[128,1024]{1,0:T(8,128)S(1)} %get-tuple-element.48.part, bf16[512,1024]{1,0:T(8,128)(2,1)S(1)} %get-tuple-element.49.spread_other, ...), custom_call_target="tpu_custom_call" | custom-call | tf_op jit(solution)/shard_map/last/pallas_call | solution.py:598
  (13 shorter events, 0.1 us)
Async XLA Ops:
  3.2 4.5 %collective-permute-start = (f32[512,128]{1,0:T(8,128)S(1)}, f32[512,128]{1,0:T(8,128)S(1)}, u32[]{:S(2)}, u32[]{:S(2)}) collective-permute-start(f32[512,128]{1,0:T(8,128)S(1)} %get-tuple-element.32), channel_id=1, source_target_pairs={{0,1},{1,0},{2,3},{3,2},{4,5},{5,4},{6,7},{7,6},{8,9},{9,8},{10,11... | collective-permute-start | bytes 786440 | tf_op jit(solution)/shard_map/ppermute | solution.py:491
  6.5 15.7 %copy-start.5 = (s32[2]{0:T(128)S(1)}, s32[2]{0:T(128)}, u32[]{:S(2)}) copy-start(s32[2]{0:T(128)} %key.1) | copy-start | bytes 28
  8.4 26.7 %all-to-all-start = ((f32[128,1,512]{2,1,0:T(1,128)}), f32[128,1,512]{2,1,0:T(1,128)S(1)}, u32[]{:S(2)}, u32[]{:S(2)}) async-start(f32[128,1,512]{2,1,0:T(1,128)} %bitcast.1), calls=%async_computation | async-start | bytes 524288 | tf_op jit(solution)/shard_map/all_to_all | solution.py:497
  22.2 12.9 %copy-start = (bf16[8,1,32,1024]{3,2,1,0:T(8,128)(2,1)S(1)}, bf16[8,1,32,1024]{3,2,1,0:T(8,128)(2,1)}, u32[]{:S(2)}) copy-start(bf16[8,1,32,1024]{3,2,1,0:T(8,128)(2,1)} %param.13) | copy-start | bytes 1572868
  22.2 12.9 %copy-start.1 = (bf16[128,96]{1,0:T(8,128)(2,1)S(1)}, bf16[128,96]{1,0:T(8,128)(2,1)}, u32[]{:S(2)}) copy-start(bf16[128,96]{1,0:T(8,128)(2,1)} %constant.14.clone.scatter) | copy-start | bytes 73732
  22.2 12.9 %copy-start.2 = (bf16[64,256]{1,0:T(8,128)(2,1)S(1)}, bf16[64,256]{1,0:T(8,128)(2,1)}, u32[]{:S(2)}) copy-start(bf16[64,256]{1,0:T(8,128)(2,1)} %constant.13.clone.gather) | copy-start | bytes 98308
  54.7 5.6 %copy-start.3 = (bf16[32,32]{1,0:T(8,128)(2,1)S(1)}, bf16[32,32]{1,0:T(8,128)(2,1)}, u32[]{:S(2)}) copy-start(bf16[32,32]{1,0:T(8,128)(2,1)} %bypass.3) | copy-start | bytes 6148
  54.7 5.6 %copy-start.4 = (f32[32]{0:T(128)S(1)}, f32[32]{0:T(128)}, u32[]{:S(2)}) copy-start(f32[32]{0:T(128)} %param.15) | copy-start | bytes 388
  54.7 5.6 %collective-permute-start.1 = (f32[512,128]{1,0:T(8,128)S(1)}, f32[512,128]{1,0:T(8,128)S(1)}, u32[]{:S(2)}, u32[]{:S(2)}) collective-permute-start(f32[512,128]{1,0:T(8,128)S(1)} %bitcast.25), channel_id=1, source_target_pairs={{0,1},{1,0},{2,3},{3,2},{4,5},{5,4},{6,7},{7,6},{8,9},{9,8},{10,11... | collective-permute-start | bytes 786440 | tf_op jit(solution)/shard_map/ppermute | solution.py:491
  63.9 1.9 %collective-permute-start.2 = (f32[640,128]{1,0:T(8,128)S(1)}, f32[640,128]{1,0:T(8,128)S(1)}, u32[]{:S(2)}, u32[]{:S(2)}) collective-permute-start(f32[640,128]{1,0:T(8,128)S(1)} %get-tuple-element.44), channel_id=1, source_target_pairs={{0,1},{1,0},{2,3},{3,2},{4,5},{5,4},{6,7},{7,6},{8,9},{9,8},{10,11... | collective-permute-start | bytes 983048 | tf_op jit(solution)/shard_map/ppermute | solution.py:491
  106.2 6.3 %collective-permute-start.3 = (f32[640,128]{1,0:T(8,128)S(1)}, f32[640,128]{1,0:T(8,128)S(1)}, u32[]{:S(2)}, u32[]{:S(2)}) collective-permute-start(f32[640,128]{1,0:T(8,128)S(1)} %bitcast.19), channel_id=1, source_target_pairs={{0,1},{1,0},{2,3},{3,2},{4,5},{5,4},{6,7},{7,6},{8,9},{9,8},{10,11... | collective-permute-start | bytes 983048 | tf_op jit(solution)/shard_map/ppermute | solution.py:491

commit v5 on v4

--- a/solution.py
+++ b/solution.py
@@ -199,10 +199,10 @@
     wide[...] = widen(down)
     fill_spread(wide, OTHER, spread)
     copies[1].wait()
-    for first in (0, 2, 4, 6):
-        for i in range(first, first + 2):
+    for first in (0, 4):
+        for i in range(first, first + 4):
             copies[2 + i].wait()
-        for i in range(first, first + 2):
+        for i in range(first, first + 4):
             flat[i // 4, i % 4] = mm_nt(depth[...], field[block_rows(i), :])
     cells[...] = joined(flat).astype(BF16)
     send_modes(mm(cells[...], spread[...]), other, 4)
@@ -227,8 +227,16 @@
     return jnp.bitwise_xor(hashed, lax.shift_right_logical(hashed, jnp.int32(16)))
 
 
-def prepare_kernel(key, cotangent_in, kept, cotangent, in_sems):
+def prepare_kernel(
+    key, cotangent_in, down_in, bypass, kept, mixing, mixing_turned, wide, cotangent, down, in_sems, down_sem
+):
+    narrow = start_copies([(down_in, down)], down_sem)[0]
     arriving = start_copies(block_pairs(cotangent_in, cotangent), in_sems)
+    blocks = block_mixing(bypass)
+    mixing[...] = blocks.astype(BF16)
+    mixing_turned[...] = jnp.transpose(blocks).astype(BF16)
+    narrow.wait()
+    wide[...] = widen(down)
     origin = (lax.axis_index("gx") * 2 * LY + lax.axis_index("gy") * 32) * (C * LZT)
     shape = (16, LZT)
     inside = (
@@ -302,9 +310,8 @@
     tiled = mm(wide_halves(by_mode(dmodes)), ones_where((2 * C, 128), channel, channel))
     repeated = jnp.zeros((ROWS, ROWS), F32)
     for j in range(8):
-        high, rest = halves(weight[:, j * 128 : (j + 1) * 128].astype(F32) * tiled)
-        fold = ones_where((128, 256), lambda i: group(i) + 4 * j, channel)
-        repeated = repeated + mm(high, fold) + mm(rest, fold)
+        product = (weight[:, j * 128 : (j + 1) * 128].astype(F32) * tiled).astype(BF16)
+        repeated = repeated + mm(product, ones_where((128, 256), lambda i: group(i) + 4 * j, channel))
     scatter_planes(repeated, scatter, out, 5)
     total = jnp.sum(messages[pl.ds(4, 128, stride=5), :], axis=0, keepdims=True)
     out[pl.ds(4, 128, stride=5), :] = jnp.broadcast_to(total, (128, 128))
@@ -319,42 +326,37 @@
     return (1.0 + tanh_value) * (half + rest * (1.0 - tanh_value))
 
 
-def invert_own(own_in, lines, down_modes, part, spread_other, wide, spread):
-    wide[...] = widen(down_modes)
+def invert_own(own_in, lines, wide, part, spread_other, spread):
     fill_spread(wide, ALL, spread, 0, 16)
     part[...] = mm(received_modes(own_in, lines).astype(BF16), spread[...])
     fill_spread(wide, ALL, spread_other, 16, 16)
 
 
 def middle_own_kernel(
-    own_in, field_in, depth_in, modes_in, cells_in,
+    own_in, wide_modes, wide_cells, field_in, depth_in,
     part, spread_other, spread_cells, field, depth,
-    down_modes, down_cells, wide, wide_cells, spread, sems,
+    spread, sems,
 ):
     copies = start_copies(
-        [(modes_in, down_modes), (cells_in, down_cells), (depth_in, depth)]
+        [(depth_in, depth)]
         + [(field_in.at[pl.ds(i * ROWS, ROWS)], field.at[i, pl.ds(KZT, ROWS)]) for i in range(8)],
         sems,
     )
+    invert_own(own_in, 4, wide_modes, part, spread_other, spread)
+    fill_spread(wide_cells, OTHER, spread_cells)
     copies[0].wait()
-    copies[1].wait()
-    invert_own(own_in, 4, down_modes, part, spread_other, wide, spread)
-    wide_cells[...] = widen(down_cells)
-    fill_spread(wide_cells, ALL, spread_cells)
-    copies[2].wait()
     for i in range(8):
         field[i, 0:KZT, :] = depth[0:KZT, :]
         field[i, KZT + ROWS :, :] = jnp.ones((16, LZT), BF16)
-    for copy in copies[3:]:
+    for copy in copies[1:]:
         copy.wait()
 
 
 def middle_kernel(
-    other_in, part, spread_other, spread_cells, field, kept, depth, bias, bypass,
+    other_in, part, spread_other, spread_cells, field, kept, depth, bias, mixing,
     other, cells, sums, bias_sums, dpre,
-    stack, mixing, preact_even, preact_odd, flat,
+    stack, preact_even, preact_odd, flat,
 ):
-    mixing[...] = jnp.transpose(block_mixing(bypass)).astype(BF16)
     sums[...] = jnp.zeros_like(sums)
     bias_sums[...] = jnp.zeros_like(bias_sums)
     inverted = part[...] + mm(received_modes(other_in, 4).astype(BF16), spread_other[...])
@@ -395,13 +397,14 @@
             activate(i)
 
     cells[...] = joined(flat).astype(BF16)
-    send_modes(mm(cells[...], spread_cells[:, OTHER]), other, 5)
+    send_modes(mm(cells[...], spread_cells[...]), other, 5)
     for side in range(2):
         other[pl.ds(side * 5 + 4, KZT, stride=10), :] = jnp.zeros((KZT, 128), F32)
 
 
-def middle_send_kernel(cells, spread_cells, sums, bias_sums, own):
-    send_modes(mm(cells[...], spread_cells[:, OWN]), own, 5)
+def middle_send_kernel(cells, wide_cells, sums, bias_sums, own, spread):
+    fill_spread(wide_cells, OWN, spread)
+    send_modes(mm(cells[...], spread[...]), own, 5)
     lane = lax.broadcasted_iota(jnp.int32, (C, ROWS), 1) >> 5
     picked = jnp.zeros((C, ROWS), F32)
     for k in range(8):
@@ -414,32 +417,28 @@
 
 
 def last_own_kernel(
-    own_in, modes, dmodes, depth_in, modes_in,
+    own_in, modes, dmodes, wide_modes, depth_in,
     part, spread_other, depth, grad_out,
-    down_modes, wide, spread, grad, sems, out_sems,
+    spread, grad, sems,
 ):
-    copies = start_copies(
-        [(modes_in, down_modes), (depth_in.at[pl.ds(0, 3 * KZT)], depth)], sems
-    )
+    arriving = pltpu.make_async_copy(depth_in.at[pl.ds(0, 3 * KZT)], depth, sems.at[0])
+    arriving.start()
     tiled = mm(wide_halves(by_mode(dmodes[...])), ones_where((2 * C, 128), channel, channel))
     expanded = mm(wide_halves(by_mode(modes[...])), ones_where((2 * C, C * C), channel, group))
     for j in range(8):
         grad[:, j * 128 : (j + 1) * 128] = expanded[:, j * 128 : (j + 1) * 128] * tiled
-    leaving = pltpu.make_async_copy(grad, grad_out, out_sems.at[0])
+    leaving = pltpu.make_async_copy(grad, grad_out, sems.at[1])
     leaving.start()
-    copies[0].wait()
-    invert_own(own_in, 5, down_modes, part, spread_other, wide, spread)
-    for copy in copies[1:]:
-        copy.wait()
+    invert_own(own_in, 5, wide_modes, part, spread_other, spread)
+    arriving.wait()
     leaving.wait()
 
 
 def last_kernel(
-    own_in, other_in, part, spread_other, dpre, depth, bypass,
+    own_in, other_in, part, spread_other, dpre, depth, mixing,
     grad_out, grad_weight, grad_bias,
-    grad, stack, mixing, sems,
+    grad, stack, sems,
 ):
-    mixing[...] = block_mixing(bypass).astype(BF16)
     inverted = part[...] + mm(received_modes(other_in, 5).astype(BF16), spread_other[...])
     fill_stack(inverted, stack)
     total = own_in[pl.ds(4, KZT, stride=10), :] + other_in[pl.ds(4, KZT, stride=10), :]
@@ -450,12 +449,10 @@
         pltpu.make_async_copy(source, target, sems.at[i])
         for i, (source, target) in enumerate(block_pairs(grad, grad_out))
     ]
-    for first in range(0, 8, 2):
-        for i in (first, first + 1):
-            spectral = mm_tn(stack[i // 4, :, block_rows(i % 4)], depth[...])
-            grad[block_rows(i), :] = (spectral + mm(mixing[...], dpre[block_rows(i), :])).astype(BF16)
-        copies[first].start()
-        copies[first + 1].start()
+    for i in range(8):
+        spectral = mm_tn(stack[i // 4, :, block_rows(i % 4)], depth[...])
+        grad[block_rows(i), :] = (spectral + mm(mixing[...], dpre[block_rows(i), :])).astype(BF16)
+        copies[i].start()
     for copy in copies:
         copy.wait()
 
@@ -515,9 +512,7 @@
     sems = lambda count: pltpu.SemaphoreType.DMA((count,))
     field_held = held(2048, LZT)
     flat = held(2, 4, KZT, ROWS, dtype=F32)
-    mixing = held(ROWS, ROWS)
     down = held(GY, 32, 32)
-    wide = held(32, 1024, dtype=F32)
     half_rows = held(512, 1024)
     half_columns = held(1024, 512)
     part_like = like(128, 1024)
@@ -539,10 +534,17 @@
     )
     messages = exchange(own + arriving, 4)
 
-    kept = call(
-        prepare_kernel, "prepare", [SMEM, FAR], HELD, field_like, [field_held, sems(8)], cost=LONG
-    )(hash_key, far(cotangent.reshape(-1, LZT)))
-    messages, kept = lax.optimization_barrier((messages, kept))
+    mixing_like = like(ROWS, ROWS, dtype=BF16)
+    prepared = call(
+        prepare_kernel,
+        "prepare",
+        [SMEM, FAR, FAR, HELD],
+        [HELD] * 4,
+        [field_like, mixing_like, mixing_like, like(32, 1024)],
+        [field_held, down, sems(8), sems(1)],
+        LONG,
+    )(hash_key, far(cotangent.reshape(-1, LZT)), down_modes, bypass_weight)
+    messages, (kept, mixing, mixing_turned, wide_modes) = lax.optimization_barrier((messages, prepared))
 
     planes, modes = call(mix_kernel, "mix", [HELD] * 4, [HELD] * 2, [like(512, 128), like(KX, ROWS)])(
         messages, weight, gather, scatter
@@ -552,15 +554,15 @@
     part, spread_other, spread_cells, field_near, depth_near = call(
         middle_own_kernel,
         "middle_own",
-        [HELD] + [FAR] * 4,
+        [HELD] * 3 + [FAR] * 2,
         [HELD] * 5,
         [
-            part_like, spread_like, like(1024, 1024, dtype=BF16), like(8, KZT + ROWS + 16, LZT, dtype=BF16),
+            part_like, spread_like, like(1024, 512, dtype=BF16), like(8, KZT + ROWS + 16, LZT, dtype=BF16),
             like(3 * KZT + 16, LZT, dtype=BF16),
         ],
-        [down, down, wide, wide, half_rows, sems(11)],
+        [half_rows, sems(9)],
         SHORT,
-    )(own_cells, field, depth, down_modes, down_cells)
+    )(own_cells, wide_modes, wide_cells, field, depth)
 
     preact = held(ROWS, LZT, dtype=F32)
     other, cells, sums, bias_sums, dpre = call(
@@ -569,14 +571,14 @@
         [HELD] * 9,
         [HELD] * 5,
         [like(640, 128), cells_like, like(ROWS, ROWS), like(16, ROWS), field_like],
-        [held(2, 3 * KZT + 16, 1024), mixing, preact, preact, flat],
+        [held(2, 3 * KZT + 16, 1024), preact, preact, flat],
     )(
         other_cells, part, spread_other, spread_cells, field_near, kept, depth_near,
-        channel_bias.reshape(1, C), bypass_weight,
+        channel_bias.reshape(1, C), mixing_turned,
     )
     arriving = swap_cores(other)
-    own = call(middle_send_kernel, "middle_send", [HELD] * 4, HELD, like(640, 128), cost=SHORT)(
-        cells, spread_cells, sums, bias_sums
+    own = call(middle_send_kernel, "middle_send", [HELD] * 4, HELD, like(640, 128), [half_columns], SHORT)(
+        cells, wide_cells, sums, bias_sums
     )
     messages = exchange(own + arriving, 5)
 
@@ -588,12 +590,12 @@
     part, spread_other, depth_near, grad_spectral = call(
         last_own_kernel,
         "last_own",
-        [HELD] * 3 + [FAR] * 2,
+        [HELD] * 4 + [FAR],
         [HELD] * 3 + [FAR],
         [part_like, spread_like, like(3 * KZT, LZT, dtype=BF16), pltpu.HBM((ROWS, 1024), F32)],
-        [down, wide, half_rows, held(ROWS, 1024, dtype=F32), sems(10), sems(1)],
+        [half_rows, held(ROWS, 1024, dtype=F32), sems(2)],
         SHORT,
-    )(own_cells, modes, dmodes, depth, down_modes)
+    )(own_cells, modes, dmodes, wide_modes, depth)
 
     grad_input, grad_weight, grad_bias = call(
         last_kernel,
@@ -601,8 +603,8 @@
         [HELD] * 7,
         [FAR, HELD, HELD],
         [field_far, like(C, C), like(1, C)],
-        [field_held, held(2, 3 * KZT, 1024), mixing, sems(8)],
-    )(own_cells, other_cells, part, spread_other, dpre, depth_near, bypass_weight)
+        [field_held, held(2, 3 * KZT, 1024), sems(8)],
+    )(own_cells, other_cells, part, spread_other, dpre, depth_near, mixing)
     return (
         grad_input.reshape(layer_input.shape),
         grad_spectral.reshape(spectral_weight.shape),

time: 116 us -> 115 us (level)
  no operation moved by 1% of the time
where the time goes in v5:
time: 115 us
  blocking collectives  57.7 us (50%)
  starting transfers between devices  25.7 us (22%)
  Pallas kernels  20.1 us (17%)
  waiting for transfers between devices  9.59 us (8%)
    all_to_all x3, blocking collectives, exchange(): lax.all_to_all(shaped, ('gx', 'gy'), split_axis=0, concat_axis=0, tiled=T...  57.7 us
    all_to_all x1, starting transfers between devices, exchange(): lax.all_to_all(shaped, ('gx', 'gy'), split_axis=0, concat_axis=0, tiled=T...  13.8 us
    ppermute x4, starting transfers between devices, swap_cores(): return lax.ppermute(value, 'gy', [(i, i ^ 1) for i in range(GY)])  11.9 us
    all_to_all x1, waiting for transfers between devices, exchange(): lax.all_to_all(shaped, ('gx', 'gy'), split_axis=0, concat_axis=0, tiled=T...  7.52 us
    pallas_call x1, Pallas kernels, local(): call(prepare_kernel, 'prepare', [SMEM, FAR, FAR, HELD], [HELD] * 4, [fiel...  5.35 us
    pallas_call x1, Pallas kernels, local(): call(middle_kernel, 'middle', [HELD] * 9, [HELD] * 5, [like(640, 128), ce...  3.47 us
    pallas_call x1, Pallas kernels, local(): call(last_kernel, 'last', [HELD] * 7, [FAR, HELD, HELD], [field_far, like...  2.84 us
    pallas_call x1, Pallas kernels, local(): call(forward_kernel, 'forward', [FAR] * 3, [HELD] * 3, [like(512, 128), c...  2.43 us
  transfers between devices with their start and end apart: 5, of which 3 were waited for; matrix products, arithmetic and copies ran while one was open for 0% of the time, Pallas kernels for 8%

profile of v5, /device:TPU:1, one launch (start us, length us, event | category | flops | bytes accessed | tf_op | source)
XLA Modules:
  0.0 114.8 jit_solution(6310340008419152244)
XLA Ops:
  0.6 2.4 %forward.1 = (f32[512,128]{1,0:T(8,128)S(1)}, bf16[128,1024]{1,0:T(8,128)(2,1)S(1)}, f32[32,1024]{1,0:T(8,128)S(1)}) custom-call(bf16[2048,512]{1,0:T(8,128)(2,1)} %bitcast.29, bf16[208,512]{1,0:T(8,128)(2,1)} %constant.12.clone.depth_in, bf16[4,32,32]{2,1,0:T(8,128)(2,1)} %constant.10.clone.down_in), custom_call_target="tpu_custom_call" | custom-call | tf_op jit(solution)/shard_map/forward/pallas_call | solution.py:523
  3.1 3.3 %collective-permute-start = (f32[512,128]{1,0:T(8,128)S(1)}, f32[512,128]{1,0:T(8,128)S(1)}, u32[]{:S(2)}, u32[]{:S(2)}) collective-permute-start(f32[512,128]{1,0:T(8,128)S(1)} %get-tuple-element.39), channel_id=1, source_target_pairs={{0,1},{1,0},{2,3},{3,2},{4,5},{5,4},{6,7},{7,6},{8,9},{9,8},{10,11... | collective-permute-start | bytes 786440 | tf_op jit(solution)/shard_map/ppermute | solution.py:488
  6.4 0.3 forward_own.1
  6.7 0.8 collective-permute-done
  7.6 0.7 add.6
  8.3 13.8 %all-to-all-start = ((f32[128,1,512]{2,1,0:T(1,128)}), f32[128,1,512]{2,1,0:T(1,128)S(1)}, u32[]{:S(2)}, u32[]{:S(2)}) async-start(f32[128,1,512]{2,1,0:T(1,128)} %bitcast.1), calls=%async_computation | async-start | bytes 524288 | tf_op jit(solution)/shard_map/all_to_all | solution.py:494
  22.1 0.0 copy-start.1
  22.1 0.0 copy-start.2
  22.1 5.3 %prepare.1 = (bf16[2048,512]{1,0:T(8,128)(2,1)S(1)}, bf16[256,256]{1,0:T(8,128)(2,1)S(1)}, bf16[256,256]{1,0:T(8,128)(2,1)S(1)}, f32[32,1024]{1,0:T(8,128)S(1)}) custom-call(s32[2]{0:T(128)S(1)} %copy-done.5, bf16[2048,512]{1,0:T(8,128)(2,1)} %bitcast.32, bf16[4,32,32]{2,1,0:T(8,128)(2,1)} %constant.11.clone.down_in, bf16[32,32]{1,0:T(8,128)(2,1)S(1)} %copy-done.4), custom_call_target="tpu_custom_call" | custom-call | flops 10000000000 | bytes 20000000 | tf_op jit(solution)/shard_map/prepare/pallas_call | solution.py:538
  27.5 7.5 %all-to-all-done = f32[128,1,512]{2,1,0:T(1,128)S(1)} async-done(((f32[128,1,512]{2,1,0:T(1,128)}), f32[128,1,512]{2,1,0:T(1,128)S(1)}, u32[]{:S(2)}, u32[]{:S(2)}) %all-to-all-start) | async-done | bytes 262176 | tf_op jit(solution)/shard_map/all_to_all | solution.py:494
  35.0 0.9 mix.1
  36.0 18.7 %all_to_all.20 = f32[128,1,512]{2,1,0:T(1,128)S(1)} all-to-all(f32[128,1,512]{2,1,0:T(1,128)S(1)} %bitcast.27), channel_id=1, replica_groups={{0,2,4,6,8,10,12,14,16,18,20,22,24,26,28,30,32,34,36,38,40,42,44,46,48,..., dimensions={0} | all-to-all | bytes 524288 | tf_op jit(solution)/shard_map/all_to_all | solution.py:494
  54.7 3.7 %collective-permute-start.1 = (f32[512,128]{1,0:T(8,128)S(1)}, f32[512,128]{1,0:T(8,128)S(1)}, u32[]{:S(2)}, u32[]{:S(2)}) collective-permute-start(f32[512,128]{1,0:T(8,128)S(1)} %bitcast.25), channel_id=1, source_target_pairs={{0,1},{1,0},{2,3},{3,2},{4,5},{5,4},{6,7},{7,6},{8,9},{9,8},{10,11... | collective-permute-start | bytes 786440 | tf_op jit(solution)/shard_map/ppermute | solution.py:488
  58.3 1.8 %middle_own.1 = (f32[128,1024]{1,0:T(8,128)S(1)}, bf16[512,1024]{1,0:T(8,128)(2,1)S(1)}, bf16[1024,512]{1,0:T(8,128)(2,1)S(1)}, bf16[8,336,512]{2,1,0:T(8,128)(2,1)S(1)}, bf16[208,512]{1,0:T(8,128)(2,1)S(1)}) custom-call(f32[512,128]{1,0:T(8,128)S(1)} %bitcast.26, f32[32,1024]{1,0:T(8,128)S(1)} %get-tuple-element.46.wide_modes, ...), custom_call_target="tpu_custom_call" | custom-call | flops 2000000000 | bytes 4000000 | tf_op jit(solution)/shard_map/middle_own/pallas_call | solution.py:554
  60.2 3.5 %middle.1 = (f32[640,128]{1,0:T(8,128)S(1)}, bf16[128,1024]{1,0:T(8,128)(2,1)S(1)}, f32[256,256]{1,0:T(8,128)S(1)}, f32[16,256]{1,0:T(8,128)S(1)}, bf16[2048,512]{1,0:T(8,128)(2,1)S(1)}) custom-call(f32[512,128]{1,0:T(8,128)S(1)} %collective-permute-done.1.other_in, f32[128,1024]{1,0:T(8,128)S(1)} %get-tuple-element.47.part, ...), custom_call_target="tpu_custom_call" | custom-call | tf_op jit(solution)/shard_map/middle/pallas_call | solution.py:568
  63.6 0.3 collective-permute-start.2
  63.9 0.4 middle_send.1
  64.3 1.2 %collective-permute-done.2 = f32[640,128]{1,0:T(8,128)S(1)} collective-permute-done((f32[640,128]{1,0:T(8,128)S(1)}, f32[640,128]{1,0:T(8,128)S(1)}, u32[]{:S(2)}, u32[]{:S(2)}) %collective-permute-start.2) | collective-permute-done | bytes 327712 | tf_op jit(solution)/shard_map/ppermute | solution.py:488
  65.6 20.2 %all_to_all.21 = f32[128,1,640]{2,1,0:T(1,128)S(1)} all-to-all(f32[128,1,640]{2,1,0:T(1,128)S(1)} %bitcast.31), channel_id=1, replica_groups={{0,2,4,6,8,10,12,14,16,18,20,22,24,26,28,30,32,34,36,38,40,42,44,46,48,..., dimensions={0} | all-to-all | bytes 655360 | tf_op jit(solution)/shard_map/all_to_all | solution.py:494
  85.7 1.1 back.1
  86.8 18.8 %all_to_all.22 = f32[128,1,640]{2,1,0:T(1,128)S(1)} all-to-all(f32[128,1,640]{2,1,0:T(1,128)S(1)} %bitcast.24), channel_id=1, replica_groups={{0,2,4,6,8,10,12,14,16,18,20,22,24,26,28,30,32,34,36,38,40,42,44,46,48,..., dimensions={0} | all-to-all | bytes 655360 | tf_op jit(solution)/shard_map/all_to_all | solution.py:494
  105.6 4.6 %collective-permute-start.3 = (f32[640,128]{1,0:T(8,128)S(1)}, f32[640,128]{1,0:T(8,128)S(1)}, u32[]{:S(2)}, u32[]{:S(2)}) collective-permute-start(f32[640,128]{1,0:T(8,128)S(1)} %bitcast.19), channel_id=1, source_target_pairs={{0,1},{1,0},{2,3},{3,2},{4,5},{5,4},{6,7},{7,6},{8,9},{9,8},{10,11... | collective-permute-start | bytes 983048 | tf_op jit(solution)/shard_map/ppermute | solution.py:488
  110.2 1.5 %last_own.1 = (f32[128,1024]{1,0:T(8,128)S(1)}, bf16[512,1024]{1,0:T(8,128)(2,1)S(1)}, bf16[192,512]{1,0:T(8,128)(2,1)S(1)}, f32[256,1024]{1,0:T(8,128)}) custom-call(f32[640,128]{1,0:T(8,128)S(1)} %bitcast.20, f32[32,256]{1,0:T(8,128)S(1)} %get-tuple-element.59.modes, f32[32,256]{1,0:T(8,128)S(1)} %get-tuple-element.60.dmodes, ...), custom_call_target="tpu_custom_call" | custom-call | flops 2000000000 | bytes 4000000 | tf_op jit(solution)/shard_map/last_own/pallas_call | solution.py:590
  111.8 2.8 %last.1 = (bf16[2048,512]{1,0:T(8,128)(2,1)}, f32[32,32]{1,0:T(8,128)}, f32[1,32]{1,0:T(1,128)}) custom-call(f32[640,128]{1,0:T(8,128)S(1)} %bitcast.21, f32[640,128]{1,0:T(8,128)S(1)} %collective-permute-done.3.other_in, f32[128,1024]{1,0:T(8,128)S(1)} %get-tuple-element.61.part, bf16[512,1024]{1,0:T(8,128)(2,1)S(1)} %get-tuple-element.62.spread_other, ...), custom_call_target="tpu_custom_call" | custom-call | tf_op jit(solution)/shard_map/last/pallas_call | solution.py:600
  (13 shorter events, 0.1 us)
Async XLA Ops:
  3.1 4.5 %collective-permute-start = (f32[512,128]{1,0:T(8,128)S(1)}, f32[512,128]{1,0:T(8,128)S(1)}, u32[]{:S(2)}, u32[]{:S(2)}) collective-permute-start(f32[512,128]{1,0:T(8,128)S(1)} %get-tuple-element.39), channel_id=1, source_target_pairs={{0,1},{1,0},{2,3},{3,2},{4,5},{5,4},{6,7},{7,6},{8,9},{9,8},{10,11... | collective-permute-start | bytes 786440 | tf_op jit(solution)/shard_map/ppermute | solution.py:488
  6.4 15.7 %copy-start.4 = (bf16[32,32]{1,0:T(8,128)(2,1)S(1)}, bf16[32,32]{1,0:T(8,128)(2,1)}, u32[]{:S(2)}) copy-start(bf16[32,32]{1,0:T(8,128)(2,1)} %bypass.1) | copy-start | bytes 6148
  6.4 15.7 %copy-start.5 = (s32[2]{0:T(128)S(1)}, s32[2]{0:T(128)}, u32[]{:S(2)}) copy-start(s32[2]{0:T(128)} %key.1) | copy-start | bytes 28
  8.3 26.7 %all-to-all-start = ((f32[128,1,512]{2,1,0:T(1,128)}), f32[128,1,512]{2,1,0:T(1,128)S(1)}, u32[]{:S(2)}, u32[]{:S(2)}) async-start(f32[128,1,512]{2,1,0:T(1,128)} %bitcast.1), calls=%async_computation | async-start | bytes 524288 | tf_op jit(solution)/shard_map/all_to_all | solution.py:494
  22.1 12.9 %copy-start = (bf16[8,1,32,1024]{3,2,1,0:T(8,128)(2,1)S(1)}, bf16[8,1,32,1024]{3,2,1,0:T(8,128)(2,1)}, u32[]{:S(2)}) copy-start(bf16[8,1,32,1024]{3,2,1,0:T(8,128)(2,1)} %param.13) | copy-start | bytes 1572868
  22.1 12.9 %copy-start.1 = (bf16[128,96]{1,0:T(8,128)(2,1)S(1)}, bf16[128,96]{1,0:T(8,128)(2,1)}, u32[]{:S(2)}) copy-start(bf16[128,96]{1,0:T(8,128)(2,1)} %constant.14.clone.scatter) | copy-start | bytes 73732
  22.1 12.9 %copy-start.2 = (bf16[64,256]{1,0:T(8,128)(2,1)S(1)}, bf16[64,256]{1,0:T(8,128)(2,1)}, u32[]{:S(2)}) copy-start(bf16[64,256]{1,0:T(8,128)(2,1)} %constant.13.clone.gather) | copy-start | bytes 98308
  54.6 5.5 %copy-start.3 = (f32[32]{0:T(128)S(1)}, f32[32]{0:T(128)}, u32[]{:S(2)}) copy-start(f32[32]{0:T(128)} %param.15) | copy-start | bytes 388
  54.7 5.5 %collective-permute-start.1 = (f32[512,128]{1,0:T(8,128)S(1)}, f32[512,128]{1,0:T(8,128)S(1)}, u32[]{:S(2)}, u32[]{:S(2)}) collective-permute-start(f32[512,128]{1,0:T(8,128)S(1)} %bitcast.25), channel_id=1, source_target_pairs={{0,1},{1,0},{2,3},{3,2},{4,5},{5,4},{6,7},{7,6},{8,9},{9,8},{10,11... | collective-permute-start | bytes 786440 | tf_op jit(solution)/shard_map/ppermute | solution.py:488
  63.6 1.9 %collective-permute-start.2 = (f32[640,128]{1,0:T(8,128)S(1)}, f32[640,128]{1,0:T(8,128)S(1)}, u32[]{:S(2)}, u32[]{:S(2)}) collective-permute-start(f32[640,128]{1,0:T(8,128)S(1)} %get-tuple-element.57), channel_id=1, source_target_pairs={{0,1},{1,0},{2,3},{3,2},{4,5},{5,4},{6,7},{7,6},{8,9},{9,8},{10,11... | collective-permute-start | bytes 983048 | tf_op jit(solution)/shard_map/ppermute | solution.py:488
  105.6 6.1 %collective-permute-start.3 = (f32[640,128]{1,0:T(8,128)S(1)}, f32[640,128]{1,0:T(8,128)S(1)}, u32[]{:S(2)}, u32[]{:S(2)}) collective-permute-start(f32[640,128]{1,0:T(8,128)S(1)} %bitcast.19), channel_id=1, source_target_pairs={{0,1},{1,0},{2,3},{3,2},{4,5},{5,4},{6,7},{7,6},{8,9},{9,8},{10,11... | collective-permute-start | bytes 983048 | tf_op jit(solution)/shard_map/ppermute | solution.py:488

commit v6 on v5

--- a/solution.py
+++ b/solution.py
@@ -228,10 +228,18 @@
 
 
 def prepare_kernel(
-    key, cotangent_in, down_in, bypass, kept, mixing, mixing_turned, wide, cotangent, down, in_sems, down_sem
+    key, cotangent_in, down_in, bypass, bias,
+    kept, mixing, mixing_turned, wide, wide_bias,
+    cotangent, down, in_sems, down_sem,
 ):
     narrow = start_copies([(down_in, down)], down_sem)[0]
     arriving = start_copies(block_pairs(cotangent_in, cotangent), in_sems)
+    first = bias[...]
+    bias_high = first.astype(BF16)
+    bias_rest, bias_last = halves(first - bias_high.astype(F32))
+    lines = jnp.concatenate([bias_high, bias_rest, bias_last], axis=0).astype(F32)
+    lines = jnp.concatenate([lines, jnp.zeros((13, C), F32)], axis=0).astype(BF16)
+    wide_bias[...] = mm(lines, ones_where((C, 32 * C), lambda i: i, channel)).astype(BF16)
     blocks = block_mixing(bypass)
     mixing[...] = blocks.astype(BF16)
     mixing_turned[...] = jnp.transpose(blocks).astype(BF16)
@@ -353,7 +361,7 @@
 
 
 def middle_kernel(
-    other_in, part, spread_other, spread_cells, field, kept, depth, bias, mixing,
+    other_in, part, spread_other, spread_cells, field, kept, depth, wide_bias, mixing,
     other, cells, sums, bias_sums, dpre,
     stack, preact_even, preact_odd, flat,
 ):
@@ -361,14 +369,8 @@
     bias_sums[...] = jnp.zeros_like(bias_sums)
     inverted = part[...] + mm(received_modes(other_in, 4).astype(BF16), spread_other[...])
     fill_stack(inverted, stack)
-    first = bias[...]
-    bias_high = first.astype(BF16)
-    bias_rest, bias_last = halves(first - bias_high.astype(F32))
-    lines = jnp.concatenate([bias_high, bias_rest, bias_last], axis=0).astype(F32)
-    lines = jnp.concatenate([lines, jnp.zeros((13, C), F32)], axis=0).astype(BF16)
-    wide_bias = mm(lines, ones_where((C, 32 * C), lambda i: i, channel)).astype(BF16)
     for x in range(2):
-        stack[x, 3 * KZT : 3 * KZT + 16, :] = wide_bias
+        stack[x, 3 * KZT : 3 * KZT + 16, :] = wide_bias[...]
     preacts = (preact_even, preact_odd)
 
     def linear(i):
@@ -376,9 +378,9 @@
         preacts[i % 2][...] = spectral + mm(mixing[...], field[i, KZT : KZT + ROWS, :])
 
     def activate(i):
-        for chunk in range(ROWS // 16):
-            rows = slice(i * ROWS + chunk * 16, i * ROWS + chunk * 16 + 16)
-            slope = scaled_slope(preacts[i % 2][chunk * 16 : chunk * 16 + 16, :])
+        for chunk in range(ROWS // 32):
+            rows = slice(i * ROWS + chunk * 32, i * ROWS + chunk * 32 + 32)
+            slope = scaled_slope(preacts[i % 2][chunk * 32 : chunk * 32 + 32, :])
             dpre[rows, :] = (kept[rows, :].astype(F32) * slope).astype(BF16)
 
     def reduce(i):
@@ -538,13 +540,13 @@
     prepared = call(
         prepare_kernel,
         "prepare",
-        [SMEM, FAR, FAR, HELD],
-        [HELD] * 4,
-        [field_like, mixing_like, mixing_like, like(32, 1024)],
+        [SMEM, FAR, FAR, HELD, HELD],
+        [HELD] * 5,
+        [field_like, mixing_like, mixing_like, like(32, 1024), like(16, 1024, dtype=BF16)],
         [field_held, down, sems(8), sems(1)],
         LONG,
-    )(hash_key, far(cotangent.reshape(-1, LZT)), down_modes, bypass_weight)
-    messages, (kept, mixing, mixing_turned, wide_modes) = lax.optimization_barrier((messages, prepared))
+    )(hash_key, far(cotangent.reshape(-1, LZT)), down_modes, bypass_weight, channel_bias.reshape(1, C))
+    messages, (kept, mixing, mixing_turned, wide_modes, wide_bias) = lax.optimization_barrier((messages, prepared))
 
     planes, modes = call(mix_kernel, "mix", [HELD] * 4, [HELD] * 2, [like(512, 128), like(KX, ROWS)])(
         messages, weight, gather, scatter
@@ -574,7 +576,7 @@
         [held(2, 3 * KZT + 16, 1024), preact, preact, flat],
     )(
         other_cells, part, spread_other, spread_cells, field_near, kept, depth_near,
-        channel_bias.reshape(1, C), mixing_turned,
+        wide_bias, mixing_turned,
     )
     arriving = swap_cores(other)
     own = call(middle_send_kernel, "middle_send", [HELD] * 4, HELD, like(640, 128), [half_columns], SHORT)(

time: 115 us -> 115 us (level)
  no operation moved by 1% of the time
where the time goes in v6:
time: 115 us
  blocking collectives  57.7 us (50%)
  starting transfers between devices  25.7 us (22%)
  Pallas kernels  19.9 us (17%)
  waiting for transfers between devices  9.57 us (8%)
    all_to_all x3, blocking collectives, exchange(): lax.all_to_all(shaped, ('gx', 'gy'), split_axis=0, concat_axis=0, tiled=T...  57.7 us
    all_to_all x1, starting transfers between devices, exchange(): lax.all_to_all(shaped, ('gx', 'gy'), split_axis=0, concat_axis=0, tiled=T...  13.8 us
    ppermute x4, starting transfers between devices, swap_cores(): return lax.ppermute(value, 'gy', [(i, i ^ 1) for i in range(GY)])  11.9 us
    all_to_all x1, waiting for transfers between devices, exchange(): lax.all_to_all(shaped, ('gx', 'gy'), split_axis=0, concat_axis=0, tiled=T...  7.52 us
    pallas_call x1, Pallas kernels, local(): call(prepare_kernel, 'prepare', [SMEM, FAR, FAR, HELD, HELD], [HELD] * 5,...  5.35 us
    pallas_call x1, Pallas kernels, local(): call(middle_kernel, 'middle', [HELD] * 9, [HELD] * 5, [like(640, 128), ce...  3.27 us
    pallas_call x1, Pallas kernels, local(): call(last_kernel, 'last', [HELD] * 7, [FAR, HELD, HELD], [field_far, like...  2.82 us
    pallas_call x1, Pallas kernels, local(): call(forward_kernel, 'forward', [FAR] * 3, [HELD] * 3, [like(512, 128), c...  2.43 us
  transfers between devices with their start and end apart: 5, of which 3 were waited for; matrix products, arithmetic and copies ran while one was open for 0% of the time, Pallas kernels for 8%

profile of v6, /device:TPU:1, one launch (start us, length us, event | category | flops | bytes accessed | tf_op | source)
XLA Modules:
  0.0 114.6 jit_solution(15224749412427842056)
XLA Ops:
  0.6 2.4 %forward.1 = (f32[512,128]{1,0:T(8,128)S(1)}, bf16[128,1024]{1,0:T(8,128)(2,1)S(1)}, f32[32,1024]{1,0:T(8,128)S(1)}) custom-call(bf16[2048,512]{1,0:T(8,128)(2,1)} %bitcast.29, bf16[208,512]{1,0:T(8,128)(2,1)} %constant.12.clone.depth_in, bf16[4,32,32]{2,1,0:T(8,128)(2,1)} %constant.10.clone.down_in), custom_call_target="tpu_custom_call" | custom-call | tf_op jit(solution)/shard_map/forward/pallas_call | solution.py:525
  3.1 3.3 %collective-permute-start = (f32[512,128]{1,0:T(8,128)S(1)}, f32[512,128]{1,0:T(8,128)S(1)}, u32[]{:S(2)}, u32[]{:S(2)}) collective-permute-start(f32[512,128]{1,0:T(8,128)S(1)} %get-tuple-element.41), channel_id=1, source_target_pairs={{0,1},{1,0},{2,3},{3,2},{4,5},{5,4},{6,7},{7,6},{8,9},{9,8},{10,11... | collective-permute-start | bytes 786440 | tf_op jit(solution)/shard_map/ppermute | solution.py:490
  6.4 0.3 forward_own.1
  6.7 0.8 collective-permute-done
  7.6 0.7 add.6
  8.3 13.8 %all-to-all-start = ((f32[128,1,512]{2,1,0:T(1,128)}), f32[128,1,512]{2,1,0:T(1,128)S(1)}, u32[]{:S(2)}, u32[]{:S(2)}) async-start(f32[128,1,512]{2,1,0:T(1,128)} %bitcast.1), calls=%async_computation | async-start | bytes 524288 | tf_op jit(solution)/shard_map/all_to_all | solution.py:496
  22.1 0.0 copy-start.1
  22.1 0.0 copy-start.2
  22.1 5.3 %prepare.1 = (bf16[2048,512]{1,0:T(8,128)(2,1)S(1)}, bf16[256,256]{1,0:T(8,128)(2,1)S(1)}, bf16[256,256]{1,0:T(8,128)(2,1)S(1)}, f32[32,1024]{1,0:T(8,128)S(1)}, bf16[16,1024]{1,0:T(8,128)(2,1)S(1)}) custom-call(s32[2]{0:T(128)S(1)} %copy-done.4, bf16[2048,512]{1,0:T(8,128)(2,1)} %bitcast.32, bf16[4,32,32]{2,1,0:T(8,128)(2,1)} %constant.11.clone.down_in, ...), custom_call_target="tpu_custom_call" | custom-call | flops 10000000000 | bytes 20000000 | tf_op jit(solution)/shard_map/prepare/pallas_call | solution.py:540
  27.5 7.5 %all-to-all-done = f32[128,1,512]{2,1,0:T(1,128)S(1)} async-done(((f32[128,1,512]{2,1,0:T(1,128)}), f32[128,1,512]{2,1,0:T(1,128)S(1)}, u32[]{:S(2)}, u32[]{:S(2)}) %all-to-all-start) | async-done | bytes 262176 | tf_op jit(solution)/shard_map/all_to_all | solution.py:496
  35.0 0.9 mix.1
  36.0 18.7 %all_to_all.20 = f32[128,1,512]{2,1,0:T(1,128)S(1)} all-to-all(f32[128,1,512]{2,1,0:T(1,128)S(1)} %bitcast.27), channel_id=1, replica_groups={{0,2,4,6,8,10,12,14,16,18,20,22,24,26,28,30,32,34,36,38,40,42,44,46,48,..., dimensions={0} | all-to-all | bytes 524288 | tf_op jit(solution)/shard_map/all_to_all | solution.py:496
  54.6 3.7 %collective-permute-start.1 = (f32[512,128]{1,0:T(8,128)S(1)}, f32[512,128]{1,0:T(8,128)S(1)}, u32[]{:S(2)}, u32[]{:S(2)}) collective-permute-start(f32[512,128]{1,0:T(8,128)S(1)} %bitcast.25), channel_id=1, source_target_pairs={{0,1},{1,0},{2,3},{3,2},{4,5},{5,4},{6,7},{7,6},{8,9},{9,8},{10,11... | collective-permute-start | bytes 786440 | tf_op jit(solution)/shard_map/ppermute | solution.py:490
  58.3 1.8 %middle_own.1 = (f32[128,1024]{1,0:T(8,128)S(1)}, bf16[512,1024]{1,0:T(8,128)(2,1)S(1)}, bf16[1024,512]{1,0:T(8,128)(2,1)S(1)}, bf16[8,336,512]{2,1,0:T(8,128)(2,1)S(1)}, bf16[208,512]{1,0:T(8,128)(2,1)S(1)}) custom-call(f32[512,128]{1,0:T(8,128)S(1)} %bitcast.26, f32[32,1024]{1,0:T(8,128)S(1)} %get-tuple-element.49.wide_modes, ...), custom_call_target="tpu_custom_call" | custom-call | flops 2000000000 | bytes 4000000 | tf_op jit(solution)/shard_map/middle_own/pallas_call | solution.py:556
  60.1 3.3 %middle.1 = (f32[640,128]{1,0:T(8,128)S(1)}, bf16[128,1024]{1,0:T(8,128)(2,1)S(1)}, f32[256,256]{1,0:T(8,128)S(1)}, f32[16,256]{1,0:T(8,128)S(1)}, bf16[2048,512]{1,0:T(8,128)(2,1)S(1)}) custom-call(f32[512,128]{1,0:T(8,128)S(1)} %collective-permute-done.1.other_in, f32[128,1024]{1,0:T(8,128)S(1)} %get-tuple-element.50.part, ...), custom_call_target="tpu_custom_call" | custom-call | tf_op jit(solution)/shard_map/middle/pallas_call | solution.py:570
  63.4 0.3 collective-permute-start.2
  63.7 0.4 middle_send.1
  64.1 1.2 %collective-permute-done.2 = f32[640,128]{1,0:T(8,128)S(1)} collective-permute-done((f32[640,128]{1,0:T(8,128)S(1)}, f32[640,128]{1,0:T(8,128)S(1)}, u32[]{:S(2)}, u32[]{:S(2)}) %collective-permute-start.2) | collective-permute-done | bytes 327712 | tf_op jit(solution)/shard_map/ppermute | solution.py:490
  65.4 20.2 %all_to_all.21 = f32[128,1,640]{2,1,0:T(1,128)S(1)} all-to-all(f32[128,1,640]{2,1,0:T(1,128)S(1)} %bitcast.31), channel_id=1, replica_groups={{0,2,4,6,8,10,12,14,16,18,20,22,24,26,28,30,32,34,36,38,40,42,44,46,48,..., dimensions={0} | all-to-all | bytes 655360 | tf_op jit(solution)/shard_map/all_to_all | solution.py:496
  85.5 1.1 back.1
  86.6 18.8 %all_to_all.22 = f32[128,1,640]{2,1,0:T(1,128)S(1)} all-to-all(f32[128,1,640]{2,1,0:T(1,128)S(1)} %bitcast.24), channel_id=1, replica_groups={{0,2,4,6,8,10,12,14,16,18,20,22,24,26,28,30,32,34,36,38,40,42,44,46,48,..., dimensions={0} | all-to-all | bytes 655360 | tf_op jit(solution)/shard_map/all_to_all | solution.py:496
  105.4 4.6 %collective-permute-start.3 = (f32[640,128]{1,0:T(8,128)S(1)}, f32[640,128]{1,0:T(8,128)S(1)}, u32[]{:S(2)}, u32[]{:S(2)}) collective-permute-start(f32[640,128]{1,0:T(8,128)S(1)} %bitcast.19), channel_id=1, source_target_pairs={{0,1},{1,0},{2,3},{3,2},{4,5},{5,4},{6,7},{7,6},{8,9},{9,8},{10,11... | collective-permute-start | bytes 983048 | tf_op jit(solution)/shard_map/ppermute | solution.py:490
  110.0 1.5 %last_own.1 = (f32[128,1024]{1,0:T(8,128)S(1)}, bf16[512,1024]{1,0:T(8,128)(2,1)S(1)}, bf16[192,512]{1,0:T(8,128)(2,1)S(1)}, f32[256,1024]{1,0:T(8,128)}) custom-call(f32[640,128]{1,0:T(8,128)S(1)} %bitcast.20, f32[32,256]{1,0:T(8,128)S(1)} %get-tuple-element.63.modes, f32[32,256]{1,0:T(8,128)S(1)} %get-tuple-element.64.dmodes, ...), custom_call_target="tpu_custom_call" | custom-call | flops 2000000000 | bytes 4000000 | tf_op jit(solution)/shard_map/last_own/pallas_call | solution.py:592
  111.6 2.8 %last.1 = (bf16[2048,512]{1,0:T(8,128)(2,1)}, f32[32,32]{1,0:T(8,128)}, f32[1,32]{1,0:T(1,128)}) custom-call(f32[640,128]{1,0:T(8,128)S(1)} %bitcast.21, f32[640,128]{1,0:T(8,128)S(1)} %collective-permute-done.3.other_in, f32[128,1024]{1,0:T(8,128)S(1)} %get-tuple-element.65.part, bf16[512,1024]{1,0:T(8,128)(2,1)S(1)} %get-tuple-element.66.spread_other, ...), custom_call_target="tpu_custom_call" | custom-call | tf_op jit(solution)/shard_map/last/pallas_call | solution.py:602
  (13 shorter events, 0.1 us)
Async XLA Ops:
  3.1 4.5 %collective-permute-start = (f32[512,128]{1,0:T(8,128)S(1)}, f32[512,128]{1,0:T(8,128)S(1)}, u32[]{:S(2)}, u32[]{:S(2)}) collective-permute-start(f32[512,128]{1,0:T(8,128)S(1)} %get-tuple-element.41), channel_id=1, source_target_pairs={{0,1},{1,0},{2,3},{3,2},{4,5},{5,4},{6,7},{7,6},{8,9},{9,8},{10,11... | collective-permute-start | bytes 786440 | tf_op jit(solution)/shard_map/ppermute | solution.py:490
  6.4 15.7 %copy-start.3 = (bf16[32,32]{1,0:T(8,128)(2,1)S(1)}, bf16[32,32]{1,0:T(8,128)(2,1)}, u32[]{:S(2)}) copy-start(bf16[32,32]{1,0:T(8,128)(2,1)} %bypass.1) | copy-start | bytes 6148
  6.4 15.7 %copy-start.4 = (s32[2]{0:T(128)S(1)}, s32[2]{0:T(128)}, u32[]{:S(2)}) copy-start(s32[2]{0:T(128)} %key.1) | copy-start | bytes 28
  6.4 15.7 %copy-start.5 = (f32[32]{0:T(128)S(1)}, f32[32]{0:T(128)}, u32[]{:S(2)}) copy-start(f32[32]{0:T(128)} %param.15) | copy-start | bytes 388
  8.3 26.7 %all-to-all-start = ((f32[128,1,512]{2,1,0:T(1,128)}), f32[128,1,512]{2,1,0:T(1,128)S(1)}, u32[]{:S(2)}, u32[]{:S(2)}) async-start(f32[128,1,512]{2,1,0:T(1,128)} %bitcast.1), calls=%async_computation | async-start | bytes 524288 | tf_op jit(solution)/shard_map/all_to_all | solution.py:496
  22.1 12.9 %copy-start = (bf16[8,1,32,1024]{3,2,1,0:T(8,128)(2,1)S(1)}, bf16[8,1,32,1024]{3,2,1,0:T(8,128)(2,1)}, u32[]{:S(2)}) copy-start(bf16[8,1,32,1024]{3,2,1,0:T(8,128)(2,1)} %param.13) | copy-start | bytes 1572868
  22.1 12.9 %copy-start.1 = (bf16[128,96]{1,0:T(8,128)(2,1)S(1)}, bf16[128,96]{1,0:T(8,128)(2,1)}, u32[]{:S(2)}) copy-start(bf16[128,96]{1,0:T(8,128)(2,1)} %constant.14.clone.scatter) | copy-start | bytes 73732
  22.1 12.9 %copy-start.2 = (bf16[64,256]{1,0:T(8,128)(2,1)S(1)}, bf16[64,256]{1,0:T(8,128)(2,1)}, u32[]{:S(2)}) copy-start(bf16[64,256]{1,0:T(8,128)(2,1)} %constant.13.clone.gather) | copy-start | bytes 98308
  54.6 5.5 %collective-permute-start.1 = (f32[512,128]{1,0:T(8,128)S(1)}, f32[512,128]{1,0:T(8,128)S(1)}, u32[]{:S(2)}, u32[]{:S(2)}) collective-permute-start(f32[512,128]{1,0:T(8,128)S(1)} %bitcast.25), channel_id=1, source_target_pairs={{0,1},{1,0},{2,3},{3,2},{4,5},{5,4},{6,7},{7,6},{8,9},{9,8},{10,11... | collective-permute-start | bytes 786440 | tf_op jit(solution)/shard_map/ppermute | solution.py:490
  63.4 1.9 %collective-permute-start.2 = (f32[640,128]{1,0:T(8,128)S(1)}, f32[640,128]{1,0:T(8,128)S(1)}, u32[]{:S(2)}, u32[]{:S(2)}) collective-permute-start(f32[640,128]{1,0:T(8,128)S(1)} %get-tuple-element.61), channel_id=1, source_target_pairs={{0,1},{1,0},{2,3},{3,2},{4,5},{5,4},{6,7},{7,6},{8,9},{9,8},{10,11... | collective-permute-start | bytes 983048 | tf_op jit(solution)/shard_map/ppermute | solution.py:490
  105.4 6.1 %collective-permute-start.3 = (f32[640,128]{1,0:T(8,128)S(1)}, f32[640,128]{1,0:T(8,128)S(1)}, u32[]{:S(2)}, u32[]{:S(2)}) collective-permute-start(f32[640,128]{1,0:T(8,128)S(1)} %bitcast.19), channel_id=1, source_target_pairs={{0,1},{1,0},{2,3},{3,2},{4,5},{5,4},{6,7},{7,6},{8,9},{9,8},{10,11... | collective-permute-start | bytes 983048 | tf_op jit(solution)/shard_map/ppermute | solution.py:490
